TPU v7x, 32 devices: a whole 2x2x4 slice. The times are simulated.
32 devices in a mesh: gx: 4 (over y, x), gy: 2 (over core), gz: 4 (over z).
Axes of the slice: x: 2, y: 2, z: 4, core: 2. Of those that a mesh axis runs over, the one named last changes fastest.
Arguments:
- point_data: float32 [32, 32, 7, 32], P(('gx', 'gy', 'gz')), may hold values from -2.8 to 2.8, as said below
- point_cells: int32 [32, 32, 3, 32], P(('gx', 'gy', 'gz')), may hold values from 0 to 127, as said below
- send_counts: int32 [32, 32], P(('gx', 'gy', 'gz')), may hold values from 0 to 32, as said below
Outputs:
- indicator: float32 [64, 32, 512], P('gx', 'gy', 'gz')
- point_values: float32 [32, 32, 32], P(('gx', 'gy', 'gz'))
Inputs may be any that keep to these rules, and one draw needn't show every extreme that they name: `point_data`: channels 0 to 2 of a slot are an oriented normal, channel 3 a confidence between 0.05 and 1, channels 4 to 6 offsets inside the cell between 0 and 1. `point_cells`: channel 0 lies below 16, channel 1 below 16, channel 2 below 128. Slot j from block s to brick d is live where j < send_counts[s, d]. In every draw some brick receives 32 live slots from every block.
All inputs are finite; a program needn't handle non-finite values.
Results may differ from a plain program's by a relative error of at most 0.00002.
Values sent between devices are 32-bit elements; how exact they have to be, the bound alone decides.
No kernel may reach another device: no remote copies, remote signals or barrier semaphores. Data moves between devices by JAX's collectives and lax.ppermute only.
A program may use at most 128 MiB of HBM per device.

v0:
```python
import jax
import jax.numpy as jnp
from jax import lax
from jax.sharding import PartitionSpec as P

CX = 16
CY = 16
CZ = 128
ITERS = 6


base_screen = 0.25
point_screen = 4.0


def shifted(shard, axis, by):
    devices = lax.axis_size(axis)
    pairs = [(i, i + by) for i in range(devices) if 0 <= i + by < devices]
    return lax.ppermute(shard, axis, pairs)


def with_halo(block, sides, width):
    for axis, dim in sides:
        count = lax.axis_size(axis)
        forward = [(i, i + 1) for i in range(count - 1)]
        backward = [(target, source) for source, target in forward]
        low = lax.ppermute(
            lax.slice_in_dim(block, block.shape[dim] - width, None, axis=dim), axis, forward
        )
        high = lax.ppermute(lax.slice_in_dim(block, 0, width, axis=dim), axis, backward)
        block = jnp.concatenate([low, block, high], axis=dim)
    return block


def trilinear(offsets, corner_x, corner_y, corner_z):
    along_x = offsets[..., 0, :] if corner_x else 1.0 - offsets[..., 0, :]
    along_y = offsets[..., 1, :] if corner_y else 1.0 - offsets[..., 1, :]
    along_z = offsets[..., 2, :] if corner_z else 1.0 - offsets[..., 2, :]
    return along_x * along_y * along_z


def six_sum(padded):
    total = padded[2:, 1:-1, 1:-1] + padded[:-2, 1:-1, 1:-1]
    total = total + padded[1:-1, 2:, 1:-1] + padded[1:-1, :-2, 1:-1]
    return total + padded[1:-1, 1:-1, 2:] + padded[1:-1, 1:-1, :-2]


def divergence(padded):
    total = padded[0, 2:, 1:-1, 1:-1] - padded[0, :-2, 1:-1, 1:-1]
    total = total + padded[1, 1:-1, 2:, 1:-1] - padded[1, 1:-1, :-2, 1:-1]
    return total + padded[2, 1:-1, 1:-1, 2:] - padded[2, 1:-1, 1:-1, :-2]


def chebyshev(source_term, diagonal, operate, inside):
    half_width = 6.0 / (6.0 + base_screen)
    sigma_ratio = 1.0 / half_width
    rho_prev = half_width
    solution = jnp.zeros_like(source_term)
    residual = source_term
    direction = source_term / diagonal
    for sweep in range(ITERS):
        solution = solution + direction
        residual = residual - operate(direction)
        if sweep + 1 < ITERS:
            rho_next = 1.0 / (2.0 * sigma_ratio - rho_prev)
            direction = (
                rho_next * rho_prev * direction + 2.0 * rho_next / half_width * residual / diagonal
            )
            direction = direction * inside
            rho_prev = rho_next
    return solution


def grid_mask(length, depth, cells, position, count):
    global_at = jnp.arange(length, dtype=jnp.int32) - depth + position * cells
    return ((global_at >= 0) & (global_at < cells * count)).astype(jnp.float32)


def on_device(point_data, point_cells, send_counts):
    slot_count = point_data.shape[3]
    brick_count = point_data.shape[1]
    slot_index = jnp.arange(slot_count, dtype=jnp.int32)
    live_mask = (slot_index[None, None, :] < send_counts[:, :, None]).astype(jnp.float32)
    weight = point_data[:, :, 3, :] * live_mask
    outgoing = jnp.concatenate(
        [point_data[:, :, :3], weight[:, :, None], point_data[:, :, 4:]], axis=2
    )
    got_data, got_cells = (
        lax.all_to_all(outgoing, ("gx", "gy", "gz"), split_axis=1, concat_axis=0, tiled=True),
        lax.all_to_all(point_cells, ("gx", "gy", "gz"), split_axis=1, concat_axis=0, tiled=True),
    )
    got_data = got_data.reshape(brick_count, 7, slot_count)
    got_cells = got_cells.reshape(brick_count, 3, slot_count)
    offsets = got_data[:, 4:7, :]
    got_weight = got_data[:, 3, :]
    cell_x = got_cells[:, 0, :]
    cell_y = got_cells[:, 1, :]
    cell_z = got_cells[:, 2, :]
    volume = jnp.zeros((4, (CX + 1) * (CY + 1) * (CZ + 1)), jnp.float32)
    for corner_x in (0, 1):
        for corner_y in (0, 1):
            for corner_z in (0, 1):
                point_mass = got_weight * trilinear(offsets, corner_x, corner_y, corner_z)
                contrib = jnp.stack(
                    [
                        got_data[:, 0, :] * point_mass,
                        got_data[:, 1, :] * point_mass,
                        got_data[:, 2, :] * point_mass,
                        point_mass,
                    ]
                ).reshape(4, -1)
                linear_at = (
                    ((cell_x + corner_x) * (CY + 1) + cell_y + corner_y) * (CZ + 1)
                    + cell_z
                    + corner_z
                )
                volume = volume.at[:, linear_at.reshape(-1)].add(contrib)
    partial_value = volume.reshape(4, CX + 1, CY + 1, CZ + 1)
    arrived = shifted(partial_value[:, CX], "gx", 1)
    partial_value = partial_value[:, :CX].at[:, 0].add(arrived)
    arrived = shifted(partial_value[:, :, CY], "gy", 1)
    partial_value = partial_value[:, :, :CY].at[:, :, 0].add(arrived)
    arrived = shifted(partial_value[:, :, :, CZ], "gz", 1)
    splat = partial_value[:, :, :, :CZ].at[:, :, :, 0].add(arrived)
    depth = ITERS + 1
    wide = with_halo(splat, (("gx", 1), ("gy", 2), ("gz", 3)), depth)
    mask_x = grid_mask(CX + 2 * depth, depth, CX, lax.axis_index("gx"), lax.axis_size("gx"))
    mask_y = grid_mask(CY + 2 * depth, depth, CY, lax.axis_index("gy"), lax.axis_size("gy"))
    mask_z = grid_mask(CZ + 2 * depth, depth, CZ, lax.axis_index("gz"), lax.axis_size("gz"))
    inside = mask_x[:, None, None] * mask_y[None, :, None] * mask_z[None, None, :]
    wide_source = -0.5 * divergence(jnp.pad(wide[:3], ((0, 0), (1, 1), (1, 1), (1, 1)))) * inside
    wide_diagonal = 6.0 + base_screen + point_screen * wide[3]

    def operate_wide(field):
        return wide_diagonal * field - six_sum(jnp.pad(field, 1))

    solution = chebyshev(wide_source, wide_diagonal, operate_wide, inside)
    indicator = solution[depth : depth + CX, depth : depth + CY, depth : depth + CZ]
    extended = solution[
        depth - 1 : depth + CX + 1, depth - 1 : depth + CY + 1, depth - 1 : depth + CZ + 1
    ]
    extended = extended.reshape(-1)
    values = jnp.zeros(got_weight.shape, jnp.float32)
    for corner_x in (0, 1):
        for corner_y in (0, 1):
            for corner_z in (0, 1):
                linear_at = (
                    ((cell_x + 1 + corner_x) * (CY + 2) + cell_y + 1 + corner_y) * (CZ + 2)
                    + cell_z
                    + 1
                    + corner_z
                )
                values = (
                    values + trilinear(offsets, corner_x, corner_y, corner_z) * extended[linear_at]
                )
    returned = lax.all_to_all(
        values.reshape(brick_count, 1, slot_count),
        ("gx", "gy", "gz"),
        split_axis=0,
        concat_axis=1,
        tiled=True,
    )
    point_values = returned * live_mask
    return (indicator, point_values)


def solution(mesh):
    in_specs = (
        P(("gx", "gy", "gz"), None, None, None),
        P(("gx", "gy", "gz"), None, None, None),
        P(("gx", "gy", "gz"), None),
    )
    out_specs = (P("gx", "gy", "gz"), P(("gx", "gy", "gz"), None, None))
    return jax.shard_map(
        on_device, mesh=mesh, in_specs=in_specs, out_specs=out_specs, check_vma=False
    )
```

profile of v0, /device:TPU:0, one launch (start us, length us, event | category | flops | bytes accessed | tf_op | source)
XLA Modules:
  0.0 342.3 jit_solution(14408379903279858559)
XLA Ops:
  0.6 1.5 copy.257
  2.1 7.3 %all-to-all-start = ((s32[1,32,3,32]{3,2,0,1:T(4,128)}), s32[1,32,3,32]{3,2,0,1:T(4,128)S(1)}, u32[]{:S(2)}, u32[]{:S(2)}) async-start(s32[1,32,3,32]{3,2,0,1:T(4,128)} %copy.257), calls=%async_computation | async-start | bytes 131072 | tf_op jit(solution)/shard_map/all_to_all | solution.py:90
  9.4 0.8 fusion.37
  11.1 0.8 compare_select_fusion
  13.1 0.9 reduce.8
  14.8 2.1 all-to-all-done
  16.9 3.7 %all-to-all-start.1 = ((f32[32,1,224]{2,1,0:T(1,128)}), f32[32,1,224]{2,1,0:T(1,128)S(1)}, u32[]{:S(2)}, u32[]{:S(2)}) async-start(f32[32,1,224]{2,1,0:T(1,128)} %reshape.2164), calls=%async_computation.1 | async-start | bytes 65536 | tf_op jit(solution)/shard_map/all_to_all | solution.py:89
  21.8 6.1 %all-to-all-done.1 = f32[32,1,224]{2,1,0:T(1,128)S(1)} async-done(((f32[32,1,224]{2,1,0:T(1,128)}), f32[32,1,224]{2,1,0:T(1,128)S(1)}, u32[]{:S(2)}, u32[]{:S(2)}) %all-to-all-start.1) | async-done | bytes 28704 | tf_op jit(solution)/shard_map/all_to_all | solution.py:89
  30.2 1.0 copy.263
  32.5 1.0 copy.269
  33.7 14.1 %scatter_custom_fusion = f32[4,37281]{0,1:T(8,128)} fusion(s32[1024]{0:T(1024)S(1)} %bitcast.146, f32[1024,4]{1,0:T(8,128)} %copy.263, f32[]{:T(128)} %constant.143.clone.1), kind=kCustom, calls=%fused_computation.16 | custom fusion | flops 4096 | bytes 597008 | tf_op jit(solution)/shard_map/scatter-add | solution.py:117
  47.9 18.4 %scatter_fusion = f32[4,37281]{0,1:T(8,128)} fusion(f32[4,37281]{0,1:T(8,128)} %scatter_custom_fusion, s32[1024]{0:T(1024)S(1)} %bitcast.142, f32[1024,4]{1,0:T(8,128)S(1)} %copy.264), kind=kCustom, calls=%fused_computation.9 | custom fusion | flops 4096 | bytes 53248 | tf_op jit(solution)/shard_map/scatter-add | solution.py:117
  66.2 18.6 %scatter_fusion.1 = f32[4,37281]{0,1:T(8,128)} fusion(f32[4,37281]{0,1:T(8,128)} %scatter_fusion, s32[1024]{0:T(1024)S(1)} %bitcast.143, f32[1024,4]{1,0:T(8,128)S(1)} %copy.265), kind=kCustom, calls=%fused_computation.10 | custom fusion | flops 4096 | bytes 53248 | tf_op jit(solution)/shard_map/scatter-add | solution.py:117
  84.8 18.4 %scatter_fusion.2 = f32[4,37281]{0,1:T(8,128)} fusion(f32[4,37281]{0,1:T(8,128)} %scatter_fusion.1, s32[1024]{0:T(1024)S(1)} %bitcast.140, f32[1024,4]{1,0:T(8,128)S(1)} %copy.266), kind=kCustom, calls=%fused_computation.11 | custom fusion | flops 4096 | bytes 53248 | tf_op jit(solution)/shard_map/scatter-add | solution.py:117
  103.2 18.4 %scatter_fusion.3 = f32[4,37281]{0,1:T(8,128)} fusion(f32[4,37281]{0,1:T(8,128)} %scatter_fusion.2, s32[1024]{0:T(1024)S(1)} %bitcast.141, f32[1024,4]{1,0:T(8,128)S(1)} %copy.267), kind=kCustom, calls=%fused_computation.12 | custom fusion | flops 4096 | bytes 53248 | tf_op jit(solution)/shard_map/scatter-add | solution.py:117
  121.5 18.4 %scatter_fusion.4 = f32[4,37281]{0,1:T(8,128)} fusion(f32[4,37281]{0,1:T(8,128)} %scatter_fusion.3, s32[1024]{0:T(1024)S(1)} %bitcast.139, f32[1024,4]{1,0:T(8,128)S(1)} %copy.268), kind=kCustom, calls=%fused_computation.13 | custom fusion | flops 4096 | bytes 53248 | tf_op jit(solution)/shard_map/scatter-add | solution.py:117
  139.9 18.8 %scatter_fusion.5 = f32[4,37281]{0,1:T(8,128)} fusion(f32[4,37281]{0,1:T(8,128)} %scatter_fusion.4, s32[1024]{0:T(1024)S(1)} %bitcast.145, f32[1024,4]{1,0:T(8,128)} %copy.269), kind=kCustom, calls=%fused_computation.14 | custom fusion | flops 4096 | bytes 53248 | tf_op jit(solution)/shard_map/scatter-add | solution.py:117
  158.6 18.4 %scatter_fusion.6 = f32[4,37281]{0,1:T(8,128)} fusion(f32[4,37281]{0,1:T(8,128)} %scatter_fusion.5, s32[1024]{0:T(1024)S(1)} %bitcast.144, f32[1024,4]{1,0:T(8,128)S(1)} %copy.270), kind=kCustom, calls=%fused_computation.15 | custom fusion | flops 4096 | bytes 53248 | tf_op jit(solution)/shard_map/scatter-add | solution.py:117
  177.0 10.8 %copy.271 = f32[4,37281]{1,0:T(4,128)S(1)} copy(f32[4,37281]{0,1:T(8,128)} %scatter_fusion.6) | data formatting | bytes 1192992 | tf_op jit(solution)/shard_map/scatter-add | solution.py:117
  187.8 0.8 reshape.1957
  188.6 2.5 collective-permute-start
  191.4 2.0 collective-permute-done
  193.4 13.4 %collective-permute-start.1 = (f32[4,16,129]{2,1,0:T(8,128)S(1)}, f32[4,16,129]{2,1,0:T(8,128)S(1)}, u32[]{:S(2)}, u32[]{:S(2)}) collective-permute-start(f32[4,16,129]{2,1,0:T(8,128)S(1)} %bitcast.135), channel_id=1, source_target_pairs={{0,4},{1,5},{2,6},{3,7},{8,12},{9,13},{10,14},{11,15},{16,20},{17,... | collective-permute-start | bytes 99080 | tf_op jit(solution)/shard_map/ppermute | solution.py:19
  206.8 0.8 reshape.2019
  207.8 0.9 scatter-add.80
  208.9 2.4 collective-permute-start.2
  211.5 1.5 collective-permute-done.2
  213.5 1.0 scatter-add.81
  214.5 4.4 %collective-permute-start.3 = (f32[4,7,16,128]{3,2,1,0:T(8,128)S(1)}, f32[4,7,16,128]{3,2,1,0:T(8,128)S(1)}, u32[]{:S(2)}, u32[]{:S(2)}) collective-permute-start(f32[4,7,16,128]{3,2,1,0:T(8,128)S(1)} %get-tuple-element.69), channel_id=1, source_target_pairs={{0,8},{8,16},{16,24},{1,9},{9,17},{17,25},{2,10},{10,18},{18,26},{... | collective-permute-start | bytes 688136 | tf_op jit(solution)/shard_map/ppermute | solution.py:27
  218.9 1.3 collective-permute-start.4
  220.5 1.9 collective-permute-done.3
  222.5 7.7 %collective-permute-done.4 = f32[4,7,16,128]{3,2,1,0:T(8,128)S(1)} collective-permute-done((f32[4,7,16,128]{3,2,1,0:T(8,128)S(1)}, f32[4,7,16,128]{3,2,1,0:T(8,128)S(1)}, u32[]{:S(2)}, u32[]{:S(2)}) %collective-permute-start.4) | collective-permute-done | bytes 229408 | tf_op jit(solution)/shard_map/ppermute | solution.py:30
  230.3 1.3 collective-permute-start.5
  231.6 1.3 collective-permute-start.6
  233.1 2.3 collective-permute-done.6
  235.7 2.0 fusion.33
  237.7 3.2 copy.276
  240.8 4.7 %collective-permute-start.7 = (f32[4,30,30,7]{2,0,3,1:T(4,128)}, f32[4,30,30,7]{2,0,3,1:T(4,128)}, u32[]{:S(2)}, u32[]{:S(2)}) collective-permute-start(f32[4,30,30,7]{2,0,3,1:T(4,128)} %copy.276), channel_id=1, source_target_pairs={{0,1},{1,2},{2,3},{4,5},{5,6},{6,7},{8,9},{9,10},{10,11},{12,13},{... | collective-permute-start | bytes 302408 | tf_op jit(solution)/shard_map/ppermute | solution.py:27
  245.5 1.6 copy.277
  247.1 1.3 collective-permute-start.8
  248.4 6.1 %collective-permute-done.7 = f32[4,30,30,7]{2,0,3,1:T(4,128)} collective-permute-done((f32[4,30,30,7]{2,0,3,1:T(4,128)}, f32[4,30,30,7]{2,0,3,1:T(4,128)}, u32[]{:S(2)}, u32[]{:S(2)}) %collective-permute-start.7) | collective-permute-done | bytes 100832 | tf_op jit(solution)/shard_map/ppermute | solution.py:27
  254.5 1.9 copy.278
  256.4 4.6 %collective-permute-done.8 = f32[4,30,30,7]{2,0,3,1:T(4,128)} collective-permute-done((f32[4,30,30,7]{2,0,3,1:T(4,128)}, f32[4,30,30,7]{2,0,3,1:T(4,128)}, u32[]{:S(2)}, u32[]{:S(2)}) %collective-permute-start.8) | collective-permute-done | bytes 100832 | tf_op jit(solution)/shard_map/ppermute | solution.py:30
  261.0 3.2 copy.279
  264.2 4.3 %pad_maximum_fusion = f32[4,30,30,142]{3,2,1,0:T(8,128)S(1)} fusion(f32[4,30,30,7]{3,2,1,0:T(8,128)} %copy.279, f32[4,30,7,128]{3,2,1,0:T(8,128)S(1)} %collective-permute-done.6, f32[4,7,16,128]{3,2,1,0:T(8,128)} %copy-done.3, f32[4,16,16,128]{3,2,1,0:T(8,128)S(1)} %scatter-add.81, f32[4,7,16,128]{3,2,1,0:T(8,128)} %copy-done.1, ...), kind=kLoop, calls=%fused_computation.18 | loop fusion | flops 3067200 | bytes 4089600 | tf_op jit(solution)/shard_map/concatenate | solution.py:31
  268.7 1.3 copy-done
  270.1 1.9 fusion.23
  272.0 1.0 multiply_multiply_fusion.4
  273.0 1.1 multiply_multiply_fusion.3
  274.1 2.2 multiply_multiply_fusion.2
  276.4 1.1 multiply_multiply_fusion.1
  277.5 2.7 fusion.9
  280.6 6.2 %gather_fusion.3 = f32[1024]{0:T(1024)S(1)} fusion(f32[42120]{0:T(1024)S(1)} %reshape.1961, s32[1024]{0:T(1024)S(1)} %broadcast_clamp_fusion.4), kind=kCustom, calls=%fused_computation.3 | custom fusion | bytes 12288 | tf_op jit(solution)/shard_map/gather | solution.py:154
  286.8 6.1 %gather_fusion.2 = f32[1024]{0:T(1024)S(1)} fusion(f32[42120]{0:T(1024)S(1)} %reshape.1961, s32[1024]{0:T(1024)S(1)} %broadcast_clamp_fusion.5), kind=kCustom, calls=%fused_computation.2 | custom fusion | bytes 12288 | tf_op jit(solution)/shard_map/gather | solution.py:154
  293.1 6.1 %gather_fusion = f32[1024]{0:T(1024)S(1)} fusion(f32[42120]{0:T(1024)S(1)} %reshape.1961, s32[1024]{0:T(1024)S(1)} %broadcast_clamp_fusion.7), kind=kCustom, calls=%fused_computation | custom fusion | bytes 12288 | tf_op jit(solution)/shard_map/gather | solution.py:154
  299.3 6.1 %gather_fusion.5 = f32[1024]{0:T(1024)S(1)} fusion(f32[42120]{0:T(1024)S(1)} %reshape.1961, s32[1024]{0:T(1024)S(1)} %broadcast_clamp_fusion.2), kind=kCustom, calls=%fused_computation.5 | custom fusion | bytes 12288 | tf_op jit(solution)/shard_map/gather | solution.py:154
  305.5 6.1 %gather_fusion.6 = f32[1024]{0:T(1024)S(1)} fusion(f32[42120]{0:T(1024)S(1)} %reshape.1961, s32[1024]{0:T(1024)S(1)} %broadcast_clamp_fusion.1), kind=kCustom, calls=%fused_computation.6 | custom fusion | bytes 12288 | tf_op jit(solution)/shard_map/gather | solution.py:154
  311.7 6.1 %gather_fusion.7 = f32[1024]{0:T(1024)S(1)} fusion(f32[42120]{0:T(1024)S(1)} %reshape.1961, s32[1024]{0:T(1024)S(1)} %broadcast_clamp_fusion), kind=kCustom, calls=%fused_computation.7 | custom fusion | bytes 12288 | tf_op jit(solution)/shard_map/gather | solution.py:154
  318.0 6.1 %gather_fusion.1 = f32[1024]{0:T(1024)S(1)} fusion(f32[42120]{0:T(1024)S(1)} %reshape.1961, s32[1024]{0:T(1024)S(1)} %broadcast_clamp_fusion.6), kind=kCustom, calls=%fused_computation.1 | custom fusion | bytes 12288 | tf_op jit(solution)/shard_map/gather | solution.py:154
  324.2 6.1 %gather_fusion.4 = f32[1024]{0:T(1024)S(1)} fusion(f32[42120]{0:T(1024)S(1)} %reshape.1961, s32[1024]{0:T(1024)S(1)} %broadcast_clamp_fusion.3), kind=kCustom, calls=%fused_computation.4 | custom fusion | bytes 12288 | tf_op jit(solution)/shard_map/gather | solution.py:154
  330.4 1.4 multiply_add_fusion.6
  331.8 2.5 all-to-all-start.2
  334.3 0.8 slice.459
  335.1 6.3 %all-to-all-done.2 = f32[32,1,32]{2,1,0:T(1,128)S(1)} async-done(((f32[32,1,32]{2,1,0:T(1,128)}), f32[32,1,32]{2,1,0:T(1,128)S(1)}, u32[]{:S(2)}, u32[]{:S(2)}) %all-to-all-start.2) | async-done | bytes 4128 | tf_op jit(solution)/shard_map/all_to_all | solution.py:156
  (103 shorter events, 11.7 us)
Async XLA Ops:
  2.1 14.8 %all-to-all-start = ((s32[1,32,3,32]{3,2,0,1:T(4,128)}), s32[1,32,3,32]{3,2,0,1:T(4,128)S(1)}, u32[]{:S(2)}, u32[]{:S(2)}) async-start(s32[1,32,3,32]{3,2,0,1:T(4,128)} %copy.257), calls=%async_computation | async-start | bytes 131072 | tf_op jit(solution)/shard_map/all_to_all | solution.py:90
  16.9 11.0 %all-to-all-start.1 = ((f32[32,1,224]{2,1,0:T(1,128)}), f32[32,1,224]{2,1,0:T(1,128)S(1)}, u32[]{:S(2)}, u32[]{:S(2)}) async-start(f32[32,1,224]{2,1,0:T(1,128)} %reshape.2164), calls=%async_computation.1 | async-start | bytes 65536 | tf_op jit(solution)/shard_map/all_to_all | solution.py:89
  28.8 0.6 copy-start.5
  188.6 4.7 %collective-permute-start = (f32[4,17,129]{2,1,0:T(8,128)S(1)}, f32[4,17,129]{2,1,0:T(8,128)S(1)}, u32[]{:S(2)}, u32[]{:S(2)}) collective-permute-start(f32[4,17,129]{2,1,0:T(8,128)S(1)} %slice_bitcast_fusion), channel_id=1, source_target_pairs={{0,8},{8,16},{16,24},{1,9},{9,17},{17,25},{2,10},{10,18},{18,26},{... | collective-permute-start | bytes 105272 | tf_op jit(solution)/shard_map/ppermute | solution.py:19
  193.4 14.3 %collective-permute-start.1 = (f32[4,16,129]{2,1,0:T(8,128)S(1)}, f32[4,16,129]{2,1,0:T(8,128)S(1)}, u32[]{:S(2)}, u32[]{:S(2)}) collective-permute-start(f32[4,16,129]{2,1,0:T(8,128)S(1)} %bitcast.135), channel_id=1, source_target_pairs={{0,4},{1,5},{2,6},{3,7},{8,12},{9,13},{10,14},{11,15},{16,20},{17,... | collective-permute-start | bytes 99080 | tf_op jit(solution)/shard_map/ppermute | solution.py:19
  208.9 4.0 %collective-permute-start.2 = (f32[4,16,16]{2,1,0:T(8,128)S(1)}, f32[4,16,16]{2,1,0:T(8,128)S(1)}, u32[]{:S(2)}, u32[]{:S(2)}) collective-permute-start(f32[4,16,16]{2,1,0:T(8,128)S(1)} %slice_reduce_fusion), channel_id=1, source_target_pairs={{0,1},{1,2},{2,3},{4,5},{5,6},{6,7},{8,9},{9,10},{10,11},{12,13},{... | collective-permute-start | bytes 12296 | tf_op jit(solution)/shard_map/ppermute | solution.py:19
  214.5 7.9 %collective-permute-start.3 = (f32[4,7,16,128]{3,2,1,0:T(8,128)S(1)}, f32[4,7,16,128]{3,2,1,0:T(8,128)S(1)}, u32[]{:S(2)}, u32[]{:S(2)}) collective-permute-start(f32[4,7,16,128]{3,2,1,0:T(8,128)S(1)} %get-tuple-element.69), channel_id=1, source_target_pairs={{0,8},{8,16},{16,24},{1,9},{9,17},{17,25},{2,10},{10,18},{18,26},{... | collective-permute-start | bytes 688136 | tf_op jit(solution)/shard_map/ppermute | solution.py:27
  218.9 11.2 %collective-permute-start.4 = (f32[4,7,16,128]{3,2,1,0:T(8,128)S(1)}, f32[4,7,16,128]{3,2,1,0:T(8,128)S(1)}, u32[]{:S(2)}, u32[]{:S(2)}) collective-permute-start(f32[4,7,16,128]{3,2,1,0:T(8,128)S(1)} %get-tuple-element.70), channel_id=1, source_target_pairs={{8,0},{16,8},{24,16},{9,1},{17,9},{25,17},{10,2},{18,10},{26,18},{... | collective-permute-start | bytes 688136 | tf_op jit(solution)/shard_map/ppermute | solution.py:30
  222.5 12.9 %copy-start.1 = (f32[4,7,16,128]{3,2,1,0:T(8,128)}, f32[4,7,16,128]{3,2,1,0:T(8,128)S(1)}, u32[]{:S(2)}) copy-start(f32[4,7,16,128]{3,2,1,0:T(8,128)S(1)} %collective-permute-done.3) | copy-start | bytes 688132
  230.1 5.3 %copy-start.3 = (f32[4,7,16,128]{3,2,1,0:T(8,128)}, f32[4,7,16,128]{3,2,1,0:T(8,128)S(1)}, u32[]{:S(2)}) copy-start(f32[4,7,16,128]{3,2,1,0:T(8,128)S(1)} %collective-permute-done.4) | copy-start | bytes 688132
  230.3 2.8 collective-permute-start.5
  231.6 3.8 %collective-permute-start.6 = (f32[4,30,7,128]{3,2,1,0:T(8,128)S(1)}, f32[4,30,7,128]{3,2,1,0:T(8,128)S(1)}, u32[]{:S(2)}, u32[]{:S(2)}) collective-permute-start(f32[4,30,7,128]{3,2,1,0:T(8,128)S(1)} %get-tuple-element.68), channel_id=1, source_target_pairs={{4,0},{5,1},{6,2},{7,3},{12,8},{13,9},{14,10},{15,11},{20,16},{21,... | collective-permute-start | bytes 1290248 | tf_op jit(solution)/shard_map/ppermute | solution.py:30
  240.8 13.7 %collective-permute-start.7 = (f32[4,30,30,7]{2,0,3,1:T(4,128)}, f32[4,30,30,7]{2,0,3,1:T(4,128)}, u32[]{:S(2)}, u32[]{:S(2)}) collective-permute-start(f32[4,30,30,7]{2,0,3,1:T(4,128)} %copy.276), channel_id=1, source_target_pairs={{0,1},{1,2},{2,3},{4,5},{5,6},{6,7},{8,9},{9,10},{10,11},{12,13},{... | collective-permute-start | bytes 302408 | tf_op jit(solution)/shard_map/ppermute | solution.py:27
  247.1 13.9 %collective-permute-start.8 = (f32[4,30,30,7]{2,0,3,1:T(4,128)}, f32[4,30,30,7]{2,0,3,1:T(4,128)}, u32[]{:S(2)}, u32[]{:S(2)}) collective-permute-start(f32[4,30,30,7]{2,0,3,1:T(4,128)} %copy.277), channel_id=1, source_target_pairs={{1,0},{2,1},{3,2},{5,4},{6,5},{7,6},{9,8},{10,9},{11,10},{13,12},{... | collective-permute-start | bytes 302408 | tf_op jit(solution)/shard_map/ppermute | solution.py:30
  268.5 1.5 copy-start
  268.5 1.5 copy-start.2
  268.5 1.6 copy-start.4
  268.5 1.6 copy-start.6
  324.2 17.3 %copy-start.7 = (s32[1,32]{1,0:T(1,128)S(1)}, s32[1,32]{1,0:T(1,128)}, u32[]{:S(2)}) copy-start(s32[1,32]{1,0:T(1,128)} %param.11) | copy-start | bytes 388
  331.8 9.6 %all-to-all-start.2 = ((f32[32,1,32]{2,1,0:T(1,128)}), f32[32,1,32]{2,1,0:T(1,128)S(1)}, u32[]{:S(2)}, u32[]{:S(2)}) async-start(f32[32,1,32]{2,1,0:T(1,128)} %bitcast.42), calls=%async_computation.2 | async-start | bytes 32768 | tf_op jit(solution)/shard_map/all_to_all | solution.py:156
where the time goes:
time: 346 us; the launch traced here: 342 us
  other arithmetic  164 us (47%)
  local copies, waits for them, and re-layouts  89.6 us (26%)
  starting transfers between devices  46.1 us (13%)
  waiting for transfers between devices  40.7 us (12%)
    scatter-add x8, other arithmetic, on_device(): volume = volume.at[:, linear_at.reshape(-1)].add(contrib)  143 us
    gather x16, local copies, waits for them, and re-layouts, on_device(): extended[linear_at]  49.7 us
    ppermute x3, starting transfers between devices, shifted(): return lax.ppermute(shard, axis, pairs)  18.3 us
    ppermute x3, waiting for transfers between devices, with_halo(): lax.ppermute(lax.slice_in_dim(block, 0, width, axis=dim), axis, backward)  14.6 us
    scatter-add x1, local copies, waits for them, and re-layouts, on_device(): volume = volume.at[:, linear_at.reshape(-1)].add(contrib)  10.8 us
    ppermute x3, starting transfers between devices, with_halo(): lax.ppermute(lax.slice_in_dim(block, block.shape[dim] - width, None, axis...  10.4 us
    ppermute x3, waiting for transfers between devices, with_halo(): lax.ppermute(lax.slice_in_dim(block, block.shape[dim] - width, None, axis...  8.12 us
    all_to_all x1, starting transfers between devices, on_device(): lax.all_to_all(point_cells, ('gx', 'gy', 'gz'), split_axis=1, concat_axis...  7.3 us
  transfers between devices with their start and end apart: 12, of which 11 were waited for; matrix products, arithmetic and copies ran while one was open for 4% of the time, Pallas kernels for 0%

commit v1 on v0

v1 whole, which is shorter than its diff:
```python
import functools

import jax
import jax.numpy as jnp
from jax import lax
from jax.experimental import pallas as pl
from jax.experimental.pallas import tpu as pltpu
from jax.sharding import PartitionSpec as P

CX = 16
CY = 16
CZ = 128
ITERS = 6

base_screen = 0.25
point_screen = 4.0

AXES = ("gx", "gy", "gz")
REACH = ITERS - 1
XO = REACH
YO = 9
ZO = 8
YS = 32
XPT = 128 // YS
XTILES = -(-(CX + 2 * REACH + 1) // XPT)
LANES = XTILES * 128
ROWS = CZ + 16
CENTER = tuple(range((XO - 1) // XPT, (XO + CX + 1) // XPT + 1))
LOWER = tuple(range(0, (XO + 1) // XPT + 1))
UPPER = tuple(range((XO + CX - 1) // XPT, XTILES))
WINDOW_LOW = YO - REACH
WINDOW_HIGH = YO + CY - 1
UP_AT = ZO + CZ - REACH
DOWN_AT = ZO - 1
HALO = 8
GROUPS = 8
VMEM_LIMIT = 56 * 1024 * 1024

f32 = jnp.float32
bf16 = jnp.bfloat16


def split(value):
    high = value.astype(bf16)
    return high, (value - high.astype(f32)).astype(bf16)


def dot_nt(lhs, rhs):
    return lax.dot_general(lhs, rhs, (((1,), (1,)), ((), ())), preferred_element_type=f32)


def dot_nn(lhs, rhs):
    return lax.dot_general(lhs, rhs, (((1,), (0,)), ((), ())), preferred_element_type=f32)


def other_count(gy):
    return min(gy - 1, 2)


def extra_place(brick, bricks):
    return bricks + brick // 4, 2 * (brick % 4)


def pack_kernel(shape, data_ref, cells_ref, counts_ref, out_ref, main, extra):
    gx, gy, gz = shape
    slots = data_ref.shape[3]
    lane = lax.broadcasted_iota(jnp.int32, (1, slots), 1)
    others = other_count(gy)
    bricks = 3 * (1 + others)
    for d in range(gx * gy * gz):
        block = data_ref[0, d]
        cell = cells_ref[0, d].astype(f32)
        weight = jnp.where(lane < counts_ref[0, d], block[3:4], 0.0)
        main[d, 0:3] = block[0:3] * (-0.5 * weight)
        main[d, 3:4] = weight
        main[d, 4:7] = block[4:7]
        main[d, 7:8] = cell[0:1]
        extra[d] = cell[1:3]
    out_ref[...] = jnp.zeros_like(out_ref)
    for d in range(gx * gy * gz):
        x, y, z = d // (gy * gz), (d // gz) % gy, d % gz
        if others == 0:
            ys = (y,)
        elif others == 1:
            ys = (y, 1 - y)
        else:
            ys = (y, y - 1, y + 1)
        for e, by in enumerate(ys):
            for o, bx in enumerate((x, x - 1, x + 1)):
                if not (0 <= bx < gx and 0 <= by < gy):
                    continue
                b = e * 3 + o
                source = (bx * gy + by) * gz + z
                tile, part = b // 4, b % 4
                out_ref[d, 8 * tile : 8 * tile + 8, slots * part : slots * part + slots] = main[source]
                place, row = extra_place(b, bricks)
                tile, part = place // 4, place % 4
                out_ref[
                    d, 8 * tile + row : 8 * tile + row + 2, slots * part : slots * part + slots
                ] = extra[source]


def hat(coordinate, cell, low, high):
    away = coordinate - cell
    return jnp.where(away == 0.0, low, jnp.where(away == 1.0, high, 0.0))


def hat_slope(coordinate, cell, low, high):
    away = coordinate - cell
    rising = jnp.where(away == -1.0, low, jnp.where(away == 0.0, high, 0.0))
    return rising - jnp.where(away == 1.0, low, jnp.where(away == 2.0, high, 0.0))


def row_iota(rows):
    return lax.broadcasted_iota(jnp.int32, (rows, 128), 0).astype(f32)


def splat_kernel(
    shape, recv_ref, rhs_ref, density_ref, up_ref, down_ref, own_ref,
    points, high_ref, low_ref, hz_ref, hx_ref, wide,
):
    gx, gy, gz = shape
    mx, my, mz = lax.axis_index("gx"), lax.axis_index("gy"), lax.axis_index("gz")
    step = pl.program_id(0)
    others = other_count(gy)
    bricks = 3 * (1 + others)
    tiles = recv_ref.shape[2] // 8
    lane = lax.broadcasted_iota(jnp.int32, (8, 128), 1)
    lane_part = lane // 32

    @pl.when(step == 0)
    def _():
        wide[...] = jnp.zeros_like(wide)

    for t in range(tiles):
        for g in range(GROUPS):
            given = [recv_ref[q, g, 8 * t : 8 * t + 8, :] for q in range(4)]
            for k in range(4):
                if 4 * t + k >= bricks + -(-bricks // 4):
                    continue
                merged = None
                for q in range(4):
                    moved = given[q] if q == k else pltpu.roll(given[q], (32 * (q - k)) % 128, 1)
                    merged = moved if merged is None else jnp.where(lane_part == q, moved, merged)
                points[4 * t + k, g] = merged
    own_ref[0] = points[0]
    own_ref[1] = points[bricks]

    z_limit = jnp.where(mz == gz - 1, CZ, CZ + 1).astype(f32)
    z_row = row_iota(ROWS) - float(ZO)
    own_row = row_iota(24) + float(8 - YO)

    for e in range(1 + others):
        if e == 0:
            y_limit = jnp.where(my == gy - 1, CY, CY + 1).astype(f32)
            y_row = own_row
        else:
            if others == 1:
                above = my == 0
            else:
                above = e == 2
            y_limit = jnp.where(
                jnp.logical_and(above, my + 1 == gy - 1), CY, CY + 1
            ).astype(f32)
            window = jnp.where(above, WINDOW_HIGH, WINDOW_LOW)
            first = jnp.where(above, WINDOW_HIGH - YO - CY, WINDOW_LOW - YO + CY)
            y_row = row_iota(8) + first.astype(f32)
        for o, (shift, x_tiles) in enumerate(((0, CENTER), (-1, LOWER), (1, UPPER))):
            b = e * 3 + o
            place, row = extra_place(b, bricks)
            x_limit = jnp.where(mx + shift == gx - 1, CX, CX + 1).astype(f32)
            cell_x = points[b, :, 7, :]
            off_x = points[b, :, 6 - 2, :]
            low_x = 1.0 - off_x
            high_x = jnp.where(cell_x + 1.0 < x_limit, off_x, 0.0)
            planes = [XPT * t + i for t in x_tiles for i in range(XPT)]
            for n, plane in enumerate(planes):
                at = float(plane - XO - CX * shift)
                hx_ref[0, n] = hat(at, cell_x, low_x, high_x)
                hx_ref[1, n] = hat_slope(at, cell_x, low_x, high_x)
            y_parts = []
            for g in range(GROUPS):
                main = points[b, g]
                more = points[place, g]
                cell_y, cell_z = more[row : row + 1], more[row + 1 : row + 2]
                off_y, off_z = main[5:6], main[6:7]
                high_z = jnp.where(cell_z + 1.0 < z_limit, off_z, 0.0)
                hz_high, hz_low = split(hat(z_row, cell_z, 1.0 - off_z, high_z))
                hz_ref[0:ROWS, 128 * g : 128 * g + 128] = hz_high
                hz_ref[ROWS : 2 * ROWS, 128 * g : 128 * g + 128] = hz_low
                high_y = jnp.where(cell_y + 1.0 < y_limit, off_y, 0.0)
                hy = hat(y_row, cell_y, 1.0 - off_y, high_y)
                dy = hat_slope(y_row, cell_y, 1.0 - off_y, high_y)
                y_parts.append((main[0:1] * hy, main[1:2] * dy, main[2:3] * hy, main[3:4] * hy))
            if e == 0:
                blocks = [(t,) for t in x_tiles]
            else:
                blocks = [x_tiles[i : i + 4] for i in range(0, len(x_tiles), 4)]
            for n, block in enumerate(blocks):
                base = 384 * n
                for g in range(GROUPS):
                    part_x0, part_y1, part_z, part_w = y_parts[g]
                    at = slice(128 * g, 128 * g + 128)
                    for i in range(XPT):
                        rows = ([], [], [])
                        for t in block:
                            plane = planes.index(XPT * t + i)
                            hx = hx_ref[0, plane, g : g + 1, :]
                            dx = hx_ref[1, plane, g : g + 1, :]
                            rows[0].append(dx * part_x0 + hx * part_y1)
                            rows[1].append(hx * part_z)
                            rows[2].append(hx * part_w)
                        for c in range(3):
                            have = sum(v.shape[0] for v in rows[c])
                            pad = [jnp.zeros((YS - have, 128), f32)] if have < YS else []
                            full = pad + rows[c] if e == 0 else rows[c] + pad
                            full = jnp.concatenate(full, axis=0) if len(full) > 1 else full[0]
                            high, low = split(full)
                            start = base + 128 * c + YS * i
                            high_ref[start : start + YS, at] = high
                            low_ref[start : start + YS, at] = low
            for n, block in enumerate(blocks):
                span = slice(384 * n, 384 * n + 384)
                both = dot_nt(hz_ref[...], high_ref[span, :])
                got = both[:ROWS] + both[ROWS:] + dot_nt(hz_ref[0:ROWS, :], low_ref[span, :])
                for k, t in enumerate(block):
                    for c in range(3):
                        value = got[:, 128 * c : 128 * c + 128]
                        if e > 0:
                            value = pltpu.roll(value, window + (128 - 8 * k), 1)
                            in_group = lax.broadcasted_iota(jnp.int32, (ROWS, 128), 1) % YS
                            inside = jnp.logical_and(in_group >= window, in_group < window + 8)
                            value = jnp.where(inside, value, 0.0)
                        wide[c, :, 128 * t : 128 * t + 128] += value

    @pl.when(step == pl.num_programs(0) - 1)
    def _():
        for t in range(XTILES):
            at = slice(128 * t, 128 * t + 128)
            along_z = wide[1, :, at]
            rhs_ref[:, at] = (
                wide[0, :, at]
                + pltpu.roll(along_z, ROWS - 1, 0)
                - pltpu.roll(along_z, 1, 0)
            )
            density_ref[:, at] = wide[2, :, at]
        up_ref[0] = rhs_ref[UP_AT : UP_AT + HALO, :]
        up_ref[1] = density_ref[UP_AT : UP_AT + HALO, :]
        down_ref[0] = rhs_ref[DOWN_AT : DOWN_AT + HALO, :]
        down_ref[1] = density_ref[DOWN_AT : DOWN_AT + HALO, :]


def chebyshev_factors():
    half_width = 6.0 / (6.0 + base_screen)
    sigma_ratio = 1.0 / half_width
    rho_prev = half_width
    factors = []
    for _ in range(ITERS - 1):
        rho_next = 1.0 / (2.0 * sigma_ratio - rho_prev)
        factors.append((rho_next * rho_prev, 2.0 * rho_next / half_width))
        rho_prev = rho_next
    return factors


def solve_kernel(
    shape, rhs_ref, density_ref, from_low_ref, from_high_ref, own_ref,
    indicator_ref, values_ref,
    first, second, scaled, inverse, total, edge, high_ref, low_ref,
):
    gx, gy, gz = shape
    mx, my, mz = lax.axis_index("gx"), lax.axis_index("gy"), lax.axis_index("gz")
    edge[...] = jnp.zeros_like(edge)
    low_at, high_at = UP_AT - CZ, DOWN_AT + CZ - (ROWS - 16)
    edge[0, :, low_at : low_at + HALO, :] = from_low_ref[...]
    edge[1, :, high_at : high_at + HALO, :] = from_high_ref[...]

    def with_edge(ref, channel, i):
        value = ref[8 * i : 8 * i + 8, :]
        if i < 2:
            return value + edge[0, channel, 8 * i : 8 * i + 8, :]
        if i >= ROWS // 8 - 2:
            at = 8 * (i - ROWS // 8 + 2)
            return value + edge[1, channel, at : at + 8, :]
        return value

    lane = lax.broadcasted_iota(jnp.int32, (8, LANES), 1)
    x, y = lane // YS - XO + mx * CX, lane % YS - YO + my * CY
    inside_xy = (x >= 0) & (x < gx * CX) & (y >= 0) & (y < gy * CY)
    zero = jnp.zeros((8, LANES), f32)
    first[0:8, :] = zero
    first[ROWS + 8 : ROWS + 16, :] = zero
    second[0:8, :] = zero
    second[ROWS + 8 : ROWS + 16, :] = zero
    for i in range(ROWS // 8):
        at = slice(8 * i, 8 * i + 8)
        z = lax.broadcasted_iota(jnp.int32, (8, LANES), 0) + (8 * i - ZO) + mz * CZ
        inside = inside_xy & (z >= 0) & (z < gz * CZ)
        diagonal = 6.0 + base_screen + point_screen * with_edge(density_ref, 1, i)
        inv = jnp.where(inside, 1.0 / diagonal, 0.0)
        start = with_edge(rhs_ref, 0, i) * inv
        inverse[at, :] = inv
        scaled[at, :] = start
        total[at, :] = start
        first[8 * i + 8 : 8 * i + 16, :] = start

    now, later = first, second
    factors = chebyshev_factors()
    for k, (keep, gain) in enumerate(factors):
        last = k + 1 == len(factors)
        for i in range(ROWS // 8):
            at = slice(8 * i, 8 * i + 8)
            here = now[8 * i + 8 : 8 * i + 16, :]
            near = now[8 * i + 7 : 8 * i + 15, :] + now[8 * i + 9 : 8 * i + 17, :]
            near = near + pltpu.roll(here, 1, 1) + pltpu.roll(here, LANES - 1, 1)
            near = near + pltpu.roll(here, YS, 1) + pltpu.roll(here, LANES - YS, 1)
            left = scaled[at, :] - here + inverse[at, :] * near
            ahead = keep * here + gain * left
            total[at, :] += ahead
            if not last:
                scaled[at, :] = left
                later[8 * i + 8 : 8 * i + 16, :] = ahead
        now, later = later, now

    for t in CENTER:
        turned = total[ZO : ZO + CZ, 128 * t : 128 * t + 128].T
        for i in range(XPT):
            plane = XPT * t + i - XO
            if 0 <= plane < CX:
                indicator_ref[plane] = turned[YS * i + YO : YS * i + YO + CY, :]

    groups = own_ref.shape[1]
    first_lane, end_lane = 128 * CENTER[0], 128 * CENTER[-1] + 128
    depth = end_lane - first_lane
    u_high, u_low = split(total[:, first_lane:end_lane])
    z_row = row_iota(ROWS) - float(ZO)
    y_row = row_iota(24) + float(8 - YO)
    blank = jnp.zeros((8, 128), f32)
    for chunk in range(groups // GROUPS):
        for g in range(GROUPS):
            main = own_ref[0, chunk * GROUPS + g]
            more = own_ref[1, chunk * GROUPS + g]
            off_x, off_y = main[4:5], main[5:6]
            hy = hat(y_row, more[0:1], 1.0 - off_y, off_y)
            at = slice(128 * g, 128 * g + 128)
            for plane in range(XPT * CENTER[0], XPT * CENTER[-1] + XPT):
                start = YS * plane - first_lane
                if 0 <= plane - XO <= CX:
                    hx = hat(float(plane - XO), main[7:8], 1.0 - off_x, off_x)
                    high, low = split(jnp.concatenate([blank, hx * hy], axis=0))
                else:
                    high = jnp.zeros((YS, 128), bf16)
                    low = high
                high_ref[start : start + YS, at] = high
                low_ref[start : start + YS, at] = low
        got = dot_nn(u_high, high_ref[...]) + dot_nn(u_low, high_ref[...])
        got = got + dot_nn(u_high, low_ref[...])
        rows = []
        for g in range(GROUPS):
            main = own_ref[0, chunk * GROUPS + g]
            more = own_ref[1, chunk * GROUPS + g]
            off_z = main[6:7]
            hz = hat(z_row, more[1:2], 1.0 - off_z, off_z)
            value = jnp.sum(hz * got[:, 128 * g : 128 * g + 128], axis=0, keepdims=True)
            rows.append(jnp.where(main[3:4] > 0.0, value, 0.0))
        values = jnp.concatenate(rows, axis=0)
        for q in range(4):
            moved = values if q == 0 else pltpu.roll(values, 128 - 32 * q, 1)
            start = q * groups + chunk * GROUPS
            values_ref[start : start + GROUPS, :] = moved[:, 0:32]


def on_device(shape, point_data, point_cells, send_counts):
    gx, gy, gz = shape
    sources = gx * gy * gz
    slots = point_data.shape[3]
    bricks = 3 * (1 + other_count(gy))
    rows = 8 * -(-(bricks + -(-bricks // 4)) // 4)
    groups = sources // 4
    params = pltpu.CompilerParams(vmem_limit_bytes=VMEM_LIMIT)
    whole = pl.BlockSpec(memory_space=pltpu.VMEM)

    outgoing = pl.pallas_call(
        functools.partial(pack_kernel, shape),
        out_shape=jax.ShapeDtypeStruct((sources, rows, 128), f32),
        in_specs=[whole, whole, pl.BlockSpec(memory_space=pltpu.SMEM)],
        out_specs=whole,
        scratch_shapes=[
            pltpu.VMEM((sources, 8, slots), f32),
            pltpu.VMEM((sources, 2, slots), f32),
        ],
        compiler_params=params,
        name="pack_points",
    )(point_data, point_cells, send_counts)

    arrived = lax.all_to_all(outgoing, AXES, split_axis=0, concat_axis=0, tiled=True)
    arrived = arrived.reshape(4, groups, rows, 128)

    most = 384 * len(CENTER)
    wide_shape = jax.ShapeDtypeStruct((ROWS, LANES), f32)
    edge_shape = jax.ShapeDtypeStruct((2, HALO, LANES), f32)
    steps = groups // GROUPS
    rhs, density, up, down, own = pl.pallas_call(
        functools.partial(splat_kernel, shape),
        grid=(steps,),
        out_shape=(
            wide_shape, wide_shape, edge_shape, edge_shape,
            jax.ShapeDtypeStruct((2, groups, 8, 128), f32),
        ),
        in_specs=[pl.BlockSpec((4, GROUPS, rows, 128), lambda s: (0, s, 0, 0))],
        out_specs=(
            pl.BlockSpec((ROWS, LANES), lambda s: (0, 0)),
            pl.BlockSpec((ROWS, LANES), lambda s: (0, 0)),
            pl.BlockSpec((2, HALO, LANES), lambda s: (0, 0, 0)),
            pl.BlockSpec((2, HALO, LANES), lambda s: (0, 0, 0)),
            pl.BlockSpec((2, GROUPS, 8, 128), lambda s: (0, s, 0, 0)),
        ),
        scratch_shapes=[
            pltpu.VMEM((rows // 2, GROUPS, 8, 128), f32),
            pltpu.VMEM((most, 128 * GROUPS), bf16),
            pltpu.VMEM((most, 128 * GROUPS), bf16),
            pltpu.VMEM((2 * ROWS, 128 * GROUPS), bf16),
            pltpu.VMEM((2, XPT * len(CENTER), GROUPS, 128), f32),
            pltpu.VMEM((3, ROWS, LANES), f32),
        ],
        compiler_params=params,
        name="splat_points",
    )(arrived)

    from_low = lax.ppermute(up, "gz", [(i, i + 1) for i in range(gz - 1)])
    from_high = lax.ppermute(down, "gz", [(i + 1, i) for i in range(gz - 1)])

    depth = 128 * len(CENTER)
    indicator, values = pl.pallas_call(
        functools.partial(solve_kernel, shape),
        out_shape=(
            jax.ShapeDtypeStruct((CX, CY, CZ), f32),
            jax.ShapeDtypeStruct((sources, slots), f32),
        ),
        in_specs=[whole] * 5,
        out_specs=(whole, whole),
        scratch_shapes=[
            pltpu.VMEM((ROWS + 16, LANES), f32),
            pltpu.VMEM((ROWS + 16, LANES), f32),
            pltpu.VMEM((ROWS, LANES), f32),
            pltpu.VMEM((ROWS, LANES), f32),
            pltpu.VMEM((ROWS, LANES), f32),
            pltpu.VMEM((2, 2, 16, LANES), f32),
            pltpu.VMEM((depth, 128 * GROUPS), bf16),
            pltpu.VMEM((depth, 128 * GROUPS), bf16),
        ],
        compiler_params=params,
        name="solve_and_read",
    )(rhs, density, from_low, from_high, own)

    returned = lax.all_to_all(values, AXES, split_axis=0, concat_axis=0, tiled=True)
    return indicator, returned.reshape(1, sources, slots)


def solution(mesh):
    shape = tuple(mesh.shape[axis] for axis in AXES)
    in_specs = (
        P(AXES, None, None, None),
        P(AXES, None, None, None),
        P(AXES, None),
    )
    out_specs = (P("gx", "gy", "gz"), P(AXES, None, None))
    return jax.shard_map(
        functools.partial(on_device, shape),
        mesh=mesh,
        in_specs=in_specs,
        out_specs=out_specs,
        check_vma=False,
    )
```

time: 346 us -> 63.8 us (0.18)
  other arithmetic: 164 us -> 0 us
  local copies, waits for them, and re-layouts: 89.6 us -> 3.46 us
  starting transfers between devices: 46.1 us -> 4.47 us
  waiting for transfers between devices: 40.7 us -> 4.98 us
  blocking collectives: 0 us -> 27.2 us
  Pallas kernels: 0 us -> 22.6 us
    scatter-add x9 -> x0, other arithmetic: 143 us -> none  [the longest x8 143 us: on_device(): volume = volume.at[:, linear_at.reshape(-1)].add(contrib)]
    gather x16 -> x0, local copies, waits for them, and re-layouts: 49.7 us -> none  [on_device(): extended[linear_at]]
    ppermute x9 -> x2, starting transfers between devices: 32.6 us -> 4.47 us  [the longest x1 3.17 us: on_device(): from_low = lax.ppermute(up, 'gz', [(i, i + 1) for i in range(gz - 1)])]
    all_to_all x0 -> x2, blocking collectives: none -> 27.2 us  [the longest x1 17.6 us: on_device(): lax.all_to_all(outgoing, AXES, split_axis=0, concat_axis=0, tiled=True)]
    pallas_call x0 -> x3, Pallas kernels: none -> 22.6 us  [the longest x1 14.3 us: on_device(): pl.pallas_call(functools.partial(splat_kernel, shape), grid=(steps,), out...]
    ppermute x9 -> x2, waiting for transfers between devices: 26.1 us -> 4.98 us  [the longest x1 4.15 us: on_device(): from_high = lax.ppermute(down, 'gz', [(i + 1, i) for i in range(gz - 1)])]
    all_to_all x3 -> x0, waiting for transfers between devices: 14.6 us -> none  [the longest x1 6.34 us: on_device(): lax.all_to_all(values.reshape(brick_count, 1, slot_count), ('gx', 'gy', '...]
    all_to_all x3 -> x0, starting transfers between devices: 13.5 us -> none  [the longest x1 7.3 us: on_device(): lax.all_to_all(point_cells, ('gx', 'gy', 'gz'), split_axis=1, concat_axis...]
  transfers between devices with their start and end apart: 12 -> 2, of which waited for: 11 -> 2; matrix products, arithmetic and copies ran while one was open for 4% -> 0% of each run, Pallas kernels for 0% -> 0%
where the time goes in v1:
time: 63.8 us; the launch traced here: 63.4 us
  blocking collectives  27.2 us (43%)
  Pallas kernels  22.6 us (35%)
  waiting for transfers between devices  4.98 us (8%)
  starting transfers between devices  4.47 us (7%)
  local copies, waits for them, and re-layouts  3.46 us (5%)
  between operations  0.66 us (1%)
    all_to_all x1, blocking collectives, on_device(): lax.all_to_all(outgoing, AXES, split_axis=0, concat_axis=0, tiled=True)  17.6 us
    pallas_call x1, Pallas kernels, on_device(): pl.pallas_call(functools.partial(splat_kernel, shape), grid=(steps,), out...  14.3 us
    all_to_all x1, blocking collectives, on_device(): lax.all_to_all(values, AXES, split_axis=0, concat_axis=0, tiled=True)  9.63 us
    pallas_call x1, Pallas kernels, on_device(): pl.pallas_call(functools.partial(solve_kernel, shape), out_shape=(jax.Sha...  6.31 us
    ppermute x1, waiting for transfers between devices, on_device(): from_high = lax.ppermute(down, 'gz', [(i + 1, i) for i in range(gz - 1)])  4.15 us
    unnamed x9, local copies, waits for them, and re-layouts  3.46 us
    ppermute x1, starting transfers between devices, on_device(): from_low = lax.ppermute(up, 'gz', [(i, i + 1) for i in range(gz - 1)])  3.17 us
    pallas_call x1, Pallas kernels, on_device(): pl.pallas_call(functools.partial(pack_kernel, shape), out_shape=jax.Shape...  2 us
  transfers between devices with their start and end apart: 2, of which 2 were waited for; matrix products, arithmetic and copies ran while one was open for 0% of the time, Pallas kernels for 0%

profile of v1, /device:TPU:0, one launch (start us, length us, event | category | flops | bytes accessed | tf_op | source)
XLA Modules:
  0.0 63.4 jit_solution(13161005343891309522)
XLA Ops:
  0.6 0.0 copy-start
  0.6 1.5 %copy.8.cells_ref = s32[1,32,3,32]{3,2,1,0:T(4,128)} copy(s32[1,32,3,32]{3,1,2,0:T(8,128)} %param.4) | data formatting | bytes 24576 | tf_op args[1]
  2.1 0.0 copy-done
  2.1 0.7 %copy.7.data_ref = f32[1,32,7,32]{3,2,1,0:T(8,128)} copy(f32[1,32,7,32]{3,1,2,0:T(8,128)S(1)} %copy-done) | data formatting | bytes 57344 | tf_op args[0]
  2.9 2.0 %pack_points.1 = f32[32,16,128]{2,1,0:T(8,128)} custom-call(f32[1,32,7,32]{3,2,1,0:T(8,128)} %copy.7.data_ref, s32[1,32,3,32]{3,2,1,0:T(4,128)} %copy.8.cells_ref, s32[1,32]{1,0:T(1,128)} %counts_ref.1), custom_call_target="tpu_custom_call" | custom-call | tf_op jit(solution)/shard_map/pack_points/pallas_call | solution.py:382
  4.9 17.6 %all_to_all.14 = f32[32,16,128]{2,1,0:T(8,128)} all-to-all(f32[32,16,128]{2,1,0:T(8,128)} %pack_points.1), channel_id=1, replica_groups=mesh['gx'=4,'gy'=2,'gz'=4] {'gx','gy','gz'}, dimensions={0} | all-to-all | bytes 524288 | tf_op jit(solution)/shard_map/all_to_all | solution.py:395
  22.5 14.3 %splat_points.1 = (f32[144,896]{1,0:T(8,128)}, f32[144,896]{1,0:T(8,128)}, f32[2,8,896]{2,1,0:T(8,128)}, f32[2,8,896]{2,1,0:T(8,128)}, f32[2,8,8,128]{3,2,1,0:T(8,128)}) custom-call(f32[4,8,16,128]{3,2,1,0:T(8,128)} %bitcast.5), custom_call_target="tpu_custom_call" | custom-call | tf_op jit(solution)/shard_map/splat_points/pallas_call | solution.py:402
  36.8 3.2 %collective-permute-start = (f32[2,8,896]{2,1,0:T(8,128)}, f32[2,8,896]{2,1,0:T(8,128)S(1)}, u32[]{:S(2)}, u32[]{:S(2)}) collective-permute-start(f32[2,8,896]{2,1,0:T(8,128)} %get-tuple-element.11), channel_id=1, source_target_pairs={{0,1},{1,2},{2,3},{4,5},{5,6},{6,7},{8,9},{9,10},{10,11},{12,13},{... | collective-permute-start | bytes 172040 | tf_op jit(solution)/shard_map/ppermute | solution.py:429
  40.0 1.3 %collective-permute-start.1 = (f32[2,8,896]{2,1,0:T(8,128)}, f32[2,8,896]{2,1,0:T(8,128)S(1)}, u32[]{:S(2)}, u32[]{:S(2)}) collective-permute-start(f32[2,8,896]{2,1,0:T(8,128)} %get-tuple-element.12), channel_id=1, source_target_pairs={{1,0},{2,1},{3,2},{5,4},{6,5},{7,6},{9,8},{10,9},{11,10},{13,12},{... | collective-permute-start | bytes 172040 | tf_op jit(solution)/shard_map/ppermute | solution.py:430
  41.3 0.8 %collective-permute-done.from_low_ref = f32[2,8,896]{2,1,0:T(8,128)S(1)} collective-permute-done((f32[2,8,896]{2,1,0:T(8,128)}, f32[2,8,896]{2,1,0:T(8,128)S(1)}, u32[]{:S(2)}, u32[]{:S(2)}) %collective-permute-start) | collective-permute-done | bytes 57376 | tf_op jit(solution)/shard_map/ppermute | solution.py:429
  42.1 0.0 copy-start.1
  42.1 4.2 %collective-permute-done.1.from_high_ref = f32[2,8,896]{2,1,0:T(8,128)S(1)} collective-permute-done((f32[2,8,896]{2,1,0:T(8,128)}, f32[2,8,896]{2,1,0:T(8,128)S(1)}, u32[]{:S(2)}, u32[]{:S(2)}) %collective-permute-start.1) | collective-permute-done | bytes 57376 | tf_op jit(solution)/shard_map/ppermute | solution.py:430
  46.3 0.0 copy-start.2
  46.3 0.0 copy-done.1
  46.3 0.6 copy-done.2
  46.9 6.3 %solve_and_read.1 = (f32[16,16,128]{2,1,0:T(8,128)}, f32[32,32]{1,0:T(8,128)}) custom-call(f32[144,896]{1,0:T(8,128)} %get-tuple-element.9.rhs_ref, f32[144,896]{1,0:T(8,128)} %get-tuple-element.10.density_ref, f32[2,8,896]{2,1,0:T(8,128)} %copy-done.1, f32[2,8,896]{2,1,0:T(8,128)} %copy-done.2, f32[2,8,8,128]{3,2,1,0:T(8,128)} %get-tuple-element.13.own_ref), custom_call_target="tpu_custom_call" | custom-call | tf_op jit(solution)/shard_map/solve_and_read/pallas_call | solution.py:433
  53.2 9.6 %all_to_all.15 = f32[32,1,32]{2,1,0:T(1,128)S(1)} all-to-all(f32[32,1,32]{2,1,0:T(1,128)} %bitcast.7), channel_id=1, replica_groups=mesh['gx'=4,'gy'=2,'gz'=4] {'gx','gy','gz'}, dimensions={0} | all-to-all | bytes 8192 | tf_op jit(solution)/shard_map/all_to_all | solution.py:455
  62.8 0.6 copy.11
Async XLA Ops:
  0.6 1.5 %copy-start = (f32[1,32,7,32]{3,1,2,0:T(8,128)S(1)}, f32[1,32,7,32]{3,1,2,0:T(8,128)}, u32[]{:S(2)}) copy-start(f32[1,32,7,32]{3,1,2,0:T(8,128)} %param.3) | copy-start | bytes 86020
  36.8 5.3 %collective-permute-start = (f32[2,8,896]{2,1,0:T(8,128)}, f32[2,8,896]{2,1,0:T(8,128)S(1)}, u32[]{:S(2)}, u32[]{:S(2)}) collective-permute-start(f32[2,8,896]{2,1,0:T(8,128)} %get-tuple-element.11), channel_id=1, source_target_pairs={{0,1},{1,2},{2,3},{4,5},{5,6},{6,7},{8,9},{9,10},{10,11},{12,13},{... | collective-permute-start | bytes 172040 | tf_op jit(solution)/shard_map/ppermute | solution.py:429
  40.0 6.3 %collective-permute-start.1 = (f32[2,8,896]{2,1,0:T(8,128)}, f32[2,8,896]{2,1,0:T(8,128)S(1)}, u32[]{:S(2)}, u32[]{:S(2)}) collective-permute-start(f32[2,8,896]{2,1,0:T(8,128)} %get-tuple-element.12), channel_id=1, source_target_pairs={{1,0},{2,1},{3,2},{5,4},{6,5},{7,6},{9,8},{10,9},{11,10},{13,12},{... | collective-permute-start | bytes 172040 | tf_op jit(solution)/shard_map/ppermute | solution.py:430
  42.1 4.2 %copy-start.1 = (f32[2,8,896]{2,1,0:T(8,128)}, f32[2,8,896]{2,1,0:T(8,128)S(1)}, u32[]{:S(2)}) copy-start(f32[2,8,896]{2,1,0:T(8,128)S(1)} %collective-permute-done.from_low_ref) | copy-start | bytes 172036
  46.3 0.6 copy-start.2

commit v2 on v1

--- a/solution.py
+++ b/solution.py
@@ -25,9 +25,10 @@
 XTILES = -(-(CX + 2 * REACH + 1) // XPT)
 LANES = XTILES * 128
 ROWS = CZ + 16
-CENTER = tuple(range((XO - 1) // XPT, (XO + CX + 1) // XPT + 1))
-LOWER = tuple(range(0, (XO + 1) // XPT + 1))
-UPPER = tuple(range((XO + CX - 1) // XPT, XTILES))
+CENTER = tuple(range(XO - 1, XO + CX + 2))
+LOWER = tuple(range(0, XO + 2))
+UPPER = tuple(range(XO + CX - 1, XO + CX + REACH + 1))
+FIRST_TILE, END_TILE = XO // XPT, (XO + CX) // XPT + 1
 WINDOW_LOW = YO - REACH
 WINDOW_HIGH = YO + CY - 1
 UP_AT = ZO + CZ - REACH
@@ -64,18 +65,18 @@
 def pack_kernel(shape, data_ref, cells_ref, counts_ref, out_ref, main, extra):
     gx, gy, gz = shape
     slots = data_ref.shape[3]
-    lane = lax.broadcasted_iota(jnp.int32, (1, slots), 1)
+    lane = lax.broadcasted_iota(jnp.int32, (gx * gy * gz, slots), 1)
     others = other_count(gy)
     bricks = 3 * (1 + others)
-    for d in range(gx * gy * gz):
-        block = data_ref[0, d]
-        cell = cells_ref[0, d].astype(f32)
-        weight = jnp.where(lane < counts_ref[0, d], block[3:4], 0.0)
-        main[d, 0:3] = block[0:3] * (-0.5 * weight)
-        main[d, 3:4] = weight
-        main[d, 4:7] = block[4:7]
-        main[d, 7:8] = cell[0:1]
-        extra[d] = cell[1:3]
+    weight = jnp.where(lane < counts_ref[...], data_ref[0, 3], 0.0)
+    for c in range(3):
+        main[:, c, :] = data_ref[0, c] * (-0.5 * weight)
+    main[:, 3, :] = weight
+    for c in range(4, 7):
+        main[:, c, :] = data_ref[0, c]
+    main[:, 7, :] = cells_ref[0, 0].astype(f32)
+    extra[:, 0, :] = cells_ref[0, 1].astype(f32)
+    extra[:, 1, :] = cells_ref[0, 2].astype(f32)
     out_ref[...] = jnp.zeros_like(out_ref)
     for d in range(gx * gy * gz):
         x, y, z = d // (gy * gz), (d // gz) % gy, d % gz
@@ -115,22 +116,40 @@
     return lax.broadcasted_iota(jnp.int32, (rows, 128), 0).astype(f32)
 
 
+def stack_rows(parts, multiple):
+    have = sum(part.shape[0] for part in parts)
+    if have % multiple:
+        parts = parts + [jnp.zeros((multiple - have % multiple, 128), f32)]
+    return jnp.concatenate(parts, axis=0) if len(parts) > 1 else parts[0]
+
+
 def splat_kernel(
     shape, recv_ref, rhs_ref, density_ref, up_ref, down_ref, own_ref,
-    points, high_ref, low_ref, hz_ref, hx_ref, wide,
+    points, left_ref, right_ref, hx_ref, near, beside,
 ):
     gx, gy, gz = shape
     mx, my, mz = lax.axis_index("gx"), lax.axis_index("gy"), lax.axis_index("gz")
     step = pl.program_id(0)
+    single = recv_ref.shape[1] * 4 == gx * gy * gz
     others = other_count(gy)
     bricks = 3 * (1 + others)
     tiles = recv_ref.shape[2] // 8
-    lane = lax.broadcasted_iota(jnp.int32, (8, 128), 1)
-    lane_part = lane // 32
-
-    @pl.when(step == 0)
-    def _():
-        wide[...] = jnp.zeros_like(wide)
+    lane_part = lax.broadcasted_iota(jnp.int32, (8, 128), 1) // 32
+    span = 128 * GROUPS
+    written = set()
+
+    def add(ref, place, value):
+        if single and place not in written:
+            written.add(place)
+            ref[place + (slice(None), slice(0, ROWS))] = value
+        else:
+            ref[place + (slice(None), slice(0, ROWS))] += value
+
+    if not single:
+        @pl.when(step == 0)
+        def _():
+            near[...] = jnp.zeros_like(near)
+            beside[...] = jnp.zeros_like(beside)
 
     for t in range(tiles):
         for g in range(GROUPS):
@@ -150,34 +169,31 @@
     z_row = row_iota(ROWS) - float(ZO)
     own_row = row_iota(24) + float(8 - YO)
 
+    row_at = 0
     for e in range(1 + others):
         if e == 0:
             y_limit = jnp.where(my == gy - 1, CY, CY + 1).astype(f32)
             y_row = own_row
         else:
-            if others == 1:
-                above = my == 0
-            else:
-                above = e == 2
+            above = my == 0 if others == 1 else jnp.bool_(e == 2)
             y_limit = jnp.where(
                 jnp.logical_and(above, my + 1 == gy - 1), CY, CY + 1
             ).astype(f32)
-            window = jnp.where(above, WINDOW_HIGH, WINDOW_LOW)
             first = jnp.where(above, WINDOW_HIGH - YO - CY, WINDOW_LOW - YO + CY)
             y_row = row_iota(8) + first.astype(f32)
-        for o, (shift, x_tiles) in enumerate(((0, CENTER), (-1, LOWER), (1, UPPER))):
+        high = y_row.shape[0]
+        for o, (shift, planes) in enumerate(((0, CENTER), (-1, LOWER), (1, UPPER))):
             b = e * 3 + o
             place, row = extra_place(b, bricks)
             x_limit = jnp.where(mx + shift == gx - 1, CX, CX + 1).astype(f32)
             cell_x = points[b, :, 7, :]
-            off_x = points[b, :, 6 - 2, :]
+            off_x = points[b, :, 4, :]
             low_x = 1.0 - off_x
             high_x = jnp.where(cell_x + 1.0 < x_limit, off_x, 0.0)
-            planes = [XPT * t + i for t in x_tiles for i in range(XPT)]
             for n, plane in enumerate(planes):
                 at = float(plane - XO - CX * shift)
-                hx_ref[0, n] = hat(at, cell_x, low_x, high_x)
-                hx_ref[1, n] = hat_slope(at, cell_x, low_x, high_x)
+                hx_ref[b, 0, n] = hat(at, cell_x, low_x, high_x)
+                hx_ref[b, 1, n] = hat_slope(at, cell_x, low_x, high_x)
             y_parts = []
             for g in range(GROUPS):
                 main = points[b, g]
@@ -186,64 +202,82 @@
                 off_y, off_z = main[5:6], main[6:7]
                 high_z = jnp.where(cell_z + 1.0 < z_limit, off_z, 0.0)
                 hz_high, hz_low = split(hat(z_row, cell_z, 1.0 - off_z, high_z))
-                hz_ref[0:ROWS, 128 * g : 128 * g + 128] = hz_high
-                hz_ref[ROWS : 2 * ROWS, 128 * g : 128 * g + 128] = hz_low
+                at = slice(128 * g, 128 * g + 128)
+                right_ref[b, 0, :, at] = hz_high
+                right_ref[b, 1, :, at] = hz_low
                 high_y = jnp.where(cell_y + 1.0 < y_limit, off_y, 0.0)
                 hy = hat(y_row, cell_y, 1.0 - off_y, high_y)
                 dy = hat_slope(y_row, cell_y, 1.0 - off_y, high_y)
                 y_parts.append((main[0:1] * hy, main[1:2] * dy, main[2:3] * hy, main[3:4] * hy))
-            if e == 0:
-                blocks = [(t,) for t in x_tiles]
-            else:
-                blocks = [x_tiles[i : i + 4] for i in range(0, len(x_tiles), 4)]
-            for n, block in enumerate(blocks):
-                base = 384 * n
+            size = 4 if e == 0 else 12
+            for start in range(0, len(planes), size):
+                block = range(start, min(start + size, len(planes)))
+                count = -(-len(block) * high // 16) * 16
                 for g in range(GROUPS):
                     part_x0, part_y1, part_z, part_w = y_parts[g]
                     at = slice(128 * g, 128 * g + 128)
-                    for i in range(XPT):
-                        rows = ([], [], [])
-                        for t in block:
-                            plane = planes.index(XPT * t + i)
-                            hx = hx_ref[0, plane, g : g + 1, :]
-                            dx = hx_ref[1, plane, g : g + 1, :]
-                            rows[0].append(dx * part_x0 + hx * part_y1)
-                            rows[1].append(hx * part_z)
-                            rows[2].append(hx * part_w)
-                        for c in range(3):
-                            have = sum(v.shape[0] for v in rows[c])
-                            pad = [jnp.zeros((YS - have, 128), f32)] if have < YS else []
-                            full = pad + rows[c] if e == 0 else rows[c] + pad
-                            full = jnp.concatenate(full, axis=0) if len(full) > 1 else full[0]
-                            high, low = split(full)
-                            start = base + 128 * c + YS * i
-                            high_ref[start : start + YS, at] = high
-                            low_ref[start : start + YS, at] = low
-            for n, block in enumerate(blocks):
-                span = slice(384 * n, 384 * n + 384)
-                both = dot_nt(hz_ref[...], high_ref[span, :])
-                got = both[:ROWS] + both[ROWS:] + dot_nt(hz_ref[0:ROWS, :], low_ref[span, :])
-                for k, t in enumerate(block):
+                    rows = ([], [], [])
+                    for n in block:
+                        hx = hx_ref[b, 0, n, g : g + 1, :]
+                        dx = hx_ref[b, 1, n, g : g + 1, :]
+                        rows[0].append(dx * part_x0 + hx * part_y1)
+                        rows[1].append(hx * part_z)
+                        rows[2].append(hx * part_w)
                     for c in range(3):
-                        value = got[:, 128 * c : 128 * c + 128]
-                        if e > 0:
-                            value = pltpu.roll(value, window + (128 - 8 * k), 1)
-                            in_group = lax.broadcasted_iota(jnp.int32, (ROWS, 128), 1) % YS
-                            inside = jnp.logical_and(in_group >= window, in_group < window + 8)
-                            value = jnp.where(inside, value, 0.0)
-                        wide[c, :, 128 * t : 128 * t + 128] += value
+                        main_part, rest = split(stack_rows(rows[c], 16))
+                        lines = slice(row_at + c * count, row_at + c * count + count)
+                        left_ref[0, lines, at] = main_part
+                        left_ref[1, lines, at] = rest
+                lines = slice(row_at, row_at + 3 * count)
+                got = dot_nt(left_ref[0, lines, :], right_ref[b, 0])
+                got = got + dot_nt(left_ref[1, lines, :], right_ref[b, 0])
+                got = got + dot_nt(left_ref[0, lines, :], right_ref[b, 1])
+                for c in range(3):
+                    for i, n in enumerate(block):
+                        begin = c * count + i * high
+                        value = got[begin : begin + high]
+                        if e == 0:
+                            add(near, (c, planes[n]), value)
+                        else:
+                            add(beside, (e - 1, c, planes[n]), value)
+                row_at += 3 * count
 
     @pl.when(step == pl.num_programs(0) - 1)
     def _():
+        row8 = lax.broadcasted_iota(jnp.int32, (8, 2 * 128), 0)
+        zero = jnp.zeros((8, 2 * 128), f32)
         for t in range(XTILES):
+            turned = []
+            for c in range(3):
+                pieces = []
+                for plane in range(XPT * t, XPT * t + XPT):
+                    if plane > UPPER[-1]:
+                        pieces.append(jnp.zeros((YS, 2 * 128), f32))
+                        continue
+                    parts = [zero] + [near[c, plane, 8 * i : 8 * i + 8, :] for i in range(3)]
+                    if others:
+                        if others == 1:
+                            value = beside[0, c, plane]
+                            low_part = jnp.where(my == 0, 0.0, value)
+                            high_part = jnp.where(my == 0, value, 0.0)
+                        else:
+                            low_part, high_part = beside[0, c, plane], beside[1, c, plane]
+                        moved = pltpu.roll(low_part, 4, 0)
+                        parts[0] = jnp.where(row8 >= 4, moved, 0.0)
+                        parts[1] = parts[1] + jnp.where(row8 < 4, moved, 0.0)
+                        parts[3] = parts[3] + high_part
+                    pieces.extend(parts)
+                stacked = jnp.concatenate(pieces, axis=0)
+                turned.append(
+                    jnp.concatenate([stacked[:, :128].T, stacked[:, 128:].T[: ROWS - 128]], axis=0)
+                )
             at = slice(128 * t, 128 * t + 128)
-            along_z = wide[1, :, at]
             rhs_ref[:, at] = (
-                wide[0, :, at]
-                + pltpu.roll(along_z, ROWS - 1, 0)
-                - pltpu.roll(along_z, 1, 0)
+                turned[0]
+                + pltpu.roll(turned[1], ROWS - 1, 0)
+                - pltpu.roll(turned[1], 1, 0)
             )
-            density_ref[:, at] = wide[2, :, at]
+            density_ref[:, at] = turned[2]
         up_ref[0] = rhs_ref[UP_AT : UP_AT + HALO, :]
         up_ref[1] = density_ref[UP_AT : UP_AT + HALO, :]
         down_ref[0] = rhs_ref[DOWN_AT : DOWN_AT + HALO, :]
@@ -321,7 +355,7 @@
                 later[8 * i + 8 : 8 * i + 16, :] = ahead
         now, later = later, now
 
-    for t in CENTER:
+    for t in range(FIRST_TILE, END_TILE):
         turned = total[ZO : ZO + CZ, 128 * t : 128 * t + 128].T
         for i in range(XPT):
             plane = XPT * t + i - XO
@@ -329,8 +363,7 @@
                 indicator_ref[plane] = turned[YS * i + YO : YS * i + YO + CY, :]
 
     groups = own_ref.shape[1]
-    first_lane, end_lane = 128 * CENTER[0], 128 * CENTER[-1] + 128
-    depth = end_lane - first_lane
+    first_lane, end_lane = 128 * FIRST_TILE, 128 * END_TILE
     u_high, u_low = split(total[:, first_lane:end_lane])
     z_row = row_iota(ROWS) - float(ZO)
     y_row = row_iota(24) + float(8 - YO)
@@ -342,7 +375,7 @@
             off_x, off_y = main[4:5], main[5:6]
             hy = hat(y_row, more[0:1], 1.0 - off_y, off_y)
             at = slice(128 * g, 128 * g + 128)
-            for plane in range(XPT * CENTER[0], XPT * CENTER[-1] + XPT):
+            for plane in range(XPT * FIRST_TILE, XPT * END_TILE):
                 start = YS * plane - first_lane
                 if 0 <= plane - XO <= CX:
                     hx = hat(float(plane - XO), main[7:8], 1.0 - off_x, off_x)
@@ -382,7 +415,7 @@
     outgoing = pl.pallas_call(
         functools.partial(pack_kernel, shape),
         out_shape=jax.ShapeDtypeStruct((sources, rows, 128), f32),
-        in_specs=[whole, whole, pl.BlockSpec(memory_space=pltpu.SMEM)],
+        in_specs=[whole, whole, whole],
         out_specs=whole,
         scratch_shapes=[
             pltpu.VMEM((sources, 8, slots), f32),
@@ -390,12 +423,22 @@
         ],
         compiler_params=params,
         name="pack_points",
-    )(point_data, point_cells, send_counts)
+    )(
+        jnp.transpose(point_data, (0, 2, 1, 3)),
+        jnp.transpose(point_cells, (0, 2, 1, 3)),
+        send_counts.reshape(sources, 1),
+    )
 
     arrived = lax.all_to_all(outgoing, AXES, split_axis=0, concat_axis=0, tiled=True)
     arrived = arrived.reshape(4, groups, rows, 128)
 
-    most = 384 * len(CENTER)
+    others = other_count(gy)
+    lines = 0
+    for planes in (CENTER, LOWER, UPPER):
+        for high, size in ((24, 4),) + ((8, 12),) * others:
+            for start in range(0, len(planes), size):
+                count = min(size, len(planes) - start)
+                lines += 3 * 16 * -(-count * high // 16)
     wide_shape = jax.ShapeDtypeStruct((ROWS, LANES), f32)
     edge_shape = jax.ShapeDtypeStruct((2, HALO, LANES), f32)
     steps = groups // GROUPS
@@ -416,11 +459,11 @@
         ),
         scratch_shapes=[
             pltpu.VMEM((rows // 2, GROUPS, 8, 128), f32),
-            pltpu.VMEM((most, 128 * GROUPS), bf16),
-            pltpu.VMEM((most, 128 * GROUPS), bf16),
-            pltpu.VMEM((2 * ROWS, 128 * GROUPS), bf16),
-            pltpu.VMEM((2, XPT * len(CENTER), GROUPS, 128), f32),
-            pltpu.VMEM((3, ROWS, LANES), f32),
+            pltpu.VMEM((2, lines, 128 * GROUPS), bf16),
+            pltpu.VMEM((bricks, 2, ROWS, 128 * GROUPS), bf16),
+            pltpu.VMEM((bricks, 2, len(CENTER), GROUPS, 128), f32),
+            pltpu.VMEM((3, XPT * XTILES, 24, 2 * 128), f32),
+            pltpu.VMEM((max(others, 1), 3, XPT * XTILES, 8, 2 * 128), f32),
         ],
         compiler_params=params,
         name="splat_points",
@@ -429,7 +472,7 @@
     from_low = lax.ppermute(up, "gz", [(i, i + 1) for i in range(gz - 1)])
     from_high = lax.ppermute(down, "gz", [(i + 1, i) for i in range(gz - 1)])
 
-    depth = 128 * len(CENTER)
+    depth = 128 * (END_TILE - FIRST_TILE)
     indicator, values = pl.pallas_call(
         functools.partial(solve_kernel, shape),
         out_shape=(

time: 63.8 us -> 59.3 us (0.929)
  Pallas kernels: 22.6 us -> 19.2 us
  local copies, waits for them, and re-layouts: 3.46 us -> 2.57 us
    pallas_call x1, Pallas kernels: 14.3 us -> 10.9 us  [on_device(): pl.pallas_call(functools.partial(splat_kernel, shape), grid=(steps,), out...]
    unnamed x9 -> x7, local copies, waits for them, and re-layouts: 3.46 us -> 1.88 us
    reshape x0 -> x1, local copies, waits for them, and re-layouts: none -> 0.69 us  [on_device(): send_counts.reshape(sources, 1)]
where the time goes in v2:
time: 59.3 us; the launch traced here: 59 us
  blocking collectives  27.2 us (46%)
  Pallas kernels  19.2 us (32%)
  waiting for transfers between devices  4.8 us (8%)
  starting transfers between devices  4.47 us (8%)
  local copies, waits for them, and re-layouts  2.57 us (4%)
  between operations  0.66 us (1%)
    all_to_all x1, blocking collectives, on_device(): lax.all_to_all(outgoing, AXES, split_axis=0, concat_axis=0, tiled=True)  17.6 us
    pallas_call x1, Pallas kernels, on_device(): pl.pallas_call(functools.partial(splat_kernel, shape), grid=(steps,), out...  10.9 us
    all_to_all x1, blocking collectives, on_device(): lax.all_to_all(values, AXES, split_axis=0, concat_axis=0, tiled=True)  9.63 us
    pallas_call x1, Pallas kernels, on_device(): pl.pallas_call(functools.partial(solve_kernel, shape), out_shape=(jax.Sha...  6.3 us
    ppermute x1, waiting for transfers between devices, on_device(): from_high = lax.ppermute(down, 'gz', [(i + 1, i) for i in range(gz - 1)])  4.15 us
    ppermute x1, starting transfers between devices, on_device(): from_low = lax.ppermute(up, 'gz', [(i, i + 1) for i in range(gz - 1)])  2.99 us
    pallas_call x1, Pallas kernels, on_device(): pl.pallas_call(functools.partial(pack_kernel, shape), out_shape=jax.Shape...  2.05 us
    unnamed x7, local copies, waits for them, and re-layouts  1.88 us
  transfers between devices with their start and end apart: 2, of which 2 were waited for; matrix products, arithmetic and copies ran while one was open for 0% of the time, Pallas kernels for 0%

profile of v2, /device:TPU:0, one launch (start us, length us, event | category | flops | bytes accessed | tf_op | source)
XLA Modules:
  0.0 59.0 jit_solution(14306229062558130316)
XLA Ops:
  0.6 0.0 copy-start.2
  0.6 0.6 %copy-done.2 = s32[1,32]{1,0:T(1,128)S(1)} copy-done((s32[1,32]{1,0:T(1,128)S(1)}, s32[1,32]{1,0:T(1,128)}, u32[]{:S(2)}) %copy-start.2) | copy-done | bytes 152
  1.3 0.7 %copy.6.counts_ref = s32[32,1]{1,0:T(8,128)} copy(s32[32,1]{0,1:T(1,128)S(1)} %bitcast.13) | data formatting | bytes 256 | tf_op jit(solution)/shard_map/reshape | solution.py:429
  2.0 2.0 %pack_points.1 = f32[32,16,128]{2,1,0:T(8,128)} custom-call(f32[1,7,32,32]{3,2,1,0:T(8,128)} %bitcast.9, s32[1,3,32,32]{3,2,1,0:T(8,128)} %bitcast.11, s32[32,1]{1,0:T(8,128)} %copy.6.counts_ref), custom_call_target="tpu_custom_call" | custom-call | tf_op jit(solution)/shard_map/pack_points/pallas_call | solution.py:415
  4.0 17.6 %all_to_all.14 = f32[32,16,128]{2,1,0:T(8,128)} all-to-all(f32[32,16,128]{2,1,0:T(8,128)} %pack_points.1), channel_id=1, replica_groups=mesh['gx'=4,'gy'=2,'gz'=4] {'gx','gy','gz'}, dimensions={0} | all-to-all | bytes 524288 | tf_op jit(solution)/shard_map/all_to_all | solution.py:432
  21.6 10.9 %splat_points.1 = (f32[144,896]{1,0:T(8,128)}, f32[144,896]{1,0:T(8,128)}, f32[2,8,896]{2,1,0:T(8,128)}, f32[2,8,896]{2,1,0:T(8,128)}, f32[2,8,8,128]{3,2,1,0:T(8,128)}) custom-call(f32[4,8,16,128]{3,2,1,0:T(8,128)} %bitcast.8), custom_call_target="tpu_custom_call" | custom-call | tf_op jit(solution)/shard_map/splat_points/pallas_call | solution.py:445
  32.5 3.0 %collective-permute-start = (f32[2,8,896]{2,1,0:T(8,128)}, f32[2,8,896]{2,1,0:T(8,128)S(1)}, u32[]{:S(2)}, u32[]{:S(2)}) collective-permute-start(f32[2,8,896]{2,1,0:T(8,128)} %get-tuple-element.11), channel_id=1, source_target_pairs={{0,1},{1,2},{2,3},{4,5},{5,6},{6,7},{8,9},{9,10},{10,11},{12,13},{... | collective-permute-start | bytes 172040 | tf_op jit(solution)/shard_map/ppermute | solution.py:472
  35.5 1.5 %collective-permute-start.1 = (f32[2,8,896]{2,1,0:T(8,128)}, f32[2,8,896]{2,1,0:T(8,128)S(1)}, u32[]{:S(2)}, u32[]{:S(2)}) collective-permute-start(f32[2,8,896]{2,1,0:T(8,128)} %get-tuple-element.12), channel_id=1, source_target_pairs={{1,0},{2,1},{3,2},{5,4},{6,5},{7,6},{9,8},{10,9},{11,10},{13,12},{... | collective-permute-start | bytes 172040 | tf_op jit(solution)/shard_map/ppermute | solution.py:473
  37.0 0.6 %collective-permute-done.from_low_ref = f32[2,8,896]{2,1,0:T(8,128)S(1)} collective-permute-done((f32[2,8,896]{2,1,0:T(8,128)}, f32[2,8,896]{2,1,0:T(8,128)S(1)}, u32[]{:S(2)}, u32[]{:S(2)}) %collective-permute-start) | collective-permute-done | bytes 57376 | tf_op jit(solution)/shard_map/ppermute | solution.py:472
  37.6 0.0 copy-start
  37.6 4.2 %collective-permute-done.1.from_high_ref = f32[2,8,896]{2,1,0:T(8,128)S(1)} collective-permute-done((f32[2,8,896]{2,1,0:T(8,128)}, f32[2,8,896]{2,1,0:T(8,128)S(1)}, u32[]{:S(2)}, u32[]{:S(2)}) %collective-permute-start.1) | collective-permute-done | bytes 57376 | tf_op jit(solution)/shard_map/ppermute | solution.py:473
  41.8 0.0 copy-start.1
  41.8 0.0 copy-done
  41.8 0.6 %copy-done.1 = f32[2,8,896]{2,1,0:T(8,128)} copy-done((f32[2,8,896]{2,1,0:T(8,128)}, f32[2,8,896]{2,1,0:T(8,128)S(1)}, u32[]{:S(2)}) %copy-start.1) | copy-done | bytes 57368
  42.4 6.3 %solve_and_read.1 = (f32[16,16,128]{2,1,0:T(8,128)}, f32[32,32]{1,0:T(8,128)}) custom-call(f32[144,896]{1,0:T(8,128)} %get-tuple-element.9.rhs_ref, f32[144,896]{1,0:T(8,128)} %get-tuple-element.10.density_ref, f32[2,8,896]{2,1,0:T(8,128)} %copy-done, f32[2,8,896]{2,1,0:T(8,128)} %copy-done.1, f32[2,8,8,128]{3,2,1,0:T(8,128)} %get-tuple-element.13.own_ref), custom_call_target="tpu_custom_call" | custom-call | tf_op jit(solution)/shard_map/solve_and_read/pallas_call | solution.py:476
  48.7 9.6 %all_to_all.15 = f32[32,1,32]{2,1,0:T(1,128)S(1)} all-to-all(f32[32,1,32]{2,1,0:T(1,128)} %bitcast.12), channel_id=1, replica_groups=mesh['gx'=4,'gy'=2,'gz'=4] {'gx','gy','gz'}, dimensions={0} | all-to-all | bytes 8192 | tf_op jit(solution)/shard_map/all_to_all | solution.py:498
  58.4 0.6 %copy.9 = f32[1,32,32]{2,1,0:T(8,128)} copy(f32[1,32,32]{2,1,0:T(8,128)S(1)} %bitcast.10) | data formatting | bytes 8192
Async XLA Ops:
  0.6 0.7 %copy-start.2 = (s32[1,32]{1,0:T(1,128)S(1)}, s32[1,32]{1,0:T(1,128)}, u32[]{:S(2)}) copy-start(s32[1,32]{1,0:T(1,128)} %param.5) | copy-start | bytes 388
  32.5 5.1 %collective-permute-start = (f32[2,8,896]{2,1,0:T(8,128)}, f32[2,8,896]{2,1,0:T(8,128)S(1)}, u32[]{:S(2)}, u32[]{:S(2)}) collective-permute-start(f32[2,8,896]{2,1,0:T(8,128)} %get-tuple-element.11), channel_id=1, source_target_pairs={{0,1},{1,2},{2,3},{4,5},{5,6},{6,7},{8,9},{9,10},{10,11},{12,13},{... | collective-permute-start | bytes 172040 | tf_op jit(solution)/shard_map/ppermute | solution.py:472
  35.5 6.3 %collective-permute-start.1 = (f32[2,8,896]{2,1,0:T(8,128)}, f32[2,8,896]{2,1,0:T(8,128)S(1)}, u32[]{:S(2)}, u32[]{:S(2)}) collective-permute-start(f32[2,8,896]{2,1,0:T(8,128)} %get-tuple-element.12), channel_id=1, source_target_pairs={{1,0},{2,1},{3,2},{5,4},{6,5},{7,6},{9,8},{10,9},{11,10},{13,12},{... | collective-permute-start | bytes 172040 | tf_op jit(solution)/shard_map/ppermute | solution.py:473
  37.6 4.2 %copy-start = (f32[2,8,896]{2,1,0:T(8,128)}, f32[2,8,896]{2,1,0:T(8,128)S(1)}, u32[]{:S(2)}) copy-start(f32[2,8,896]{2,1,0:T(8,128)S(1)} %collective-permute-done.from_low_ref) | copy-start | bytes 172036
  41.8 0.6 %copy-start.1 = (f32[2,8,896]{2,1,0:T(8,128)}, f32[2,8,896]{2,1,0:T(8,128)S(1)}, u32[]{:S(2)}) copy-start(f32[2,8,896]{2,1,0:T(8,128)S(1)} %collective-permute-done.1.from_high_ref) | copy-start | bytes 172036

commit v3 on v2

--- a/solution.py
+++ b/solution.py
@@ -65,10 +65,15 @@
 def pack_kernel(shape, data_ref, cells_ref, counts_ref, out_ref, main, extra):
     gx, gy, gz = shape
     slots = data_ref.shape[3]
-    lane = lax.broadcasted_iota(jnp.int32, (gx * gy * gz, slots), 1)
+    sources = gx * gy * gz
+    lane = lax.broadcasted_iota(jnp.int32, (sources, slots), 1)
+    at_row = lax.broadcasted_iota(jnp.int32, (sources, sources), 0)
+    at_lane = lax.broadcasted_iota(jnp.int32, (sources, sources), 1)
+    counts = jnp.where(at_row == at_lane, counts_ref[...], 0).astype(f32)
+    counts = jnp.sum(counts, axis=1, keepdims=True).astype(jnp.int32)
     others = other_count(gy)
     bricks = 3 * (1 + others)
-    weight = jnp.where(lane < counts_ref[...], data_ref[0, 3], 0.0)
+    weight = jnp.where(lane < counts, data_ref[0, 3], 0.0)
     for c in range(3):
         main[:, c, :] = data_ref[0, c] * (-0.5 * weight)
     main[:, 3, :] = weight
@@ -170,7 +175,7 @@
     own_row = row_iota(24) + float(8 - YO)
 
     row_at = 0
-    for e in range(1 + others):
+    for e in reversed(range(1 + others)):
         if e == 0:
             y_limit = jnp.where(my == gy - 1, CY, CY + 1).astype(f32)
             y_row = own_row
@@ -182,7 +187,7 @@
             first = jnp.where(above, WINDOW_HIGH - YO - CY, WINDOW_LOW - YO + CY)
             y_row = row_iota(8) + first.astype(f32)
         high = y_row.shape[0]
-        for o, (shift, planes) in enumerate(((0, CENTER), (-1, LOWER), (1, UPPER))):
+        for o, shift, planes in ((1, -1, LOWER), (0, 0, CENTER), (2, 1, UPPER)):
             b = e * 3 + o
             place, row = extra_place(b, bricks)
             x_limit = jnp.where(mx + shift == gx - 1, CX, CX + 1).astype(f32)
@@ -203,44 +208,44 @@
                 high_z = jnp.where(cell_z + 1.0 < z_limit, off_z, 0.0)
                 hz_high, hz_low = split(hat(z_row, cell_z, 1.0 - off_z, high_z))
                 at = slice(128 * g, 128 * g + 128)
-                right_ref[b, 0, :, at] = hz_high
-                right_ref[b, 1, :, at] = hz_low
+                right_ref[b, 0, at, 0:ROWS] = hz_high.T
+                right_ref[b, 1, at, 0:ROWS] = hz_low.T
                 high_y = jnp.where(cell_y + 1.0 < y_limit, off_y, 0.0)
                 hy = hat(y_row, cell_y, 1.0 - off_y, high_y)
                 dy = hat_slope(y_row, cell_y, 1.0 - off_y, high_y)
                 y_parts.append((main[0:1] * hy, main[1:2] * dy, main[2:3] * hy, main[3:4] * hy))
-            size = 4 if e == 0 else 12
-            for start in range(0, len(planes), size):
-                block = range(start, min(start + size, len(planes)))
-                count = -(-len(block) * high // 16) * 16
+            count = -(-len(planes) * high // 16) * 16
+            for c in range(3):
                 for g in range(GROUPS):
                     part_x0, part_y1, part_z, part_w = y_parts[g]
                     at = slice(128 * g, 128 * g + 128)
-                    rows = ([], [], [])
-                    for n in block:
-                        hx = hx_ref[b, 0, n, g : g + 1, :]
-                        dx = hx_ref[b, 1, n, g : g + 1, :]
-                        rows[0].append(dx * part_x0 + hx * part_y1)
-                        rows[1].append(hx * part_z)
-                        rows[2].append(hx * part_w)
-                    for c in range(3):
-                        main_part, rest = split(stack_rows(rows[c], 16))
-                        lines = slice(row_at + c * count, row_at + c * count + count)
+                    for start in range(0, len(planes), 2):
+                        rows = []
+                        for n in range(start, min(start + 2, len(planes))):
+                            hx = hx_ref[b, 0, n, g : g + 1, :]
+                            if c == 0:
+                                dx = hx_ref[b, 1, n, g : g + 1, :]
+                                rows.append(dx * part_x0 + hx * part_y1)
+                            else:
+                                rows.append(hx * (part_z if c == 1 else part_w))
+                        main_part, rest = split(stack_rows(rows, 16))
+                        begin = row_at + c * count + start * high
+                        lines = slice(begin, begin + main_part.shape[0])
                         left_ref[0, lines, at] = main_part
                         left_ref[1, lines, at] = rest
-                lines = slice(row_at, row_at + 3 * count)
-                got = dot_nt(left_ref[0, lines, :], right_ref[b, 0])
-                got = got + dot_nt(left_ref[1, lines, :], right_ref[b, 0])
-                got = got + dot_nt(left_ref[0, lines, :], right_ref[b, 1])
-                for c in range(3):
-                    for i, n in enumerate(block):
-                        begin = c * count + i * high
-                        value = got[begin : begin + high]
-                        if e == 0:
-                            add(near, (c, planes[n]), value)
-                        else:
-                            add(beside, (e - 1, c, planes[n]), value)
-                row_at += 3 * count
+            lines = slice(row_at, row_at + 3 * count)
+            got = dot_nn(left_ref[0, lines, :], right_ref[b, 0, :, 0:ROWS])
+            got = got + dot_nn(left_ref[1, lines, :], right_ref[b, 0, :, 0:ROWS])
+            got = got + dot_nn(left_ref[0, lines, :], right_ref[b, 1, :, 0:ROWS])
+            for c in range(3):
+                for n, plane in enumerate(planes):
+                    begin = c * count + n * high
+                    value = got[begin : begin + high]
+                    if e == 0:
+                        add(near, (c, plane), value)
+                    else:
+                        add(beside, (e - 1, c, plane), value)
+            row_at += 3 * count
 
     @pl.when(step == pl.num_programs(0) - 1)
     def _():
@@ -426,7 +431,7 @@
     )(
         jnp.transpose(point_data, (0, 2, 1, 3)),
         jnp.transpose(point_cells, (0, 2, 1, 3)),
-        send_counts.reshape(sources, 1),
+        send_counts,
     )
 
     arrived = lax.all_to_all(outgoing, AXES, split_axis=0, concat_axis=0, tiled=True)
@@ -435,10 +440,8 @@
     others = other_count(gy)
     lines = 0
     for planes in (CENTER, LOWER, UPPER):
-        for high, size in ((24, 4),) + ((8, 12),) * others:
-            for start in range(0, len(planes), size):
-                count = min(size, len(planes) - start)
-                lines += 3 * 16 * -(-count * high // 16)
+        for high in (24,) + (8,) * others:
+            lines += 3 * 16 * -(-len(planes) * high // 16)
     wide_shape = jax.ShapeDtypeStruct((ROWS, LANES), f32)
     edge_shape = jax.ShapeDtypeStruct((2, HALO, LANES), f32)
     steps = groups // GROUPS
@@ -460,7 +463,7 @@
         scratch_shapes=[
             pltpu.VMEM((rows // 2, GROUPS, 8, 128), f32),
             pltpu.VMEM((2, lines, 128 * GROUPS), bf16),
-            pltpu.VMEM((bricks, 2, ROWS, 128 * GROUPS), bf16),
+            pltpu.VMEM((bricks, 2, 128 * GROUPS, 2 * 128), bf16),
             pltpu.VMEM((bricks, 2, len(CENTER), GROUPS, 128), f32),
             pltpu.VMEM((3, XPT * XTILES, 24, 2 * 128), f32),
             pltpu.VMEM((max(others, 1), 3, XPT * XTILES, 8, 2 * 128), f32),

time: 59.3 us -> 59.1 us (level)
  local copies, waits for them, and re-layouts: 2.57 us -> 1.22 us
  Pallas kernels: 19.2 us -> 20.4 us
    pallas_call x1, Pallas kernels: 10.9 us -> 12 us  [on_device(): pl.pallas_call(functools.partial(splat_kernel, shape), grid=(steps,), out...]
    reshape x1 -> x0, local copies, waits for them, and re-layouts: 0.69 us -> none  [on_device(): send_counts.reshape(sources, 1)]
    unnamed x7 -> x5, local copies, waits for them, and re-layouts: 1.88 us -> 1.22 us
where the time goes in v3:
time: 59.1 us; the launch traced here: 58.8 us
  blocking collectives  27.2 us (46%)
  Pallas kernels  20.4 us (35%)
  waiting for transfers between devices  4.8 us (8%)
  starting transfers between devices  4.47 us (8%)
  local copies, waits for them, and re-layouts  1.22 us (2%)
  between operations  0.65 us (1%)
    all_to_all x1, blocking collectives, on_device(): lax.all_to_all(outgoing, AXES, split_axis=0, concat_axis=0, tiled=True)  17.6 us
    pallas_call x1, Pallas kernels, on_device(): pl.pallas_call(functools.partial(splat_kernel, shape), grid=(steps,), out...  12 us
    all_to_all x1, blocking collectives, on_device(): lax.all_to_all(values, AXES, split_axis=0, concat_axis=0, tiled=True)  9.63 us
    pallas_call x1, Pallas kernels, on_device(): pl.pallas_call(functools.partial(solve_kernel, shape), out_shape=(jax.Sha...  6.3 us
    ppermute x1, waiting for transfers between devices, on_device(): from_high = lax.ppermute(down, 'gz', [(i + 1, i) for i in range(gz - 1)])  4.15 us
    ppermute x1, starting transfers between devices, on_device(): from_low = lax.ppermute(up, 'gz', [(i, i + 1) for i in range(gz - 1)])  2.99 us
    pallas_call x1, Pallas kernels, on_device(): pl.pallas_call(functools.partial(pack_kernel, shape), out_shape=jax.Shape...  2.06 us
    ppermute x1, starting transfers between devices, on_device(): from_high = lax.ppermute(down, 'gz', [(i + 1, i) for i in range(gz - 1)])  1.47 us
  transfers between devices with their start and end apart: 2, of which 2 were waited for; matrix products, arithmetic and copies ran while one was open for 0% of the time, Pallas kernels for 0%

profile of v3, /device:TPU:0, one launch (start us, length us, event | category | flops | bytes accessed | tf_op | source)
XLA Modules:
  0.0 58.8 jit_solution(15614279438534783642)
XLA Ops:
  0.6 2.1 %pack_points.1 = f32[32,16,128]{2,1,0:T(8,128)} custom-call(f32[1,7,32,32]{3,2,1,0:T(8,128)} %bitcast.8, s32[1,3,32,32]{3,2,1,0:T(8,128)} %bitcast.10, s32[1,32]{1,0:T(1,128)} %counts_ref.1), custom_call_target="tpu_custom_call" | custom-call | tf_op jit(solution)/shard_map/pack_points/pallas_call | solution.py:420
  2.7 17.6 %all_to_all.14 = f32[32,16,128]{2,1,0:T(8,128)} all-to-all(f32[32,16,128]{2,1,0:T(8,128)} %pack_points.1), channel_id=1, replica_groups=mesh['gx'=4,'gy'=2,'gz'=4] {'gx','gy','gz'}, dimensions={0} | all-to-all | bytes 524288 | tf_op jit(solution)/shard_map/all_to_all | solution.py:437
  20.3 12.0 %splat_points.1 = (f32[144,896]{1,0:T(8,128)}, f32[144,896]{1,0:T(8,128)}, f32[2,8,896]{2,1,0:T(8,128)}, f32[2,8,896]{2,1,0:T(8,128)}, f32[2,8,8,128]{3,2,1,0:T(8,128)}) custom-call(f32[4,8,16,128]{3,2,1,0:T(8,128)} %bitcast.7), custom_call_target="tpu_custom_call" | custom-call | tf_op jit(solution)/shard_map/splat_points/pallas_call | solution.py:448
  32.3 3.0 %collective-permute-start = (f32[2,8,896]{2,1,0:T(8,128)}, f32[2,8,896]{2,1,0:T(8,128)S(1)}, u32[]{:S(2)}, u32[]{:S(2)}) collective-permute-start(f32[2,8,896]{2,1,0:T(8,128)} %get-tuple-element.11), channel_id=1, source_target_pairs={{0,1},{1,2},{2,3},{4,5},{5,6},{6,7},{8,9},{9,10},{10,11},{12,13},{... | collective-permute-start | bytes 172040 | tf_op jit(solution)/shard_map/ppermute | solution.py:475
  35.3 1.5 %collective-permute-start.1 = (f32[2,8,896]{2,1,0:T(8,128)}, f32[2,8,896]{2,1,0:T(8,128)S(1)}, u32[]{:S(2)}, u32[]{:S(2)}) collective-permute-start(f32[2,8,896]{2,1,0:T(8,128)} %get-tuple-element.12), channel_id=1, source_target_pairs={{1,0},{2,1},{3,2},{5,4},{6,5},{7,6},{9,8},{10,9},{11,10},{13,12},{... | collective-permute-start | bytes 172040 | tf_op jit(solution)/shard_map/ppermute | solution.py:476
  36.8 0.6 %collective-permute-done.from_low_ref = f32[2,8,896]{2,1,0:T(8,128)S(1)} collective-permute-done((f32[2,8,896]{2,1,0:T(8,128)}, f32[2,8,896]{2,1,0:T(8,128)S(1)}, u32[]{:S(2)}, u32[]{:S(2)}) %collective-permute-start) | collective-permute-done | bytes 57376 | tf_op jit(solution)/shard_map/ppermute | solution.py:475
  37.4 0.0 copy-start
  37.4 4.2 %collective-permute-done.1.from_high_ref = f32[2,8,896]{2,1,0:T(8,128)S(1)} collective-permute-done((f32[2,8,896]{2,1,0:T(8,128)}, f32[2,8,896]{2,1,0:T(8,128)S(1)}, u32[]{:S(2)}, u32[]{:S(2)}) %collective-permute-start.1) | collective-permute-done | bytes 57376 | tf_op jit(solution)/shard_map/ppermute | solution.py:476
  41.6 0.0 copy-start.1
  41.6 0.0 copy-done
  41.6 0.6 %copy-done.1 = f32[2,8,896]{2,1,0:T(8,128)} copy-done((f32[2,8,896]{2,1,0:T(8,128)}, f32[2,8,896]{2,1,0:T(8,128)S(1)}, u32[]{:S(2)}) %copy-start.1) | copy-done | bytes 57368
  42.2 6.3 %solve_and_read.1 = (f32[16,16,128]{2,1,0:T(8,128)}, f32[32,32]{1,0:T(8,128)}) custom-call(f32[144,896]{1,0:T(8,128)} %get-tuple-element.9.rhs_ref, f32[144,896]{1,0:T(8,128)} %get-tuple-element.10.density_ref, f32[2,8,896]{2,1,0:T(8,128)} %copy-done, f32[2,8,896]{2,1,0:T(8,128)} %copy-done.1, f32[2,8,8,128]{3,2,1,0:T(8,128)} %get-tuple-element.13.own_ref), custom_call_target="tpu_custom_call" | custom-call | tf_op jit(solution)/shard_map/solve_and_read/pallas_call | solution.py:479
  48.5 9.6 %all_to_all.15 = f32[32,1,32]{2,1,0:T(1,128)S(1)} all-to-all(f32[32,1,32]{2,1,0:T(1,128)} %bitcast.11), channel_id=1, replica_groups=mesh['gx'=4,'gy'=2,'gz'=4] {'gx','gy','gz'}, dimensions={0} | all-to-all | bytes 8192 | tf_op jit(solution)/shard_map/all_to_all | solution.py:501
  58.1 0.6 %copy.7 = f32[1,32,32]{2,1,0:T(8,128)} copy(f32[1,32,32]{2,1,0:T(8,128)S(1)} %bitcast.9) | data formatting | bytes 8192
Async XLA Ops:
  32.3 5.1 %collective-permute-start = (f32[2,8,896]{2,1,0:T(8,128)}, f32[2,8,896]{2,1,0:T(8,128)S(1)}, u32[]{:S(2)}, u32[]{:S(2)}) collective-permute-start(f32[2,8,896]{2,1,0:T(8,128)} %get-tuple-element.11), channel_id=1, source_target_pairs={{0,1},{1,2},{2,3},{4,5},{5,6},{6,7},{8,9},{9,10},{10,11},{12,13},{... | collective-permute-start | bytes 172040 | tf_op jit(solution)/shard_map/ppermute | solution.py:475
  35.3 6.3 %collective-permute-start.1 = (f32[2,8,896]{2,1,0:T(8,128)}, f32[2,8,896]{2,1,0:T(8,128)S(1)}, u32[]{:S(2)}, u32[]{:S(2)}) collective-permute-start(f32[2,8,896]{2,1,0:T(8,128)} %get-tuple-element.12), channel_id=1, source_target_pairs={{1,0},{2,1},{3,2},{5,4},{6,5},{7,6},{9,8},{10,9},{11,10},{13,12},{... | collective-permute-start | bytes 172040 | tf_op jit(solution)/shard_map/ppermute | solution.py:476
  37.4 4.2 %copy-start = (f32[2,8,896]{2,1,0:T(8,128)}, f32[2,8,896]{2,1,0:T(8,128)S(1)}, u32[]{:S(2)}) copy-start(f32[2,8,896]{2,1,0:T(8,128)S(1)} %collective-permute-done.from_low_ref) | copy-start | bytes 172036
  41.6 0.6 %copy-start.1 = (f32[2,8,896]{2,1,0:T(8,128)}, f32[2,8,896]{2,1,0:T(8,128)S(1)}, u32[]{:S(2)}) copy-start(f32[2,8,896]{2,1,0:T(8,128)S(1)} %collective-permute-done.1.from_high_ref) | copy-start | bytes 172036

commit v4 on v3

--- a/solution.py
+++ b/solution.py
@@ -23,7 +23,6 @@
 YS = 32
 XPT = 128 // YS
 XTILES = -(-(CX + 2 * REACH + 1) // XPT)
-LANES = XTILES * 128
 ROWS = CZ + 16
 CENTER = tuple(range(XO - 1, XO + CX + 2))
 LOWER = tuple(range(0, XO + 2))
@@ -35,7 +34,7 @@
 DOWN_AT = ZO - 1
 HALO = 8
 GROUPS = 8
-VMEM_LIMIT = 56 * 1024 * 1024
+MIB = 1024 * 1024
 
 f32 = jnp.float32
 bf16 = jnp.bfloat16
@@ -129,7 +128,7 @@
 
 
 def splat_kernel(
-    shape, recv_ref, rhs_ref, density_ref, up_ref, down_ref, own_ref,
+    shape, recv_ref, fields_ref, up_ref, down_ref, own_ref,
     points, left_ref, right_ref, hx_ref, near, beside,
 ):
     gx, gy, gz = shape
@@ -174,7 +173,21 @@
     z_row = row_iota(ROWS) - float(ZO)
     own_row = row_iota(24) + float(8 - YO)
 
+    def multiply(begin, count, b, e, high, planes):
+        lines = slice(begin, begin + 3 * count)
+        got = dot_nn(left_ref[0, lines, :], right_ref[b, 0, :, 0:ROWS])
+        got = got + dot_nn(left_ref[1, lines, :], right_ref[b, 0, :, 0:ROWS])
+        got = got + dot_nn(left_ref[0, lines, :], right_ref[b, 1, :, 0:ROWS])
+        for c in range(3):
+            for i, plane in enumerate(planes):
+                value = got[c * count + i * high : c * count + i * high + high]
+                if e == 0:
+                    add(near, (c, plane), value)
+                else:
+                    add(beside, (e - 1, c, plane), value)
+
     row_at = 0
+    waiting = None
     for e in reversed(range(1 + others)):
         if e == 0:
             y_limit = jnp.where(my == gy - 1, CY, CY + 1).astype(f32)
@@ -214,14 +227,16 @@
                 hy = hat(y_row, cell_y, 1.0 - off_y, high_y)
                 dy = hat_slope(y_row, cell_y, 1.0 - off_y, high_y)
                 y_parts.append((main[0:1] * hy, main[1:2] * dy, main[2:3] * hy, main[3:4] * hy))
-            count = -(-len(planes) * high // 16) * 16
-            for c in range(3):
-                for g in range(GROUPS):
-                    part_x0, part_y1, part_z, part_w = y_parts[g]
-                    at = slice(128 * g, 128 * g + 128)
-                    for start in range(0, len(planes), 2):
+            size = 4 if e == 0 else 12
+            for start in range(0, len(planes), size):
+                block = range(start, min(start + size, len(planes)))
+                count = -(-len(block) * high // 16) * 16
+                for c in range(3):
+                    for g in range(GROUPS):
+                        part_x0, part_y1, part_z, part_w = y_parts[g]
+                        at = slice(128 * g, 128 * g + 128)
                         rows = []
-                        for n in range(start, min(start + 2, len(planes))):
+                        for n in block:
                             hx = hx_ref[b, 0, n, g : g + 1, :]
                             if c == 0:
                                 dx = hx_ref[b, 1, n, g : g + 1, :]
@@ -229,23 +244,16 @@
                             else:
                                 rows.append(hx * (part_z if c == 1 else part_w))
                         main_part, rest = split(stack_rows(rows, 16))
-                        begin = row_at + c * count + start * high
-                        lines = slice(begin, begin + main_part.shape[0])
-                        left_ref[0, lines, at] = main_part
-                        left_ref[1, lines, at] = rest
-            lines = slice(row_at, row_at + 3 * count)
-            got = dot_nn(left_ref[0, lines, :], right_ref[b, 0, :, 0:ROWS])
-            got = got + dot_nn(left_ref[1, lines, :], right_ref[b, 0, :, 0:ROWS])
-            got = got + dot_nn(left_ref[0, lines, :], right_ref[b, 1, :, 0:ROWS])
-            for c in range(3):
-                for n, plane in enumerate(planes):
-                    begin = c * count + n * high
-                    value = got[begin : begin + high]
-                    if e == 0:
-                        add(near, (c, plane), value)
-                    else:
-                        add(beside, (e - 1, c, plane), value)
-            row_at += 3 * count
+                        begin = row_at + c * count
+                        left_ref[0, begin : begin + count, at] = main_part
+                        left_ref[1, begin : begin + count, at] = rest
+                if waiting is not None:
+                    waiting()
+                waiting = functools.partial(
+                    multiply, row_at, count, b, e, high, [planes[n] for n in block]
+                )
+                row_at += 3 * count
+    waiting()
 
     @pl.when(step == pl.num_programs(0) - 1)
     def _():
@@ -276,17 +284,15 @@
                 turned.append(
                     jnp.concatenate([stacked[:, :128].T, stacked[:, 128:].T[: ROWS - 128]], axis=0)
                 )
-            at = slice(128 * t, 128 * t + 128)
-            rhs_ref[:, at] = (
+            fields_ref[0, t] = (
                 turned[0]
                 + pltpu.roll(turned[1], ROWS - 1, 0)
                 - pltpu.roll(turned[1], 1, 0)
             )
-            density_ref[:, at] = turned[2]
-        up_ref[0] = rhs_ref[UP_AT : UP_AT + HALO, :]
-        up_ref[1] = density_ref[UP_AT : UP_AT + HALO, :]
-        down_ref[0] = rhs_ref[DOWN_AT : DOWN_AT + HALO, :]
-        down_ref[1] = density_ref[DOWN_AT : DOWN_AT + HALO, :]
+            fields_ref[1, t] = turned[2]
+        for c in range(2):
+            up_ref[c] = fields_ref[c, :, UP_AT : UP_AT + HALO, :]
+            down_ref[c] = fields_ref[c, :, DOWN_AT : DOWN_AT + HALO, :]
 
 
 def chebyshev_factors():
@@ -302,102 +308,125 @@
 
 
 def solve_kernel(
-    shape, rhs_ref, density_ref, from_low_ref, from_high_ref, own_ref,
+    shape, fields_ref, from_low_ref, from_high_ref, own_ref,
     indicator_ref, values_ref,
-    first, second, scaled, inverse, total, edge, high_ref, low_ref,
+    given, low_halo, high_halo, owned, first, second, scaled, inverse, total,
+    hx_ref, high_ref, low_ref, arrivals,
 ):
     gx, gy, gz = shape
     mx, my, mz = lax.axis_index("gx"), lax.axis_index("gy"), lax.axis_index("gz")
-    edge[...] = jnp.zeros_like(edge)
-    low_at, high_at = UP_AT - CZ, DOWN_AT + CZ - (ROWS - 16)
-    edge[0, :, low_at : low_at + HALO, :] = from_low_ref[...]
-    edge[1, :, high_at : high_at + HALO, :] = from_high_ref[...]
-
-    def with_edge(ref, channel, i):
-        value = ref[8 * i : 8 * i + 8, :]
-        if i < 2:
-            return value + edge[0, channel, 8 * i : 8 * i + 8, :]
-        if i >= ROWS // 8 - 2:
-            at = 8 * (i - ROWS // 8 + 2)
-            return value + edge[1, channel, at : at + 8, :]
-        return value
-
-    lane = lax.broadcasted_iota(jnp.int32, (8, LANES), 1)
-    x, y = lane // YS - XO + mx * CX, lane % YS - YO + my * CY
-    inside_xy = (x >= 0) & (x < gx * CX) & (y >= 0) & (y < gy * CY)
-    zero = jnp.zeros((8, LANES), f32)
-    first[0:8, :] = zero
-    first[ROWS + 8 : ROWS + 16, :] = zero
-    second[0:8, :] = zero
-    second[ROWS + 8 : ROWS + 16, :] = zero
-    for i in range(ROWS // 8):
-        at = slice(8 * i, 8 * i + 8)
-        z = lax.broadcasted_iota(jnp.int32, (8, LANES), 0) + (8 * i - ZO) + mz * CZ
-        inside = inside_xy & (z >= 0) & (z < gz * CZ)
-        diagonal = 6.0 + base_screen + point_screen * with_edge(density_ref, 1, i)
-        inv = jnp.where(inside, 1.0 / diagonal, 0.0)
-        start = with_edge(rhs_ref, 0, i) * inv
-        inverse[at, :] = inv
-        scaled[at, :] = start
-        total[at, :] = start
-        first[8 * i + 8 : 8 * i + 16, :] = start
-
-    now, later = first, second
-    factors = chebyshev_factors()
-    for k, (keep, gain) in enumerate(factors):
-        last = k + 1 == len(factors)
-        for i in range(ROWS // 8):
-            at = slice(8 * i, 8 * i + 8)
-            here = now[8 * i + 8 : 8 * i + 16, :]
-            near = now[8 * i + 7 : 8 * i + 15, :] + now[8 * i + 9 : 8 * i + 17, :]
-            near = near + pltpu.roll(here, 1, 1) + pltpu.roll(here, LANES - 1, 1)
-            near = near + pltpu.roll(here, YS, 1) + pltpu.roll(here, LANES - YS, 1)
-            left = scaled[at, :] - here + inverse[at, :] * near
-            ahead = keep * here + gain * left
-            total[at, :] += ahead
-            if not last:
-                scaled[at, :] = left
-                later[8 * i + 8 : 8 * i + 16, :] = ahead
-        now, later = later, now
-
-    for t in range(FIRST_TILE, END_TILE):
-        turned = total[ZO : ZO + CZ, 128 * t : 128 * t + 128].T
-        for i in range(XPT):
-            plane = XPT * t + i - XO
-            if 0 <= plane < CX:
-                indicator_ref[plane] = turned[YS * i + YO : YS * i + YO + CY, :]
-
-    groups = own_ref.shape[1]
-    first_lane, end_lane = 128 * FIRST_TILE, 128 * END_TILE
-    u_high, u_low = split(total[:, first_lane:end_lane])
-    z_row = row_iota(ROWS) - float(ZO)
+    copies = [
+        pltpu.make_async_copy(source, target, arrivals.at[i])
+        for i, (source, target) in enumerate(
+            ((own_ref, owned), (fields_ref, given), (from_low_ref, low_halo), (from_high_ref, high_halo))
+        )
+    ]
+    for copy in copies:
+        copy.start()
+    copies[0].wait()
+    groups = owned.shape[1]
     y_row = row_iota(24) + float(8 - YO)
     blank = jnp.zeros((8, 128), f32)
-    for chunk in range(groups // GROUPS):
+    read_planes = range(XPT * FIRST_TILE, XPT * END_TILE)
+
+    def read_operand(chunk):
+        span = slice(chunk * GROUPS, chunk * GROUPS + GROUPS)
+        cell_x, off_x = owned[0, span, 7, :], owned[0, span, 4, :]
+        for plane in read_planes:
+            if 0 <= plane - XO <= CX:
+                hx_ref[plane] = hat(float(plane - XO), cell_x, 1.0 - off_x, off_x)
         for g in range(GROUPS):
-            main = own_ref[0, chunk * GROUPS + g]
-            more = own_ref[1, chunk * GROUPS + g]
-            off_x, off_y = main[4:5], main[5:6]
-            hy = hat(y_row, more[0:1], 1.0 - off_y, off_y)
+            off_y = owned[0, chunk * GROUPS + g, 5:6, :]
+            hy = hat(y_row, owned[1, chunk * GROUPS + g, 0:1, :], 1.0 - off_y, off_y)
             at = slice(128 * g, 128 * g + 128)
-            for plane in range(XPT * FIRST_TILE, XPT * END_TILE):
-                start = YS * plane - first_lane
+            for plane in read_planes:
+                start = YS * (plane - XPT * FIRST_TILE)
                 if 0 <= plane - XO <= CX:
-                    hx = hat(float(plane - XO), main[7:8], 1.0 - off_x, off_x)
-                    high, low = split(jnp.concatenate([blank, hx * hy], axis=0))
+                    rows = jnp.concatenate([blank, hx_ref[plane, g : g + 1, :] * hy], axis=0)
+                    high, low = split(rows)
                 else:
                     high = jnp.zeros((YS, 128), bf16)
                     low = high
                 high_ref[start : start + YS, at] = high
                 low_ref[start : start + YS, at] = low
+
+    read_operand(0)
+    for copy in copies[1:]:
+        copy.wait()
+    low_at, high_at = UP_AT - CZ, DOWN_AT + CZ
+    for c in range(2):
+        given[c, :, low_at : low_at + HALO, :] += low_halo[c]
+        given[c, :, high_at : high_at + HALO, :] += high_halo[c]
+
+    lane = lax.broadcasted_iota(jnp.int32, (8, 128), 1)
+    row = lax.broadcasted_iota(jnp.int32, (8, 128), 0)
+    y = lane % YS - YO + my * CY
+    inside_y = (y >= 0) & (y < gy * CY)
+    zero = jnp.zeros((8, 128), f32)
+    for t in range(XTILES):
+        x = lane // YS + (XPT * t - XO) + mx * CX
+        inside_xy = inside_y & (x >= 0) & (x < gx * CX)
+        for scratch in (first, second):
+            scratch[t, 0:8, :] = zero
+            scratch[t, ROWS + 8 : ROWS + 16, :] = zero
+        for i in range(ROWS // 8):
+            at = slice(8 * i, 8 * i + 8)
+            z = row + (8 * i - ZO) + mz * CZ
+            inside = inside_xy & (z >= 0) & (z < gz * CZ)
+            diagonal = 6.0 + base_screen + point_screen * given[1, t, at, :]
+            inv = jnp.where(inside, 1.0 / diagonal, 0.0)
+            start = given[0, t, at, :] * inv
+            inverse[t, at, :] = inv
+            scaled[t, at, :] = start
+            first[t, 8 * i + 8 : 8 * i + 16, :] = start
+            if FIRST_TILE <= t < END_TILE:
+                total[t - FIRST_TILE, at, :] = start
+
+    now, later = first, second
+    factors = chebyshev_factors()
+    low_part, high_part = lane < YS, lane >= 128 - YS
+    for k, (keep, gain) in enumerate(factors, 1):
+        last = k == len(factors)
+        begin, end = k // XPT, (XO + CX + REACH - k + XPT) // XPT
+        for i in range(ROWS // 8):
+            at = slice(8 * i, 8 * i + 8)
+            here = {t: now[t, 8 * i + 8 : 8 * i + 16, :] for t in range(XTILES)}
+            ahead_x = {t: pltpu.roll(here[t], YS, 1) for t in range(XTILES)}
+            behind_x = {t: pltpu.roll(here[t], 128 - YS, 1) for t in range(XTILES)}
+            for t in range(begin, end):
+                mine = here[t]
+                near = now[t, 8 * i + 7 : 8 * i + 15, :] + now[t, 8 * i + 9 : 8 * i + 17, :]
+                near = near + pltpu.roll(mine, 1, 1) + pltpu.roll(mine, 127, 1)
+                before = ahead_x[t]
+                if t > 0:
+                    before = jnp.where(low_part, ahead_x[t - 1], before)
+                after = behind_x[t]
+                if t + 1 < XTILES:
+                    after = jnp.where(high_part, behind_x[t + 1], after)
+                near = near + before + after
+                left = scaled[t, at, :] - mine + inverse[t, at, :] * near
+                ahead = keep * mine + gain * left
+                if FIRST_TILE <= t < END_TILE:
+                    total[t - FIRST_TILE, at, :] += ahead
+                if not last:
+                    scaled[t, at, :] = left
+                    later[t, 8 * i + 8 : 8 * i + 16, :] = ahead
+        now, later = later, now
+
+    parts = [split(total[t - FIRST_TILE]) for t in range(FIRST_TILE, END_TILE)]
+    u_high = jnp.concatenate([part[0] for part in parts], axis=1)
+    u_low = jnp.concatenate([part[1] for part in parts], axis=1)
+    z_row = row_iota(ROWS) - float(ZO)
+    for chunk in range(groups // GROUPS):
+        if chunk > 0:
+            read_operand(chunk)
         got = dot_nn(u_high, high_ref[...]) + dot_nn(u_low, high_ref[...])
         got = got + dot_nn(u_high, low_ref[...])
         rows = []
         for g in range(GROUPS):
-            main = own_ref[0, chunk * GROUPS + g]
-            more = own_ref[1, chunk * GROUPS + g]
+            main = owned[0, chunk * GROUPS + g]
             off_z = main[6:7]
-            hz = hat(z_row, more[1:2], 1.0 - off_z, off_z)
+            hz = hat(z_row, owned[1, chunk * GROUPS + g, 1:2, :], 1.0 - off_z, off_z)
             value = jnp.sum(hz * got[:, 128 * g : 128 * g + 128], axis=0, keepdims=True)
             rows.append(jnp.where(main[3:4] > 0.0, value, 0.0))
         values = jnp.concatenate(rows, axis=0)
@@ -406,6 +435,13 @@
             start = q * groups + chunk * GROUPS
             values_ref[start : start + GROUPS, :] = moved[:, 0:32]
 
+    for t in range(FIRST_TILE, END_TILE):
+        turned = total[t - FIRST_TILE, ZO : ZO + CZ, :].T
+        for i in range(XPT):
+            plane = XPT * t + i - XO
+            if 0 <= plane < CX:
+                indicator_ref[plane] = turned[YS * i + YO : YS * i + YO + CY, :]
+
 
 def on_device(shape, point_data, point_cells, send_counts):
     gx, gy, gz = shape
@@ -414,7 +450,6 @@
     bricks = 3 * (1 + other_count(gy))
     rows = 8 * -(-(bricks + -(-bricks // 4)) // 4)
     groups = sources // 4
-    params = pltpu.CompilerParams(vmem_limit_bytes=VMEM_LIMIT)
     whole = pl.BlockSpec(memory_space=pltpu.VMEM)
 
     outgoing = pl.pallas_call(
@@ -426,7 +461,7 @@
             pltpu.VMEM((sources, 8, slots), f32),
             pltpu.VMEM((sources, 2, slots), f32),
         ],
-        compiler_params=params,
+        compiler_params=pltpu.CompilerParams(vmem_limit_bytes=56 * MIB),
         name="pack_points",
     )(
         jnp.transpose(point_data, (0, 2, 1, 3)),
@@ -440,24 +475,24 @@
     others = other_count(gy)
     lines = 0
     for planes in (CENTER, LOWER, UPPER):
-        for high in (24,) + (8,) * others:
-            lines += 3 * 16 * -(-len(planes) * high // 16)
-    wide_shape = jax.ShapeDtypeStruct((ROWS, LANES), f32)
-    edge_shape = jax.ShapeDtypeStruct((2, HALO, LANES), f32)
+        for high, size in ((24, 4),) + ((8, 12),) * others:
+            for start in range(0, len(planes), size):
+                count = min(size, len(planes) - start)
+                lines += 3 * 16 * -(-count * high // 16)
+    edge_shape = jax.ShapeDtypeStruct((2, XTILES, HALO, 128), f32)
     steps = groups // GROUPS
-    rhs, density, up, down, own = pl.pallas_call(
+    fields, up, down, own = pl.pallas_call(
         functools.partial(splat_kernel, shape),
         grid=(steps,),
         out_shape=(
-            wide_shape, wide_shape, edge_shape, edge_shape,
+            jax.ShapeDtypeStruct((2, XTILES, ROWS, 128), f32), edge_shape, edge_shape,
             jax.ShapeDtypeStruct((2, groups, 8, 128), f32),
         ),
         in_specs=[pl.BlockSpec((4, GROUPS, rows, 128), lambda s: (0, s, 0, 0))],
         out_specs=(
-            pl.BlockSpec((ROWS, LANES), lambda s: (0, 0)),
-            pl.BlockSpec((ROWS, LANES), lambda s: (0, 0)),
-            pl.BlockSpec((2, HALO, LANES), lambda s: (0, 0, 0)),
-            pl.BlockSpec((2, HALO, LANES), lambda s: (0, 0, 0)),
+            pl.BlockSpec((2, XTILES, ROWS, 128), lambda s: (0, 0, 0, 0)),
+            pl.BlockSpec((2, XTILES, HALO, 128), lambda s: (0, 0, 0, 0)),
+            pl.BlockSpec((2, XTILES, HALO, 128), lambda s: (0, 0, 0, 0)),
             pl.BlockSpec((2, GROUPS, 8, 128), lambda s: (0, s, 0, 0)),
         ),
         scratch_shapes=[
@@ -468,7 +503,7 @@
             pltpu.VMEM((3, XPT * XTILES, 24, 2 * 128), f32),
             pltpu.VMEM((max(others, 1), 3, XPT * XTILES, 8, 2 * 128), f32),
         ],
-        compiler_params=params,
+        compiler_params=pltpu.CompilerParams(vmem_limit_bytes=36 * MIB),
         name="splat_points",
     )(arrived)
 
@@ -482,21 +517,26 @@
             jax.ShapeDtypeStruct((CX, CY, CZ), f32),
             jax.ShapeDtypeStruct((sources, slots), f32),
         ),
-        in_specs=[whole] * 5,
+        in_specs=[pl.BlockSpec(memory_space=pl.ANY)] * 4,
         out_specs=(whole, whole),
         scratch_shapes=[
-            pltpu.VMEM((ROWS + 16, LANES), f32),
-            pltpu.VMEM((ROWS + 16, LANES), f32),
-            pltpu.VMEM((ROWS, LANES), f32),
-            pltpu.VMEM((ROWS, LANES), f32),
-            pltpu.VMEM((ROWS, LANES), f32),
-            pltpu.VMEM((2, 2, 16, LANES), f32),
+            pltpu.VMEM((2, XTILES, ROWS, 128), f32),
+            pltpu.VMEM((2, XTILES, HALO, 128), f32),
+            pltpu.VMEM((2, XTILES, HALO, 128), f32),
+            pltpu.VMEM((2, groups, 8, 128), f32),
+            pltpu.VMEM((XTILES, ROWS + 16, 128), f32),
+            pltpu.VMEM((XTILES, ROWS + 16, 128), f32),
+            pltpu.VMEM((XTILES, ROWS, 128), f32),
+            pltpu.VMEM((XTILES, ROWS, 128), f32),
+            pltpu.VMEM((END_TILE - FIRST_TILE, ROWS, 128), f32),
+            pltpu.VMEM((XPT * END_TILE, GROUPS, 128), f32),
             pltpu.VMEM((depth, 128 * GROUPS), bf16),
             pltpu.VMEM((depth, 128 * GROUPS), bf16),
+            pltpu.SemaphoreType.DMA((4,)),
         ],
-        compiler_params=params,
+        compiler_params=pltpu.CompilerParams(vmem_limit_bytes=16 * MIB),
         name="solve_and_read",
-    )(rhs, density, from_low, from_high, own)
+    )(fields, from_low, from_high, own)
 
     returned = lax.all_to_all(values, AXES, split_axis=0, concat_axis=0, tiled=True)
     return indicator, returned.reshape(1, sources, slots)

time: 59.1 us -> 54.6 us (0.924)
  Pallas kernels: 20.4 us -> 17.3 us
  local copies, waits for them, and re-layouts: 1.22 us -> 0.61 us
    pallas_call x1, Pallas kernels: 12 us -> 9.8 us  [on_device(): pl.pallas_call(functools.partial(splat_kernel, shape), grid=(steps,), out...]
    pallas_call x1, Pallas kernels: 6.3 us -> 5.47 us  [on_device(): pl.pallas_call(functools.partial(solve_kernel, shape), out_shape=(jax.Sha...]
    unnamed x5 -> x1, local copies, waits for them, and re-layouts: 1.22 us -> 0.61 us
where the time goes in v4:
time: 54.6 us; the launch traced here: 54.3 us
  blocking collectives  26.7 us (49%)
  Pallas kernels  17.3 us (32%)
  waiting for transfers between devices  4.59 us (8%)
  starting transfers between devices  4.48 us (8%)
  between operations  0.66 us (1%)
  local copies, waits for them, and re-layouts  0.61 us (1%)
    all_to_all x1, blocking collectives, on_device(): lax.all_to_all(outgoing, AXES, split_axis=0, concat_axis=0, tiled=True)  17.5 us
    pallas_call x1, Pallas kernels, on_device(): pl.pallas_call(functools.partial(splat_kernel, shape), grid=(steps,), out...  9.8 us
    all_to_all x1, blocking collectives, on_device(): lax.all_to_all(values, AXES, split_axis=0, concat_axis=0, tiled=True)  9.17 us
    pallas_call x1, Pallas kernels, on_device(): pl.pallas_call(functools.partial(solve_kernel, shape), out_shape=(jax.Sha...  5.47 us
    ppermute x1, waiting for transfers between devices, on_device(): from_high = lax.ppermute(down, 'gz', [(i + 1, i) for i in range(gz - 1)])  4.26 us
    ppermute x1, starting transfers between devices, on_device(): from_low = lax.ppermute(up, 'gz', [(i, i + 1) for i in range(gz - 1)])  3.01 us
    pallas_call x1, Pallas kernels, on_device(): pl.pallas_call(functools.partial(pack_kernel, shape), out_shape=jax.Shape...  2.05 us
    ppermute x1, starting transfers between devices, on_device(): from_high = lax.ppermute(down, 'gz', [(i + 1, i) for i in range(gz - 1)])  1.47 us
  transfers between devices with their start and end apart: 2, of which 2 were waited for; matrix products, arithmetic and copies ran while one was open for 0% of the time, Pallas kernels for 0%

profile of v4, /device:TPU:0, one launch (start us, length us, event | category | flops | bytes accessed | tf_op | source)
XLA Modules:
  0.0 54.3 jit_solution(4519592741994524915)
XLA Ops:
  0.6 2.1 %pack_points.1 = f32[32,16,128]{2,1,0:T(8,128)} custom-call(f32[1,7,32,32]{3,2,1,0:T(8,128)} %bitcast.9, s32[1,3,32,32]{3,2,1,0:T(8,128)} %bitcast.11, s32[1,32]{1,0:T(1,128)} %counts_ref.1), custom_call_target="tpu_custom_call" | custom-call | tf_op jit(solution)/shard_map/pack_points/pallas_call | solution.py:455
  2.7 17.5 %all_to_all.14 = f32[32,16,128]{2,1,0:T(8,128)S(1)} all-to-all(f32[32,16,128]{2,1,0:T(8,128)} %pack_points.1), channel_id=1, replica_groups=mesh['gx'=4,'gy'=2,'gz'=4] {'gx','gy','gz'}, dimensions={0} | all-to-all | bytes 524288 | tf_op jit(solution)/shard_map/all_to_all | solution.py:472
  20.2 9.8 %splat_points.1 = (f32[2,7,144,128]{3,2,1,0:T(8,128)S(1)}, f32[2,7,8,128]{3,2,1,0:T(8,128)S(1)}, f32[2,7,8,128]{3,2,1,0:T(8,128)S(1)}, f32[2,8,8,128]{3,2,1,0:T(8,128)S(1)}) custom-call(f32[4,8,16,128]{3,2,1,0:T(8,128)S(1)} %bitcast.7), custom_call_target="tpu_custom_call" | custom-call | tf_op jit(solution)/shard_map/splat_points/pallas_call | solution.py:484
  30.0 3.0 %collective-permute-start = (f32[2,7,8,128]{3,2,1,0:T(8,128)S(1)}, f32[2,7,8,128]{3,2,1,0:T(8,128)S(1)}, u32[]{:S(2)}, u32[]{:S(2)}) collective-permute-start(f32[2,7,8,128]{3,2,1,0:T(8,128)S(1)} %get-tuple-element.9), channel_id=1, source_target_pairs={{0,1},{1,2},{2,3},{4,5},{5,6},{6,7},{8,9},{9,10},{10,11},{12,13},{... | collective-permute-start | bytes 172040 | tf_op jit(solution)/shard_map/ppermute | solution.py:510
  33.0 1.5 %collective-permute-start.1 = (f32[2,7,8,128]{3,2,1,0:T(8,128)S(1)}, f32[2,7,8,128]{3,2,1,0:T(8,128)S(1)}, u32[]{:S(2)}, u32[]{:S(2)}) collective-permute-start(f32[2,7,8,128]{3,2,1,0:T(8,128)S(1)} %get-tuple-element.10), channel_id=1, source_target_pairs={{1,0},{2,1},{3,2},{5,4},{6,5},{7,6},{9,8},{10,9},{11,10},{13,12},{... | collective-permute-start | bytes 172040 | tf_op jit(solution)/shard_map/ppermute | solution.py:511
  34.5 0.3 collective-permute-done.from_low_ref
  34.8 4.3 %collective-permute-done.1.from_high_ref = f32[2,7,8,128]{3,2,1,0:T(8,128)S(1)} collective-permute-done((f32[2,7,8,128]{3,2,1,0:T(8,128)S(1)}, f32[2,7,8,128]{3,2,1,0:T(8,128)S(1)}, u32[]{:S(2)}, u32[]{:S(2)}) %collective-permute-start.1) | collective-permute-done | bytes 57376 | tf_op jit(solution)/shard_map/ppermute | solution.py:511
  39.1 5.5 %solve_and_read.1 = (f32[16,16,128]{2,1,0:T(8,128)}, f32[32,32]{1,0:T(8,128)S(1)}) custom-call(f32[2,7,144,128]{3,2,1,0:T(8,128)S(1)} %get-tuple-element.8.fields_ref, f32[2,7,8,128]{3,2,1,0:T(8,128)S(1)} %collective-permute-done.from_low_ref, f32[2,7,8,128]{3,2,1,0:T(8,128)S(1)} %collective-permute-done.1.from_high_ref, ...), custom_call_target="tpu_custom_call" | custom-call | tf_op jit(solution)/shard_map/solve_and_read/pallas_call | solution.py:514
  44.6 9.2 %all_to_all.15 = f32[32,1,32]{2,1,0:T(1,128)S(1)} all-to-all(f32[32,1,32]{2,1,0:T(1,128)S(1)} %bitcast.8), channel_id=1, replica_groups=mesh['gx'=4,'gy'=2,'gz'=4] {'gx','gy','gz'}, dimensions={0} | all-to-all | bytes 8192 | tf_op jit(solution)/shard_map/all_to_all | solution.py:541
  53.7 0.6 %copy.7 = f32[1,32,32]{2,1,0:T(8,128)} copy(f32[1,32,32]{2,1,0:T(8,128)S(1)} %bitcast.10) | data formatting | bytes 8192
Async XLA Ops:
  30.0 4.8 %collective-permute-start = (f32[2,7,8,128]{3,2,1,0:T(8,128)S(1)}, f32[2,7,8,128]{3,2,1,0:T(8,128)S(1)}, u32[]{:S(2)}, u32[]{:S(2)}) collective-permute-start(f32[2,7,8,128]{3,2,1,0:T(8,128)S(1)} %get-tuple-element.9), channel_id=1, source_target_pairs={{0,1},{1,2},{2,3},{4,5},{5,6},{6,7},{8,9},{9,10},{10,11},{12,13},{... | collective-permute-start | bytes 172040 | tf_op jit(solution)/shard_map/ppermute | solution.py:510
  33.0 6.1 %collective-permute-start.1 = (f32[2,7,8,128]{3,2,1,0:T(8,128)S(1)}, f32[2,7,8,128]{3,2,1,0:T(8,128)S(1)}, u32[]{:S(2)}, u32[]{:S(2)}) collective-permute-start(f32[2,7,8,128]{3,2,1,0:T(8,128)S(1)} %get-tuple-element.10), channel_id=1, source_target_pairs={{1,0},{2,1},{3,2},{5,4},{6,5},{7,6},{9,8},{10,9},{11,10},{13,12},{... | collective-permute-start | bytes 172040 | tf_op jit(solution)/shard_map/ppermute | solution.py:511

commit v5 on v4

--- a/solution.py
+++ b/solution.py
@@ -73,16 +73,26 @@
     others = other_count(gy)
     bricks = 3 * (1 + others)
     weight = jnp.where(lane < counts, data_ref[0, 3], 0.0)
-    for c in range(3):
-        main[:, c, :] = data_ref[0, c] * (-0.5 * weight)
-    main[:, 3, :] = weight
-    for c in range(4, 7):
-        main[:, c, :] = data_ref[0, c]
-    main[:, 7, :] = cells_ref[0, 0].astype(f32)
-    extra[:, 0, :] = cells_ref[0, 1].astype(f32)
-    extra[:, 1, :] = cells_ref[0, 2].astype(f32)
-    out_ref[...] = jnp.zeros_like(out_ref)
-    for d in range(gx * gy * gz):
+    cells = [cells_ref[0, c].astype(f32) for c in range(3)]
+    channels = [data_ref[0, c] * (-0.5 * weight) for c in range(3)]
+    channels += [weight] + [data_ref[0, c] for c in range(4, 7)] + [cells[0]]
+
+    def placed(value, part):
+        pieces = [jnp.zeros((sources, slots * part), f32)] if part else []
+        pieces.append(value)
+        if part < 3:
+            pieces.append(jnp.zeros((sources, 128 - slots * (part + 1)), f32))
+        return jnp.concatenate(pieces, axis=1)
+
+    for part in range(min(bricks, 4)):
+        for c in range(8):
+            main[part, :, c, :] = placed(channels[c], part)
+    extra[...] = jnp.zeros_like(extra)
+    for b in range(bricks):
+        place, row = extra_place(b, bricks)
+        for c in range(2):
+            extra[b, :, row + c, :] = placed(cells[1 + c], place % 4)
+    for d in range(sources):
         x, y, z = d // (gy * gz), (d // gz) % gy, d % gz
         if others == 0:
             ys = (y,)
@@ -90,19 +100,22 @@
             ys = (y, 1 - y)
         else:
             ys = (y, y - 1, y + 1)
+        sums = [None] * (out_ref.shape[1] // 8)
         for e, by in enumerate(ys):
             for o, bx in enumerate((x, x - 1, x + 1)):
                 if not (0 <= bx < gx and 0 <= by < gy):
                     continue
                 b = e * 3 + o
                 source = (bx * gy + by) * gz + z
-                tile, part = b // 4, b % 4
-                out_ref[d, 8 * tile : 8 * tile + 8, slots * part : slots * part + slots] = main[source]
-                place, row = extra_place(b, bricks)
-                tile, part = place // 4, place % 4
-                out_ref[
-                    d, 8 * tile + row : 8 * tile + row + 2, slots * part : slots * part + slots
-                ] = extra[source]
+                place, _ = extra_place(b, bricks)
+                for tile, value in (
+                    (b // 4, main[b % 4, source]), (place // 4, extra[b, source])
+                ):
+                    sums[tile] = value if sums[tile] is None else sums[tile] + value
+        for tile, value in enumerate(sums):
+            if value is None:
+                value = jnp.zeros((8, 128), f32)
+            out_ref[d, 8 * tile : 8 * tile + 8, :] = value
 
 
 def hat(coordinate, cell, low, high):
@@ -174,10 +187,10 @@
     own_row = row_iota(24) + float(8 - YO)
 
     def multiply(begin, count, b, e, high, planes):
-        lines = slice(begin, begin + 3 * count)
-        got = dot_nn(left_ref[0, lines, :], right_ref[b, 0, :, 0:ROWS])
-        got = got + dot_nn(left_ref[1, lines, :], right_ref[b, 0, :, 0:ROWS])
-        got = got + dot_nn(left_ref[0, lines, :], right_ref[b, 1, :, 0:ROWS])
+        size = 3 * count
+        both = dot_nn(left_ref[begin : begin + 2 * size, :], right_ref[b, 0, :, 0:ROWS])
+        got = both[:size] + both[size:]
+        got = got + dot_nn(left_ref[begin : begin + size, :], right_ref[b, 1, :, 0:ROWS])
         for c in range(3):
             for i, plane in enumerate(planes):
                 value = got[c * count + i * high : c * count + i * high + high]
@@ -186,6 +199,53 @@
                 else:
                     add(beside, (e - 1, c, plane), value)
 
+        if single and e == 0:
+            for t in sorted({plane // XPT for plane in planes}):
+                unfinished[t] -= 1
+                if unfinished[t] == 0:
+                    finish(t)
+
+    row8 = lax.broadcasted_iota(jnp.int32, (8, 2 * 128), 0)
+    zero = jnp.zeros((8, 2 * 128), f32)
+
+    def finish(t):
+        turned = []
+        for c in range(3):
+            pieces = []
+            for plane in range(XPT * t, XPT * t + XPT):
+                if plane > UPPER[-1]:
+                    pieces.append(jnp.zeros((YS, 2 * 128), f32))
+                    continue
+                parts = [zero] + [near[c, plane, 8 * i : 8 * i + 8, :] for i in range(3)]
+                if others:
+                    if others == 1:
+                        value = beside[0, c, plane]
+                        low_part = jnp.where(my == 0, 0.0, value)
+                        high_part = jnp.where(my == 0, value, 0.0)
+                    else:
+                        low_part, high_part = beside[0, c, plane], beside[1, c, plane]
+                    moved = pltpu.roll(low_part, 4, 0)
+                    parts[0] = jnp.where(row8 >= 4, moved, 0.0)
+                    parts[1] = parts[1] + jnp.where(row8 < 4, moved, 0.0)
+                    parts[3] = parts[3] + high_part
+                pieces.extend(parts)
+            stacked = jnp.concatenate(pieces, axis=0)
+            turned.append(
+                jnp.concatenate([stacked[:, :128].T, stacked[:, 128:].T[: ROWS - 128]], axis=0)
+            )
+        fields_ref[0, t] = (
+            turned[0] + pltpu.roll(turned[1], ROWS - 1, 0) - pltpu.roll(turned[1], 1, 0)
+        )
+        fields_ref[1, t] = turned[2]
+
+    unfinished = [
+        sum(
+            plane // XPT == t and (i == 0 or planes[i - 1] // XPT != t)
+            for planes in (CENTER, LOWER, UPPER)
+            for i, plane in enumerate(planes)
+        )
+        for t in range(XTILES)
+    ]
     row_at = 0
     waiting = None
     for e in reversed(range(1 + others)):
@@ -200,7 +260,7 @@
             first = jnp.where(above, WINDOW_HIGH - YO - CY, WINDOW_LOW - YO + CY)
             y_row = row_iota(8) + first.astype(f32)
         high = y_row.shape[0]
-        for o, shift, planes in ((1, -1, LOWER), (0, 0, CENTER), (2, 1, UPPER)):
+        for o, shift, planes in ((1, -1, LOWER), (2, 1, UPPER), (0, 0, CENTER)):
             b = e * 3 + o
             place, row = extra_place(b, bricks)
             x_limit = jnp.where(mx + shift == gx - 1, CX, CX + 1).astype(f32)
@@ -245,54 +305,25 @@
                                 rows.append(hx * (part_z if c == 1 else part_w))
                         main_part, rest = split(stack_rows(rows, 16))
                         begin = row_at + c * count
-                        left_ref[0, begin : begin + count, at] = main_part
-                        left_ref[1, begin : begin + count, at] = rest
+                        left_ref[begin : begin + count, at] = main_part
+                        begin = begin + 3 * count
+                        left_ref[begin : begin + count, at] = rest
                 if waiting is not None:
                     waiting()
                 waiting = functools.partial(
                     multiply, row_at, count, b, e, high, [planes[n] for n in block]
                 )
-                row_at += 3 * count
+                row_at += 6 * count
     waiting()
 
-    @pl.when(step == pl.num_programs(0) - 1)
-    def _():
-        row8 = lax.broadcasted_iota(jnp.int32, (8, 2 * 128), 0)
-        zero = jnp.zeros((8, 2 * 128), f32)
-        for t in range(XTILES):
-            turned = []
-            for c in range(3):
-                pieces = []
-                for plane in range(XPT * t, XPT * t + XPT):
-                    if plane > UPPER[-1]:
-                        pieces.append(jnp.zeros((YS, 2 * 128), f32))
-                        continue
-                    parts = [zero] + [near[c, plane, 8 * i : 8 * i + 8, :] for i in range(3)]
-                    if others:
-                        if others == 1:
-                            value = beside[0, c, plane]
-                            low_part = jnp.where(my == 0, 0.0, value)
-                            high_part = jnp.where(my == 0, value, 0.0)
-                        else:
-                            low_part, high_part = beside[0, c, plane], beside[1, c, plane]
-                        moved = pltpu.roll(low_part, 4, 0)
-                        parts[0] = jnp.where(row8 >= 4, moved, 0.0)
-                        parts[1] = parts[1] + jnp.where(row8 < 4, moved, 0.0)
-                        parts[3] = parts[3] + high_part
-                    pieces.extend(parts)
-                stacked = jnp.concatenate(pieces, axis=0)
-                turned.append(
-                    jnp.concatenate([stacked[:, :128].T, stacked[:, 128:].T[: ROWS - 128]], axis=0)
-                )
-            fields_ref[0, t] = (
-                turned[0]
-                + pltpu.roll(turned[1], ROWS - 1, 0)
-                - pltpu.roll(turned[1], 1, 0)
-            )
-            fields_ref[1, t] = turned[2]
-        for c in range(2):
-            up_ref[c] = fields_ref[c, :, UP_AT : UP_AT + HALO, :]
-            down_ref[c] = fields_ref[c, :, DOWN_AT : DOWN_AT + HALO, :]
+    if not single:
+        @pl.when(step == pl.num_programs(0) - 1)
+        def _():
+            for t in range(XTILES):
+                finish(t)
+    for c in range(2):
+        up_ref[c] = fields_ref[c, :, UP_AT : UP_AT + HALO, :]
+        down_ref[c] = fields_ref[c, :, DOWN_AT : DOWN_AT + HALO, :]
 
 
 def chebyshev_factors():
@@ -416,12 +447,13 @@
     parts = [split(total[t - FIRST_TILE]) for t in range(FIRST_TILE, END_TILE)]
     u_high = jnp.concatenate([part[0] for part in parts], axis=1)
     u_low = jnp.concatenate([part[1] for part in parts], axis=1)
+    u_both = jnp.concatenate([u_high, u_low], axis=0)
     z_row = row_iota(ROWS) - float(ZO)
     for chunk in range(groups // GROUPS):
         if chunk > 0:
             read_operand(chunk)
-        got = dot_nn(u_high, high_ref[...]) + dot_nn(u_low, high_ref[...])
-        got = got + dot_nn(u_high, low_ref[...])
+        got = dot_nn(u_both, high_ref[...])
+        got = got[:ROWS] + got[ROWS:] + dot_nn(u_high, low_ref[...])
         rows = []
         for g in range(GROUPS):
             main = owned[0, chunk * GROUPS + g]
@@ -458,8 +490,8 @@
         in_specs=[whole, whole, whole],
         out_specs=whole,
         scratch_shapes=[
-            pltpu.VMEM((sources, 8, slots), f32),
-            pltpu.VMEM((sources, 2, slots), f32),
+            pltpu.VMEM((4, sources, 8, 128), f32),
+            pltpu.VMEM((bricks, sources, 8, 128), f32),
         ],
         compiler_params=pltpu.CompilerParams(vmem_limit_bytes=56 * MIB),
         name="pack_points",
@@ -478,7 +510,7 @@
         for high, size in ((24, 4),) + ((8, 12),) * others:
             for start in range(0, len(planes), size):
                 count = min(size, len(planes) - start)
-                lines += 3 * 16 * -(-count * high // 16)
+                lines += 6 * 16 * -(-count * high // 16)
     edge_shape = jax.ShapeDtypeStruct((2, XTILES, HALO, 128), f32)
     steps = groups // GROUPS
     fields, up, down, own = pl.pallas_call(
@@ -497,7 +529,7 @@
         ),
         scratch_shapes=[
             pltpu.VMEM((rows // 2, GROUPS, 8, 128), f32),
-            pltpu.VMEM((2, lines, 128 * GROUPS), bf16),
+            pltpu.VMEM((lines, 128 * GROUPS), bf16),
             pltpu.VMEM((bricks, 2, 128 * GROUPS, 2 * 128), bf16),
             pltpu.VMEM((bricks, 2, len(CENTER), GROUPS, 128), f32),
             pltpu.VMEM((3, XPT * XTILES, 24, 2 * 128), f32),
@@ -538,8 +570,10 @@
         name="solve_and_read",
     )(fields, from_low, from_high, own)
 
-    returned = lax.all_to_all(values, AXES, split_axis=0, concat_axis=0, tiled=True)
-    return indicator, returned.reshape(1, sources, slots)
+    returned = lax.all_to_all(
+        values.reshape(1, sources, slots), AXES, split_axis=1, concat_axis=1, tiled=True
+    )
+    return indicator, returned
 
 
 def solution(mesh):

time: 54.6 us -> 54.5 us (level)
  no operation moved by 1% of the time
where the time goes in v5:
time: 54.5 us; the launch traced here: 54.2 us
  blocking collectives  26.7 us (49%)
  Pallas kernels  17.2 us (32%)
  waiting for transfers between devices  4.59 us (8%)
  starting transfers between devices  4.48 us (8%)
  between operations  0.66 us (1%)
  local copies, waits for them, and re-layouts  0.61 us (1%)
    all_to_all x1, blocking collectives, on_device(): lax.all_to_all(outgoing, AXES, split_axis=0, concat_axis=0, tiled=True)  17.5 us
    pallas_call x1, Pallas kernels, on_device(): pl.pallas_call(functools.partial(splat_kernel, shape), grid=(steps,), out...  9.65 us
    all_to_all x1, blocking collectives, on_device(): lax.all_to_all(values.reshape(1, sources, slots), AXES, split_axis=1, con...  9.17 us
    pallas_call x1, Pallas kernels, on_device(): pl.pallas_call(functools.partial(solve_kernel, shape), out_shape=(jax.Sha...  5.42 us
    ppermute x1, waiting for transfers between devices, on_device(): from_high = lax.ppermute(down, 'gz', [(i + 1, i) for i in range(gz - 1)])  4.26 us
    ppermute x1, starting transfers between devices, on_device(): from_low = lax.ppermute(up, 'gz', [(i, i + 1) for i in range(gz - 1)])  3 us
    pallas_call x1, Pallas kernels, on_device(): pl.pallas_call(functools.partial(pack_kernel, shape), out_shape=jax.Shape...  2.15 us
    ppermute x1, starting transfers between devices, on_device(): from_high = lax.ppermute(down, 'gz', [(i + 1, i) for i in range(gz - 1)])  1.47 us
  transfers between devices with their start and end apart: 2, of which 2 were waited for; matrix products, arithmetic and copies ran while one was open for 0% of the time, Pallas kernels for 0%

profile of v5, /device:TPU:0, one launch (start us, length us, event | category | flops | bytes accessed | tf_op | source)
XLA Modules:
  0.0 54.2 jit_solution(1347079341235399984)
XLA Ops:
  0.6 2.2 %pack_points.1 = f32[32,16,128]{2,1,0:T(8,128)} custom-call(f32[1,7,32,32]{3,2,1,0:T(8,128)} %bitcast.9, s32[1,3,32,32]{3,2,1,0:T(8,128)} %bitcast.11, s32[1,32]{1,0:T(1,128)} %counts_ref.1), custom_call_target="tpu_custom_call" | custom-call | tf_op jit(solution)/shard_map/pack_points/pallas_call | solution.py:487
  2.8 17.5 %all_to_all.10 = f32[32,16,128]{2,1,0:T(8,128)S(1)} all-to-all(f32[32,16,128]{2,1,0:T(8,128)} %pack_points.1), channel_id=1, replica_groups=mesh['gx'=4,'gy'=2,'gz'=4] {'gx','gy','gz'}, dimensions={0} | all-to-all | bytes 524288 | tf_op jit(solution)/shard_map/all_to_all | solution.py:504
  20.3 9.7 %splat_points.1 = (f32[2,7,144,128]{3,2,1,0:T(8,128)S(1)}, f32[2,7,8,128]{3,2,1,0:T(8,128)S(1)}, f32[2,7,8,128]{3,2,1,0:T(8,128)S(1)}, f32[2,8,8,128]{3,2,1,0:T(8,128)S(1)}) custom-call(f32[4,8,16,128]{3,2,1,0:T(8,128)S(1)} %bitcast.7), custom_call_target="tpu_custom_call" | custom-call | tf_op jit(solution)/shard_map/splat_points/pallas_call | solution.py:516
  29.9 3.0 %collective-permute-start = (f32[2,7,8,128]{3,2,1,0:T(8,128)S(1)}, f32[2,7,8,128]{3,2,1,0:T(8,128)S(1)}, u32[]{:S(2)}, u32[]{:S(2)}) collective-permute-start(f32[2,7,8,128]{3,2,1,0:T(8,128)S(1)} %get-tuple-element.9), channel_id=1, source_target_pairs={{0,1},{1,2},{2,3},{4,5},{5,6},{6,7},{8,9},{9,10},{10,11},{12,13},{... | collective-permute-start | bytes 172040 | tf_op jit(solution)/shard_map/ppermute | solution.py:542
  33.0 1.5 %collective-permute-start.1 = (f32[2,7,8,128]{3,2,1,0:T(8,128)S(1)}, f32[2,7,8,128]{3,2,1,0:T(8,128)S(1)}, u32[]{:S(2)}, u32[]{:S(2)}) collective-permute-start(f32[2,7,8,128]{3,2,1,0:T(8,128)S(1)} %get-tuple-element.10), channel_id=1, source_target_pairs={{1,0},{2,1},{3,2},{5,4},{6,5},{7,6},{9,8},{10,9},{11,10},{13,12},{... | collective-permute-start | bytes 172040 | tf_op jit(solution)/shard_map/ppermute | solution.py:543
  34.4 0.3 collective-permute-done.from_low_ref
  34.8 4.3 %collective-permute-done.1.from_high_ref = f32[2,7,8,128]{3,2,1,0:T(8,128)S(1)} collective-permute-done((f32[2,7,8,128]{3,2,1,0:T(8,128)S(1)}, f32[2,7,8,128]{3,2,1,0:T(8,128)S(1)}, u32[]{:S(2)}, u32[]{:S(2)}) %collective-permute-start.1) | collective-permute-done | bytes 57376 | tf_op jit(solution)/shard_map/ppermute | solution.py:543
  39.0 5.4 %solve_and_read.1 = (f32[16,16,128]{2,1,0:T(8,128)}, f32[32,32]{1,0:T(8,128)S(1)}) custom-call(f32[2,7,144,128]{3,2,1,0:T(8,128)S(1)} %get-tuple-element.8.fields_ref, f32[2,7,8,128]{3,2,1,0:T(8,128)S(1)} %collective-permute-done.from_low_ref, f32[2,7,8,128]{3,2,1,0:T(8,128)S(1)} %collective-permute-done.1.from_high_ref, ...), custom_call_target="tpu_custom_call" | custom-call | tf_op jit(solution)/shard_map/solve_and_read/pallas_call | solution.py:546
  44.5 9.2 %all_to_all.11 = f32[1,32,32]{2,0,1:T(1,128)S(1)} all-to-all(f32[1,32,32]{2,0,1:T(1,128)S(1)} %bitcast.8), channel_id=1, replica_groups=mesh['gx'=4,'gy'=2,'gz'=4] {'gx','gy','gz'}, dimensions={1} | all-to-all | bytes 8192 | tf_op jit(solution)/shard_map/all_to_all | solution.py:573
  53.6 0.6 %copy.8 = f32[1,32,32]{2,1,0:T(8,128)} copy(f32[1,32,32]{2,1,0:T(8,128)S(1)} %bitcast.10) | data formatting | bytes 8192
Async XLA Ops:
  29.9 4.8 %collective-permute-start = (f32[2,7,8,128]{3,2,1,0:T(8,128)S(1)}, f32[2,7,8,128]{3,2,1,0:T(8,128)S(1)}, u32[]{:S(2)}, u32[]{:S(2)}) collective-permute-start(f32[2,7,8,128]{3,2,1,0:T(8,128)S(1)} %get-tuple-element.9), channel_id=1, source_target_pairs={{0,1},{1,2},{2,3},{4,5},{5,6},{6,7},{8,9},{9,10},{10,11},{12,13},{... | collective-permute-start | bytes 172040 | tf_op jit(solution)/shard_map/ppermute | solution.py:542
  33.0 6.1 %collective-permute-start.1 = (f32[2,7,8,128]{3,2,1,0:T(8,128)S(1)}, f32[2,7,8,128]{3,2,1,0:T(8,128)S(1)}, u32[]{:S(2)}, u32[]{:S(2)}) collective-permute-start(f32[2,7,8,128]{3,2,1,0:T(8,128)S(1)} %get-tuple-element.10), channel_id=1, source_target_pairs={{1,0},{2,1},{3,2},{5,4},{6,5},{7,6},{9,8},{10,9},{11,10},{13,12},{... | collective-permute-start | bytes 172040 | tf_op jit(solution)/shard_map/ppermute | solution.py:543

commit v6 on v5

--- a/solution.py
+++ b/solution.py
@@ -142,7 +142,7 @@
 
 def splat_kernel(
     shape, recv_ref, fields_ref, up_ref, down_ref, own_ref,
-    points, left_ref, right_ref, hx_ref, near, beside,
+    points, left_ref, right_ref, hx_ref, near, beside, slope,
 ):
     gx, gy, gz = shape
     mx, my, mz = lax.axis_index("gx"), lax.axis_index("gy"), lax.axis_index("gz")
@@ -158,9 +158,9 @@
     def add(ref, place, value):
         if single and place not in written:
             written.add(place)
-            ref[place + (slice(None), slice(0, ROWS))] = value
+            ref[place] = value
         else:
-            ref[place + (slice(None), slice(0, ROWS))] += value
+            ref[place] += value
 
     if not single:
         @pl.when(step == 0)
@@ -183,14 +183,15 @@
     own_ref[1] = points[bricks]
 
     z_limit = jnp.where(mz == gz - 1, CZ, CZ + 1).astype(f32)
-    z_row = row_iota(ROWS) - float(ZO)
+    z_row = row_iota(CZ)
     own_row = row_iota(24) + float(8 - YO)
+    point_lane = lax.broadcasted_iota(jnp.int32, (128, 128), 1)
 
     def multiply(begin, count, b, e, high, planes):
         size = 3 * count
-        both = dot_nn(left_ref[begin : begin + 2 * size, :], right_ref[b, 0, :, 0:ROWS])
+        both = dot_nn(left_ref[begin : begin + 2 * size, :], right_ref[b, 0])
         got = both[:size] + both[size:]
-        got = got + dot_nn(left_ref[begin : begin + size, :], right_ref[b, 1, :, 0:ROWS])
+        got = got + dot_nn(left_ref[begin : begin + size, :], right_ref[b, 1])
         for c in range(3):
             for i, plane in enumerate(planes):
                 value = got[c * count + i * high : c * count + i * high + high]
@@ -230,14 +231,36 @@
                     parts[3] = parts[3] + high_part
                 pieces.extend(parts)
             stacked = jnp.concatenate(pieces, axis=0)
-            turned.append(
-                jnp.concatenate([stacked[:, :128].T, stacked[:, 128:].T[: ROWS - 128]], axis=0)
-            )
-        fields_ref[0, t] = (
-            turned[0] + pltpu.roll(turned[1], ROWS - 1, 0) - pltpu.roll(turned[1], 1, 0)
-        )
-        fields_ref[1, t] = turned[2]
-
+            turned.append(stacked[:, :CZ].T)
+            above = stacked[:, CZ:]
+            n, at = divmod(3 * t + c, 128 // GROUPS)
+            if at:
+                above = pltpu.roll(above, GROUPS * at, 1)
+            if tops[n] is not None:
+                above = jnp.where(point_lane // GROUPS == at, above, tops[n])
+            tops[n] = above
+        fields_ref[0, t, ZO : ZO + CZ, :] = turned[0]
+        slope[t, ZO + 8 : ZO + 8 + CZ, :] = turned[1]
+        fields_ref[1, t, ZO : ZO + CZ, :] = turned[2]
+
+    def finish_all():
+        zero = jnp.zeros((8, 128), f32)
+        sums = [jnp.sum(top.T.reshape(-1, GROUPS, 128), axis=1, keepdims=True) for top in tops]
+        for t in range(XTILES):
+            at = [divmod(3 * t + c, 128 // GROUPS) for c in range(3)]
+            above = [sums[n][i] for n, i in at]
+            below = jnp.concatenate([above[1], jnp.zeros((7, 128), f32)], axis=0)
+            slope[t, 0 : ZO + 8, :] = jnp.zeros((ZO + 8, 128), f32)
+            slope[t, ZO + 8 + CZ : ZO + 16 + CZ, :] = below
+            slope[t, ZO + 16 + CZ : ROWS + 16, :] = zero
+            for c in range(2):
+                fields_ref[c, t, 0:ZO, :] = zero
+                fields_ref[c, t, ZO + CZ : ROWS, :] = jnp.concatenate(
+                    [above[2 * c], jnp.zeros((7, 128), f32)], axis=0
+                )
+            fields_ref[0, t] += slope[t, 9 : ROWS + 9, :] - slope[t, 7 : ROWS + 7, :]
+
+    tops = [None] * -(-3 * XTILES * GROUPS // 128)
     unfinished = [
         sum(
             plane // XPT == t and (i == 0 or planes[i - 1] // XPT != t)
@@ -272,17 +295,23 @@
                 at = float(plane - XO - CX * shift)
                 hx_ref[b, 0, n] = hat(at, cell_x, low_x, high_x)
                 hx_ref[b, 1, n] = hat_slope(at, cell_x, low_x, high_x)
+            cell_z, off_z = points[place, :, row + 1, :], points[b, :, 6, :]
+            top = jnp.where((cell_z + 1.0 == float(CZ)) & (cell_z + 1.0 < z_limit), off_z, 0.0)
+            top_columns = jnp.concatenate([top, jnp.zeros((128 - GROUPS, 128), f32)], axis=0).T
+            top_high = top_columns.astype(bf16).astype(f32)
+            top_low = top_columns - top_high
             y_parts = []
             for g in range(GROUPS):
                 main = points[b, g]
                 more = points[place, g]
                 cell_y, cell_z = more[row : row + 1], more[row + 1 : row + 2]
                 off_y, off_z = main[5:6], main[6:7]
-                high_z = jnp.where(cell_z + 1.0 < z_limit, off_z, 0.0)
-                hz_high, hz_low = split(hat(z_row, cell_z, 1.0 - off_z, high_z))
                 at = slice(128 * g, 128 * g + 128)
-                right_ref[b, 0, at, 0:ROWS] = hz_high.T
-                right_ref[b, 1, at, 0:ROWS] = hz_low.T
+                hz_high, hz_low = split(hat(z_row, cell_z, 1.0 - off_z, off_z).T)
+                right_ref[b, 0, at, 0:CZ] = hz_high
+                right_ref[b, 1, at, 0:CZ] = hz_low
+                right_ref[b, 0, at, CZ : CZ + 128] = jnp.where(point_lane == g, top_high, 0.0).astype(bf16)
+                right_ref[b, 1, at, CZ : CZ + 128] = jnp.where(point_lane == g, top_low, 0.0).astype(bf16)
                 high_y = jnp.where(cell_y + 1.0 < y_limit, off_y, 0.0)
                 hy = hat(y_row, cell_y, 1.0 - off_y, high_y)
                 dy = hat_slope(y_row, cell_y, 1.0 - off_y, high_y)
@@ -321,6 +350,9 @@
         def _():
             for t in range(XTILES):
                 finish(t)
+            finish_all()
+    else:
+        finish_all()
     for c in range(2):
         up_ref[c] = fields_ref[c, :, UP_AT : UP_AT + HALO, :]
         down_ref[c] = fields_ref[c, :, DOWN_AT : DOWN_AT + HALO, :]
@@ -534,6 +566,7 @@
             pltpu.VMEM((bricks, 2, len(CENTER), GROUPS, 128), f32),
             pltpu.VMEM((3, XPT * XTILES, 24, 2 * 128), f32),
             pltpu.VMEM((max(others, 1), 3, XPT * XTILES, 8, 2 * 128), f32),
+            pltpu.VMEM((XTILES, ROWS + 16, 128), f32),
         ],
         compiler_params=pltpu.CompilerParams(vmem_limit_bytes=36 * MIB),
         name="splat_points",

time: 54.5 us -> 54.5 us (level)
  no operation moved by 1% of the time
where the time goes in v6:
time: 54.5 us; the launch traced here: 54.2 us
  blocking collectives  26.7 us (49%)
  Pallas kernels  17.2 us (32%)
  waiting for transfers between devices  4.59 us (8%)
  starting transfers between devices  4.48 us (8%)
  between operations  0.66 us (1%)
  local copies, waits for them, and re-layouts  0.61 us (1%)
    all_to_all x1, blocking collectives, on_device(): lax.all_to_all(outgoing, AXES, split_axis=0, concat_axis=0, tiled=True)  17.5 us
    pallas_call x1, Pallas kernels, on_device(): pl.pallas_call(functools.partial(splat_kernel, shape), grid=(steps,), out...  9.62 us
    all_to_all x1, blocking collectives, on_device(): lax.all_to_all(values.reshape(1, sources, slots), AXES, split_axis=1, con...  9.17 us
    pallas_call x1, Pallas kernels, on_device(): pl.pallas_call(functools.partial(solve_kernel, shape), out_shape=(jax.Sha...  5.42 us
    ppermute x1, waiting for transfers between devices, on_device(): from_high = lax.ppermute(down, 'gz', [(i + 1, i) for i in range(gz - 1)])  4.26 us
    ppermute x1, starting transfers between devices, on_device(): from_low = lax.ppermute(up, 'gz', [(i, i + 1) for i in range(gz - 1)])  3.01 us
    pallas_call x1, Pallas kernels, on_device(): pl.pallas_call(functools.partial(pack_kernel, shape), out_shape=jax.Shape...  2.15 us
    ppermute x1, starting transfers between devices, on_device(): from_high = lax.ppermute(down, 'gz', [(i + 1, i) for i in range(gz - 1)])  1.47 us
  transfers between devices with their start and end apart: 2, of which 2 were waited for; matrix products, arithmetic and copies ran while one was open for 0% of the time, Pallas kernels for 0%

profile of v6, /device:TPU:0, one launch (start us, length us, event | category | flops | bytes accessed | tf_op | source)
XLA Modules:
  0.0 54.2 jit_solution(13194562355346840596)
XLA Ops:
  0.6 2.2 %pack_points.1 = f32[32,16,128]{2,1,0:T(8,128)} custom-call(f32[1,7,32,32]{3,2,1,0:T(8,128)} %bitcast.9, s32[1,3,32,32]{3,2,1,0:T(8,128)} %bitcast.11, s32[1,32]{1,0:T(1,128)} %counts_ref.1), custom_call_target="tpu_custom_call" | custom-call | tf_op jit(solution)/shard_map/pack_points/pallas_call | solution.py:519
  2.8 17.5 %all_to_all.10 = f32[32,16,128]{2,1,0:T(8,128)S(1)} all-to-all(f32[32,16,128]{2,1,0:T(8,128)} %pack_points.1), channel_id=1, replica_groups=mesh['gx'=4,'gy'=2,'gz'=4] {'gx','gy','gz'}, dimensions={0} | all-to-all | bytes 524288 | tf_op jit(solution)/shard_map/all_to_all | solution.py:536
  20.3 9.6 %splat_points.1 = (f32[2,7,144,128]{3,2,1,0:T(8,128)S(1)}, f32[2,7,8,128]{3,2,1,0:T(8,128)S(1)}, f32[2,7,8,128]{3,2,1,0:T(8,128)S(1)}, f32[2,8,8,128]{3,2,1,0:T(8,128)S(1)}) custom-call(f32[4,8,16,128]{3,2,1,0:T(8,128)S(1)} %bitcast.7), custom_call_target="tpu_custom_call" | custom-call | tf_op jit(solution)/shard_map/splat_points/pallas_call | solution.py:548
  29.9 3.0 %collective-permute-start = (f32[2,7,8,128]{3,2,1,0:T(8,128)S(1)}, f32[2,7,8,128]{3,2,1,0:T(8,128)S(1)}, u32[]{:S(2)}, u32[]{:S(2)}) collective-permute-start(f32[2,7,8,128]{3,2,1,0:T(8,128)S(1)} %get-tuple-element.9), channel_id=1, source_target_pairs={{0,1},{1,2},{2,3},{4,5},{5,6},{6,7},{8,9},{9,10},{10,11},{12,13},{... | collective-permute-start | bytes 172040 | tf_op jit(solution)/shard_map/ppermute | solution.py:575
  32.9 1.5 %collective-permute-start.1 = (f32[2,7,8,128]{3,2,1,0:T(8,128)S(1)}, f32[2,7,8,128]{3,2,1,0:T(8,128)S(1)}, u32[]{:S(2)}, u32[]{:S(2)}) collective-permute-start(f32[2,7,8,128]{3,2,1,0:T(8,128)S(1)} %get-tuple-element.10), channel_id=1, source_target_pairs={{1,0},{2,1},{3,2},{5,4},{6,5},{7,6},{9,8},{10,9},{11,10},{13,12},{... | collective-permute-start | bytes 172040 | tf_op jit(solution)/shard_map/ppermute | solution.py:576
  34.4 0.3 collective-permute-done.from_low_ref
  34.7 4.3 %collective-permute-done.1.from_high_ref = f32[2,7,8,128]{3,2,1,0:T(8,128)S(1)} collective-permute-done((f32[2,7,8,128]{3,2,1,0:T(8,128)S(1)}, f32[2,7,8,128]{3,2,1,0:T(8,128)S(1)}, u32[]{:S(2)}, u32[]{:S(2)}) %collective-permute-start.1) | collective-permute-done | bytes 57376 | tf_op jit(solution)/shard_map/ppermute | solution.py:576
  39.0 5.4 %solve_and_read.1 = (f32[16,16,128]{2,1,0:T(8,128)}, f32[32,32]{1,0:T(8,128)S(1)}) custom-call(f32[2,7,144,128]{3,2,1,0:T(8,128)S(1)} %get-tuple-element.8.fields_ref, f32[2,7,8,128]{3,2,1,0:T(8,128)S(1)} %collective-permute-done.from_low_ref, f32[2,7,8,128]{3,2,1,0:T(8,128)S(1)} %collective-permute-done.1.from_high_ref, ...), custom_call_target="tpu_custom_call" | custom-call | tf_op jit(solution)/shard_map/solve_and_read/pallas_call | solution.py:579
  44.4 9.2 %all_to_all.11 = f32[1,32,32]{2,0,1:T(1,128)S(1)} all-to-all(f32[1,32,32]{2,0,1:T(1,128)S(1)} %bitcast.8), channel_id=1, replica_groups=mesh['gx'=4,'gy'=2,'gz'=4] {'gx','gy','gz'}, dimensions={1} | all-to-all | bytes 8192 | tf_op jit(solution)/shard_map/all_to_all | solution.py:606
  53.6 0.6 %copy.8 = f32[1,32,32]{2,1,0:T(8,128)} copy(f32[1,32,32]{2,1,0:T(8,128)S(1)} %bitcast.10) | data formatting | bytes 8192
Async XLA Ops:
  29.9 4.8 %collective-permute-start = (f32[2,7,8,128]{3,2,1,0:T(8,128)S(1)}, f32[2,7,8,128]{3,2,1,0:T(8,128)S(1)}, u32[]{:S(2)}, u32[]{:S(2)}) collective-permute-start(f32[2,7,8,128]{3,2,1,0:T(8,128)S(1)} %get-tuple-element.9), channel_id=1, source_target_pairs={{0,1},{1,2},{2,3},{4,5},{5,6},{6,7},{8,9},{9,10},{10,11},{12,13},{... | collective-permute-start | bytes 172040 | tf_op jit(solution)/shard_map/ppermute | solution.py:575
  32.9 6.1 %collective-permute-start.1 = (f32[2,7,8,128]{3,2,1,0:T(8,128)S(1)}, f32[2,7,8,128]{3,2,1,0:T(8,128)S(1)}, u32[]{:S(2)}, u32[]{:S(2)}) collective-permute-start(f32[2,7,8,128]{3,2,1,0:T(8,128)S(1)} %get-tuple-element.10), channel_id=1, source_target_pairs={{1,0},{2,1},{3,2},{5,4},{6,5},{7,6},{9,8},{10,9},{11,10},{13,12},{... | collective-permute-start | bytes 172040 | tf_op jit(solution)/shard_map/ppermute | solution.py:576

commit v7 on v6

--- a/solution.py
+++ b/solution.py
@@ -27,6 +27,7 @@
 CENTER = tuple(range(XO - 1, XO + CX + 2))
 LOWER = tuple(range(0, XO + 2))
 UPPER = tuple(range(XO + CX - 1, XO + CX + REACH + 1))
+PLAIN = {0: CENTER[1:-1], -1: LOWER[:-1], 1: UPPER[1:]}
 FIRST_TILE, END_TILE = XO // XPT, (XO + CX) // XPT + 1
 WINDOW_LOW = YO - REACH
 WINDOW_HIGH = YO + CY - 1
@@ -142,7 +143,7 @@
 
 def splat_kernel(
     shape, recv_ref, fields_ref, up_ref, down_ref, own_ref,
-    points, left_ref, right_ref, hx_ref, near, beside, slope,
+    points, left_ref, right_ref, hx_ref, near, beside, slope, top_x, top_y, top_sum,
 ):
     gx, gy, gz = shape
     mx, my, mz = lax.axis_index("gx"), lax.axis_index("gy"), lax.axis_index("gz")
@@ -185,29 +186,30 @@
     z_limit = jnp.where(mz == gz - 1, CZ, CZ + 1).astype(f32)
     z_row = row_iota(CZ)
     own_row = row_iota(24) + float(8 - YO)
-    point_lane = lax.broadcasted_iota(jnp.int32, (128, 128), 1)
-
-    def multiply(begin, count, b, e, high, planes):
-        size = 3 * count
-        both = dot_nn(left_ref[begin : begin + 2 * size, :], right_ref[b, 0])
-        got = both[:size] + both[size:]
-        got = got + dot_nn(left_ref[begin : begin + size, :], right_ref[b, 1])
+
+    def multiply(begin, lists, b, e, high):
+        counts = [-(-len(planes) * high // 16) * 16 for planes in lists]
+        size = sum(counts)
+        wide = dot_nn(left_ref[begin : begin + size, :], right_ref[b])
+        got = wide[:, :CZ] + wide[:, CZ:]
+        got = got + dot_nn(left_ref[begin + size : begin + 2 * size, :], right_ref[b, :, 0:CZ])
+        at = 0
         for c in range(3):
-            for i, plane in enumerate(planes):
-                value = got[c * count + i * high : c * count + i * high + high]
+            for i, plane in enumerate(lists[c]):
+                value = got[at + i * high : at + i * high + high]
                 if e == 0:
                     add(near, (c, plane), value)
                 else:
                     add(beside, (e - 1, c, plane), value)
-
+            at += counts[c]
         if single and e == 0:
-            for t in sorted({plane // XPT for plane in planes}):
+            for t in sorted({plane // XPT for plane in lists[0]}):
                 unfinished[t] -= 1
                 if unfinished[t] == 0:
                     finish(t)
 
-    row8 = lax.broadcasted_iota(jnp.int32, (8, 2 * 128), 0)
-    zero = jnp.zeros((8, 2 * 128), f32)
+    row8 = lax.broadcasted_iota(jnp.int32, (8, 128), 0)
+    zero = jnp.zeros((8, 128), f32)
 
     def finish(t):
         turned = []
@@ -215,7 +217,7 @@
             pieces = []
             for plane in range(XPT * t, XPT * t + XPT):
                 if plane > UPPER[-1]:
-                    pieces.append(jnp.zeros((YS, 2 * 128), f32))
+                    pieces.append(jnp.zeros((YS, 128), f32))
                     continue
                 parts = [zero] + [near[c, plane, 8 * i : 8 * i + 8, :] for i in range(3)]
                 if others:
@@ -230,37 +232,49 @@
                     parts[1] = parts[1] + jnp.where(row8 < 4, moved, 0.0)
                     parts[3] = parts[3] + high_part
                 pieces.extend(parts)
-            stacked = jnp.concatenate(pieces, axis=0)
-            turned.append(stacked[:, :CZ].T)
-            above = stacked[:, CZ:]
-            n, at = divmod(3 * t + c, 128 // GROUPS)
-            if at:
-                above = pltpu.roll(above, GROUPS * at, 1)
-            if tops[n] is not None:
-                above = jnp.where(point_lane // GROUPS == at, above, tops[n])
-            tops[n] = above
+            turned.append(jnp.concatenate(pieces, axis=0).T)
         fields_ref[0, t, ZO : ZO + CZ, :] = turned[0]
         slope[t, ZO + 8 : ZO + 8 + CZ, :] = turned[1]
         fields_ref[1, t, ZO : ZO + CZ, :] = turned[2]
 
     def finish_all():
-        zero = jnp.zeros((8, 128), f32)
-        sums = [jnp.sum(top.T.reshape(-1, GROUPS, 128), axis=1, keepdims=True) for top in tops]
+        planes = XPT * XTILES
+        got = dot_nt(top_x[...], top_y[0])
+        got = got[:64] + got[64:] + dot_nt(top_x[0:64, :], top_y[1])
+        by_x, by_slope = got[:32], got[32:]
+        sums = (by_slope + pltpu.roll(by_x, 128 - YS, 1), pltpu.roll(by_x, 128 - 2 * YS, 1))
+        sums += (pltpu.roll(by_x, 128 - 3 * YS, 1),)
+        above = []
+        for c in range(3):
+            if single:
+                top_sum[c] = sums[c]
+            else:
+                top_sum[c] = jnp.where(step == 0, 0.0, top_sum[c]) + sums[c]
+            line = None
+            for i in range(XPT):
+                value = top_sum[c, pl.ds(i, 32 // XPT, stride=XPT), :]
+                if i:
+                    value = pltpu.roll(value, YS * i, 1)
+                    value = jnp.where(row_lane // YS == i, value, line)
+                line = value
+            above.append(line)
+        return above
+
+    def place_all(above):
         for t in range(XTILES):
-            at = [divmod(3 * t + c, 128 // GROUPS) for c in range(3)]
-            above = [sums[n][i] for n, i in at]
-            below = jnp.concatenate([above[1], jnp.zeros((7, 128), f32)], axis=0)
+            first_of = [above[c][t : t + 1, :] for c in range(3)]
+            rest = jnp.zeros((7, 128), f32)
             slope[t, 0 : ZO + 8, :] = jnp.zeros((ZO + 8, 128), f32)
-            slope[t, ZO + 8 + CZ : ZO + 16 + CZ, :] = below
+            slope[t, ZO + 8 + CZ : ZO + 16 + CZ, :] = jnp.concatenate([first_of[1], rest], axis=0)
             slope[t, ZO + 16 + CZ : ROWS + 16, :] = zero
             for c in range(2):
                 fields_ref[c, t, 0:ZO, :] = zero
                 fields_ref[c, t, ZO + CZ : ROWS, :] = jnp.concatenate(
-                    [above[2 * c], jnp.zeros((7, 128), f32)], axis=0
+                    [first_of[2 * c], rest], axis=0
                 )
             fields_ref[0, t] += slope[t, 9 : ROWS + 9, :] - slope[t, 7 : ROWS + 7, :]
 
-    tops = [None] * -(-3 * XTILES * GROUPS // 128)
+    row_lane = lax.broadcasted_iota(jnp.int32, (32 // XPT, 128), 1)
     unfinished = [
         sum(
             plane // XPT == t and (i == 0 or planes[i - 1] // XPT != t)
@@ -276,12 +290,13 @@
             y_limit = jnp.where(my == gy - 1, CY, CY + 1).astype(f32)
             y_row = own_row
         else:
-            above = my == 0 if others == 1 else jnp.bool_(e == 2)
+            above_me = my == 0 if others == 1 else jnp.bool_(e == 2)
             y_limit = jnp.where(
-                jnp.logical_and(above, my + 1 == gy - 1), CY, CY + 1
+                jnp.logical_and(above_me, my + 1 == gy - 1), CY, CY + 1
             ).astype(f32)
-            first = jnp.where(above, WINDOW_HIGH - YO - CY, WINDOW_LOW - YO + CY)
+            first = jnp.where(above_me, WINDOW_HIGH - YO - CY, WINDOW_LOW - YO + CY)
             y_row = row_iota(8) + first.astype(f32)
+            y_shift = jnp.where(above_me, CY, -CY).astype(f32)
         high = y_row.shape[0]
         for o, shift, planes in ((1, -1, LOWER), (2, 1, UPPER), (0, 0, CENTER)):
             b = e * 3 + o
@@ -297,9 +312,6 @@
                 hx_ref[b, 1, n] = hat_slope(at, cell_x, low_x, high_x)
             cell_z, off_z = points[place, :, row + 1, :], points[b, :, 6, :]
             top = jnp.where((cell_z + 1.0 == float(CZ)) & (cell_z + 1.0 < z_limit), off_z, 0.0)
-            top_columns = jnp.concatenate([top, jnp.zeros((128 - GROUPS, 128), f32)], axis=0).T
-            top_high = top_columns.astype(bf16).astype(f32)
-            top_low = top_columns - top_high
             y_parts = []
             for g in range(GROUPS):
                 main = points[b, g]
@@ -308,24 +320,43 @@
                 off_y, off_z = main[5:6], main[6:7]
                 at = slice(128 * g, 128 * g + 128)
                 hz_high, hz_low = split(hat(z_row, cell_z, 1.0 - off_z, off_z).T)
-                right_ref[b, 0, at, 0:CZ] = hz_high
-                right_ref[b, 1, at, 0:CZ] = hz_low
-                right_ref[b, 0, at, CZ : CZ + 128] = jnp.where(point_lane == g, top_high, 0.0).astype(bf16)
-                right_ref[b, 1, at, CZ : CZ + 128] = jnp.where(point_lane == g, top_low, 0.0).astype(bf16)
+                right_ref[b, at, 0:CZ] = hz_high
+                right_ref[b, at, CZ : 2 * CZ] = hz_low
                 high_y = jnp.where(cell_y + 1.0 < y_limit, off_y, 0.0)
                 hy = hat(y_row, cell_y, 1.0 - off_y, high_y)
                 dy = hat_slope(y_row, cell_y, 1.0 - off_y, high_y)
                 y_parts.append((main[0:1] * hy, main[1:2] * dy, main[2:3] * hy, main[3:4] * hy))
+                if e == 0:
+                    wide_parts = [jnp.concatenate([zero, part], axis=0) for part in y_parts[-1]]
+                else:
+                    wide_row = row_iota(YS) - (y_shift + float(YO))
+                    hy = hat(wide_row, cell_y, 1.0 - off_y, high_y)
+                    dy = hat_slope(wide_row, cell_y, 1.0 - off_y, high_y)
+                    wide_parts = [main[0:1] * hy, main[1:2] * dy, main[2:3] * hy, main[3:4] * hy]
+                at = slice(span * b + 128 * g, span * b + 128 * g + 128)
+                high_part, low_part = split(jnp.concatenate(wide_parts, axis=0) * top[g : g + 1])
+                top_y[0, :, at] = high_part
+                top_y[1, :, at] = low_part
+                for n in range(2):
+                    rows = [jnp.zeros((planes[0], 128), f32)] if planes[0] else []
+                    rows.append(hx_ref[b, n, 0 : len(planes), g, :])
+                    rows.append(jnp.zeros((32 - planes[-1] - 1, 128), f32))
+                    high_part, low_part = split(jnp.concatenate(rows, axis=0))
+                    top_x[32 * n : 32 * n + 32, at] = high_part
+                    top_x[64 + 32 * n : 96 + 32 * n, at] = low_part
             size = 4 if e == 0 else 12
             for start in range(0, len(planes), size):
-                block = range(start, min(start + size, len(planes)))
-                count = -(-len(block) * high // 16) * 16
+                block = planes[start : start + size]
+                lists = [block] + 2 * [tuple(p for p in block if p in PLAIN[shift])]
+                counts = [-(-len(each) * high // 16) * 16 for each in lists]
                 for c in range(3):
+                    begin = row_at + sum(counts[:c])
                     for g in range(GROUPS):
                         part_x0, part_y1, part_z, part_w = y_parts[g]
                         at = slice(128 * g, 128 * g + 128)
                         rows = []
-                        for n in block:
+                        for plane in lists[c]:
+                            n = plane - planes[0]
                             hx = hx_ref[b, 0, n, g : g + 1, :]
                             if c == 0:
                                 dx = hx_ref[b, 1, n, g : g + 1, :]
@@ -333,26 +364,24 @@
                             else:
                                 rows.append(hx * (part_z if c == 1 else part_w))
                         main_part, rest = split(stack_rows(rows, 16))
-                        begin = row_at + c * count
-                        left_ref[begin : begin + count, at] = main_part
-                        begin = begin + 3 * count
-                        left_ref[begin : begin + count, at] = rest
+                        left_ref[begin : begin + counts[c], at] = main_part
+                        after = begin + sum(counts)
+                        left_ref[after : after + counts[c], at] = rest
                 if waiting is not None:
                     waiting()
-                waiting = functools.partial(
-                    multiply, row_at, count, b, e, high, [planes[n] for n in block]
-                )
-                row_at += 6 * count
+                waiting = functools.partial(multiply, row_at, lists, b, e, high)
+                row_at += 2 * sum(counts)
     waiting()
 
+    above = finish_all()
     if not single:
         @pl.when(step == pl.num_programs(0) - 1)
         def _():
             for t in range(XTILES):
                 finish(t)
-            finish_all()
+            place_all(above)
     else:
-        finish_all()
+        place_all(above)
     for c in range(2):
         up_ref[c] = fields_ref[c, :, UP_AT : UP_AT + HALO, :]
         down_ref[c] = fields_ref[c, :, DOWN_AT : DOWN_AT + HALO, :]
@@ -562,11 +591,14 @@
         scratch_shapes=[
             pltpu.VMEM((rows // 2, GROUPS, 8, 128), f32),
             pltpu.VMEM((lines, 128 * GROUPS), bf16),
-            pltpu.VMEM((bricks, 2, 128 * GROUPS, 2 * 128), bf16),
+            pltpu.VMEM((bricks, 128 * GROUPS, 2 * CZ), bf16),
             pltpu.VMEM((bricks, 2, len(CENTER), GROUPS, 128), f32),
-            pltpu.VMEM((3, XPT * XTILES, 24, 2 * 128), f32),
-            pltpu.VMEM((max(others, 1), 3, XPT * XTILES, 8, 2 * 128), f32),
+            pltpu.VMEM((3, XPT * XTILES, 24, 128), f32),
+            pltpu.VMEM((max(others, 1), 3, XPT * XTILES, 8, 128), f32),
             pltpu.VMEM((XTILES, ROWS + 16, 128), f32),
+            pltpu.VMEM((4 * 32, bricks * 128 * GROUPS), bf16),
+            pltpu.VMEM((2, 4 * YS, bricks * 128 * GROUPS), bf16),
+            pltpu.VMEM((3, 32, 128), f32),
         ],
         compiler_params=pltpu.CompilerParams(vmem_limit_bytes=36 * MIB),
         name="splat_points",

time: 54.5 us -> 55.8 us (1.024)
  Pallas kernels: 17.2 us -> 18.5 us
    pallas_call x1, Pallas kernels: 9.62 us -> 11 us  [on_device(): pl.pallas_call(functools.partial(splat_kernel, shape), grid=(steps,), out...]
where the time goes in v7:
time: 55.8 us; the launch traced here: 55.6 us
  blocking collectives  26.7 us (48%)
  Pallas kernels  18.5 us (33%)
  waiting for transfers between devices  4.59 us (8%)
  starting transfers between devices  4.48 us (8%)
  between operations  0.66 us (1%)
  local copies, waits for them, and re-layouts  0.61 us (1%)
    all_to_all x1, blocking collectives, on_device(): lax.all_to_all(outgoing, AXES, split_axis=0, concat_axis=0, tiled=True)  17.5 us
    pallas_call x1, Pallas kernels, on_device(): pl.pallas_call(functools.partial(splat_kernel, shape), grid=(steps,), out...  11 us
    all_to_all x1, blocking collectives, on_device(): lax.all_to_all(values.reshape(1, sources, slots), AXES, split_axis=1, con...  9.17 us
    pallas_call x1, Pallas kernels, on_device(): pl.pallas_call(functools.partial(solve_kernel, shape), out_shape=(jax.Sha...  5.42 us
    ppermute x1, waiting for transfers between devices, on_device(): from_high = lax.ppermute(down, 'gz', [(i + 1, i) for i in range(gz - 1)])  4.26 us
    ppermute x1, starting transfers between devices, on_device(): from_low = lax.ppermute(up, 'gz', [(i, i + 1) for i in range(gz - 1)])  3.01 us
    pallas_call x1, Pallas kernels, on_device(): pl.pallas_call(functools.partial(pack_kernel, shape), out_shape=jax.Shape...  2.15 us
    ppermute x1, starting transfers between devices, on_device(): from_high = lax.ppermute(down, 'gz', [(i + 1, i) for i in range(gz - 1)])  1.47 us
  transfers between devices with their start and end apart: 2, of which 2 were waited for; matrix products, arithmetic and copies ran while one was open for 0% of the time, Pallas kernels for 0%

profile of v7, /device:TPU:0, one launch (start us, length us, event | category | flops | bytes accessed | tf_op | source)
XLA Modules:
  0.0 55.6 jit_solution(10334406992764426115)
XLA Ops:
  0.6 2.2 %pack_points.1 = f32[32,16,128]{2,1,0:T(8,128)} custom-call(f32[1,7,32,32]{3,2,1,0:T(8,128)} %bitcast.9, s32[1,3,32,32]{3,2,1,0:T(8,128)} %bitcast.11, s32[1,32]{1,0:T(1,128)} %counts_ref.1), custom_call_target="tpu_custom_call" | custom-call | tf_op jit(solution)/shard_map/pack_points/pallas_call | solution.py:548
  2.8 17.5 %all_to_all.10 = f32[32,16,128]{2,1,0:T(8,128)S(1)} all-to-all(f32[32,16,128]{2,1,0:T(8,128)} %pack_points.1), channel_id=1, replica_groups=mesh['gx'=4,'gy'=2,'gz'=4] {'gx','gy','gz'}, dimensions={0} | all-to-all | bytes 524288 | tf_op jit(solution)/shard_map/all_to_all | solution.py:565
  20.3 11.0 %splat_points.1 = (f32[2,7,144,128]{3,2,1,0:T(8,128)S(1)}, f32[2,7,8,128]{3,2,1,0:T(8,128)S(1)}, f32[2,7,8,128]{3,2,1,0:T(8,128)S(1)}, f32[2,8,8,128]{3,2,1,0:T(8,128)S(1)}) custom-call(f32[4,8,16,128]{3,2,1,0:T(8,128)S(1)} %bitcast.7), custom_call_target="tpu_custom_call" | custom-call | tf_op jit(solution)/shard_map/splat_points/pallas_call | solution.py:577
  31.3 3.0 %collective-permute-start = (f32[2,7,8,128]{3,2,1,0:T(8,128)S(1)}, f32[2,7,8,128]{3,2,1,0:T(8,128)S(1)}, u32[]{:S(2)}, u32[]{:S(2)}) collective-permute-start(f32[2,7,8,128]{3,2,1,0:T(8,128)S(1)} %get-tuple-element.9), channel_id=1, source_target_pairs={{0,1},{1,2},{2,3},{4,5},{5,6},{6,7},{8,9},{9,10},{10,11},{12,13},{... | collective-permute-start | bytes 172040 | tf_op jit(solution)/shard_map/ppermute | solution.py:607
  34.3 1.5 %collective-permute-start.1 = (f32[2,7,8,128]{3,2,1,0:T(8,128)S(1)}, f32[2,7,8,128]{3,2,1,0:T(8,128)S(1)}, u32[]{:S(2)}, u32[]{:S(2)}) collective-permute-start(f32[2,7,8,128]{3,2,1,0:T(8,128)S(1)} %get-tuple-element.10), channel_id=1, source_target_pairs={{1,0},{2,1},{3,2},{5,4},{6,5},{7,6},{9,8},{10,9},{11,10},{13,12},{... | collective-permute-start | bytes 172040 | tf_op jit(solution)/shard_map/ppermute | solution.py:608
  35.8 0.3 collective-permute-done.from_low_ref
  36.1 4.3 %collective-permute-done.1.from_high_ref = f32[2,7,8,128]{3,2,1,0:T(8,128)S(1)} collective-permute-done((f32[2,7,8,128]{3,2,1,0:T(8,128)S(1)}, f32[2,7,8,128]{3,2,1,0:T(8,128)S(1)}, u32[]{:S(2)}, u32[]{:S(2)}) %collective-permute-start.1) | collective-permute-done | bytes 57376 | tf_op jit(solution)/shard_map/ppermute | solution.py:608
  40.4 5.4 %solve_and_read.1 = (f32[16,16,128]{2,1,0:T(8,128)}, f32[32,32]{1,0:T(8,128)S(1)}) custom-call(f32[2,7,144,128]{3,2,1,0:T(8,128)S(1)} %get-tuple-element.8.fields_ref, f32[2,7,8,128]{3,2,1,0:T(8,128)S(1)} %collective-permute-done.from_low_ref, f32[2,7,8,128]{3,2,1,0:T(8,128)S(1)} %collective-permute-done.1.from_high_ref, ...), custom_call_target="tpu_custom_call" | custom-call | tf_op jit(solution)/shard_map/solve_and_read/pallas_call | solution.py:611
  45.8 9.2 %all_to_all.11 = f32[1,32,32]{2,0,1:T(1,128)S(1)} all-to-all(f32[1,32,32]{2,0,1:T(1,128)S(1)} %bitcast.8), channel_id=1, replica_groups=mesh['gx'=4,'gy'=2,'gz'=4] {'gx','gy','gz'}, dimensions={1} | all-to-all | bytes 8192 | tf_op jit(solution)/shard_map/all_to_all | solution.py:638
  54.9 0.6 %copy.8 = f32[1,32,32]{2,1,0:T(8,128)} copy(f32[1,32,32]{2,1,0:T(8,128)S(1)} %bitcast.10) | data formatting | bytes 8192
Async XLA Ops:
  31.3 4.8 %collective-permute-start = (f32[2,7,8,128]{3,2,1,0:T(8,128)S(1)}, f32[2,7,8,128]{3,2,1,0:T(8,128)S(1)}, u32[]{:S(2)}, u32[]{:S(2)}) collective-permute-start(f32[2,7,8,128]{3,2,1,0:T(8,128)S(1)} %get-tuple-element.9), channel_id=1, source_target_pairs={{0,1},{1,2},{2,3},{4,5},{5,6},{6,7},{8,9},{9,10},{10,11},{12,13},{... | collective-permute-start | bytes 172040 | tf_op jit(solution)/shard_map/ppermute | solution.py:607
  34.3 6.1 %collective-permute-start.1 = (f32[2,7,8,128]{3,2,1,0:T(8,128)S(1)}, f32[2,7,8,128]{3,2,1,0:T(8,128)S(1)}, u32[]{:S(2)}, u32[]{:S(2)}) collective-permute-start(f32[2,7,8,128]{3,2,1,0:T(8,128)S(1)} %get-tuple-element.10), channel_id=1, source_target_pairs={{1,0},{2,1},{3,2},{5,4},{6,5},{7,6},{9,8},{10,9},{11,10},{13,12},{... | collective-permute-start | bytes 172040 | tf_op jit(solution)/shard_map/ppermute | solution.py:608

commit v8 on v6

--- a/solution.py
+++ b/solution.py
@@ -27,6 +27,7 @@
 CENTER = tuple(range(XO - 1, XO + CX + 2))
 LOWER = tuple(range(0, XO + 2))
 UPPER = tuple(range(XO + CX - 1, XO + CX + REACH + 1))
+PLAIN = {0: CENTER[1:-1], -1: LOWER[:-1], 1: UPPER[1:]}
 FIRST_TILE, END_TILE = XO // XPT, (XO + CX) // XPT + 1
 WINDOW_LOW = YO - REACH
 WINDOW_HIGH = YO + CY - 1
@@ -129,6 +130,23 @@
     return rising - jnp.where(away == 1.0, low, jnp.where(away == 2.0, high, 0.0))
 
 
+def split_hat(rows, cell, offset):
+    spread = (16, 128)
+    fill = rows.shape[0] // 16
+    ends = []
+    for value in (1.0 - offset, offset):
+        ends.extend(split(jnp.broadcast_to(value, spread)))
+    low_high, low_low, high_high, high_low = (jnp.concatenate([v] * fill, axis=0) for v in ends)
+    cells = jnp.broadcast_to(cell, spread).astype(bf16)
+    away = rows - jnp.concatenate([cells] * fill, axis=0)
+    here, above = away == 0.0, away == 1.0
+    zero = jnp.zeros(rows.shape, bf16)
+    return (
+        jnp.where(here, low_high, jnp.where(above, high_high, zero)),
+        jnp.where(here, low_low, jnp.where(above, high_low, zero)),
+    )
+
+
 def row_iota(rows):
     return lax.broadcasted_iota(jnp.int32, (rows, 128), 0).astype(f32)
 
@@ -183,25 +201,27 @@
     own_ref[1] = points[bricks]
 
     z_limit = jnp.where(mz == gz - 1, CZ, CZ + 1).astype(f32)
-    z_row = row_iota(CZ)
+    z_row = row_iota(CZ).astype(bf16)
     own_row = row_iota(24) + float(8 - YO)
     point_lane = lax.broadcasted_iota(jnp.int32, (128, 128), 1)
 
-    def multiply(begin, count, b, e, high, planes):
-        size = 3 * count
+    def multiply(begin, lists, b, e, high):
+        counts = [-(-len(planes) * high // 16) * 16 for planes in lists]
+        size = sum(counts)
         both = dot_nn(left_ref[begin : begin + 2 * size, :], right_ref[b, 0])
         got = both[:size] + both[size:]
         got = got + dot_nn(left_ref[begin : begin + size, :], right_ref[b, 1])
+        at = 0
         for c in range(3):
-            for i, plane in enumerate(planes):
-                value = got[c * count + i * high : c * count + i * high + high]
+            for i, plane in enumerate(lists[c]):
+                value = got[at + i * high : at + i * high + high]
                 if e == 0:
                     add(near, (c, plane), value)
                 else:
                     add(beside, (e - 1, c, plane), value)
-
+            at += counts[c]
         if single and e == 0:
-            for t in sorted({plane // XPT for plane in planes}):
+            for t in sorted({plane // XPT for plane in lists[0]}):
                 unfinished[t] -= 1
                 if unfinished[t] == 0:
                     finish(t)
@@ -291,10 +311,13 @@
             off_x = points[b, :, 4, :]
             low_x = 1.0 - off_x
             high_x = jnp.where(cell_x + 1.0 < x_limit, off_x, 0.0)
-            for n, plane in enumerate(planes):
-                at = float(plane - XO - CX * shift)
-                hx_ref[b, 0, n] = hat(at, cell_x, low_x, high_x)
-                hx_ref[b, 1, n] = hat_slope(at, cell_x, low_x, high_x)
+            first_x = planes[0] - XO - CX * shift
+            hats = [
+                hat(float(first_x + n - 1), cell_x, low_x, high_x) for n in range(len(planes) + 2)
+            ]
+            for n in range(len(planes)):
+                hx_ref[b, 0, n] = hats[n + 1]
+                hx_ref[b, 1, n] = hats[n + 2] - hats[n]
             cell_z, off_z = points[place, :, row + 1, :], points[b, :, 6, :]
             top = jnp.where((cell_z + 1.0 == float(CZ)) & (cell_z + 1.0 < z_limit), off_z, 0.0)
             top_columns = jnp.concatenate([top, jnp.zeros((128 - GROUPS, 128), f32)], axis=0).T
@@ -307,9 +330,9 @@
                 cell_y, cell_z = more[row : row + 1], more[row + 1 : row + 2]
                 off_y, off_z = main[5:6], main[6:7]
                 at = slice(128 * g, 128 * g + 128)
-                hz_high, hz_low = split(hat(z_row, cell_z, 1.0 - off_z, off_z).T)
-                right_ref[b, 0, at, 0:CZ] = hz_high
-                right_ref[b, 1, at, 0:CZ] = hz_low
+                hz_high, hz_low = split_hat(z_row, cell_z, off_z)
+                right_ref[b, 0, at, 0:CZ] = hz_high.T
+                right_ref[b, 1, at, 0:CZ] = hz_low.T
                 right_ref[b, 0, at, CZ : CZ + 128] = jnp.where(point_lane == g, top_high, 0.0).astype(bf16)
                 right_ref[b, 1, at, CZ : CZ + 128] = jnp.where(point_lane == g, top_low, 0.0).astype(bf16)
                 high_y = jnp.where(cell_y + 1.0 < y_limit, off_y, 0.0)
@@ -318,14 +341,17 @@
                 y_parts.append((main[0:1] * hy, main[1:2] * dy, main[2:3] * hy, main[3:4] * hy))
             size = 4 if e == 0 else 12
             for start in range(0, len(planes), size):
-                block = range(start, min(start + size, len(planes)))
-                count = -(-len(block) * high // 16) * 16
+                block = planes[start : start + size]
+                lists = [block] + 2 * [tuple(p for p in block if p in PLAIN[shift])]
+                counts = [-(-len(each) * high // 16) * 16 for each in lists]
                 for c in range(3):
+                    begin = row_at + sum(counts[:c])
                     for g in range(GROUPS):
                         part_x0, part_y1, part_z, part_w = y_parts[g]
                         at = slice(128 * g, 128 * g + 128)
                         rows = []
-                        for n in block:
+                        for plane in lists[c]:
+                            n = plane - planes[0]
                             hx = hx_ref[b, 0, n, g : g + 1, :]
                             if c == 0:
                                 dx = hx_ref[b, 1, n, g : g + 1, :]
@@ -333,16 +359,13 @@
                             else:
                                 rows.append(hx * (part_z if c == 1 else part_w))
                         main_part, rest = split(stack_rows(rows, 16))
-                        begin = row_at + c * count
-                        left_ref[begin : begin + count, at] = main_part
-                        begin = begin + 3 * count
-                        left_ref[begin : begin + count, at] = rest
+                        left_ref[begin : begin + counts[c], at] = main_part
+                        after = begin + sum(counts)
+                        left_ref[after : after + counts[c], at] = rest
                 if waiting is not None:
                     waiting()
-                waiting = functools.partial(
-                    multiply, row_at, count, b, e, high, [planes[n] for n in block]
-                )
-                row_at += 6 * count
+                waiting = functools.partial(multiply, row_at, lists, b, e, high)
+                row_at += 2 * sum(counts)
     waiting()
 
     if not single:
@@ -370,39 +393,23 @@
     return factors
 
 
-def solve_kernel(
-    shape, fields_ref, from_low_ref, from_high_ref, own_ref,
-    indicator_ref, values_ref,
-    given, low_halo, high_halo, owned, first, second, scaled, inverse, total,
-    hx_ref, high_ref, low_ref, arrivals,
-):
-    gx, gy, gz = shape
-    mx, my, mz = lax.axis_index("gx"), lax.axis_index("gy"), lax.axis_index("gz")
-    copies = [
-        pltpu.make_async_copy(source, target, arrivals.at[i])
-        for i, (source, target) in enumerate(
-            ((own_ref, owned), (fields_ref, given), (from_low_ref, low_halo), (from_high_ref, high_halo))
-        )
-    ]
-    for copy in copies:
-        copy.start()
-    copies[0].wait()
-    groups = owned.shape[1]
+READ_PLANES = range(XPT * FIRST_TILE, XPT * END_TILE)
+
+
+def read_kernel(own_ref, out_ref, hx_ref):
     y_row = row_iota(24) + float(8 - YO)
     blank = jnp.zeros((8, 128), f32)
-    read_planes = range(XPT * FIRST_TILE, XPT * END_TILE)
-
-    def read_operand(chunk):
+    for chunk in range(own_ref.shape[1] // GROUPS):
         span = slice(chunk * GROUPS, chunk * GROUPS + GROUPS)
-        cell_x, off_x = owned[0, span, 7, :], owned[0, span, 4, :]
-        for plane in read_planes:
+        cell_x, off_x = own_ref[0, span, 7, :], own_ref[0, span, 4, :]
+        for plane in READ_PLANES:
             if 0 <= plane - XO <= CX:
                 hx_ref[plane] = hat(float(plane - XO), cell_x, 1.0 - off_x, off_x)
         for g in range(GROUPS):
-            off_y = owned[0, chunk * GROUPS + g, 5:6, :]
-            hy = hat(y_row, owned[1, chunk * GROUPS + g, 0:1, :], 1.0 - off_y, off_y)
+            off_y = own_ref[0, chunk * GROUPS + g, 5:6, :]
+            hy = hat(y_row, own_ref[1, chunk * GROUPS + g, 0:1, :], 1.0 - off_y, off_y)
             at = slice(128 * g, 128 * g + 128)
-            for plane in read_planes:
+            for plane in READ_PLANES:
                 start = YS * (plane - XPT * FIRST_TILE)
                 if 0 <= plane - XO <= CX:
                     rows = jnp.concatenate([blank, hx_ref[plane, g : g + 1, :] * hy], axis=0)
@@ -410,11 +417,27 @@
                 else:
                     high = jnp.zeros((YS, 128), bf16)
                     low = high
-                high_ref[start : start + YS, at] = high
-                low_ref[start : start + YS, at] = low
-
-    read_operand(0)
-    for copy in copies[1:]:
+                out_ref[chunk, 0, start : start + YS, at] = high
+                out_ref[chunk, 1, start : start + YS, at] = low
+
+
+def solve_kernel(
+    shape, fields_ref, from_low_ref, from_high_ref, own_ref, read_ref,
+    indicator_ref, values_ref,
+    given, low_halo, high_halo, owned, first, second, base, inverse, total,
+    operand, arrivals,
+):
+    gx, gy, gz = shape
+    mx, my, mz = lax.axis_index("gx"), lax.axis_index("gy"), lax.axis_index("gz")
+    sources = (fields_ref, from_low_ref, from_high_ref, own_ref, read_ref.at[0])
+    targets = (given, low_halo, high_halo, owned, operand)
+    copies = [
+        pltpu.make_async_copy(source, target, arrivals.at[i])
+        for i, (source, target) in enumerate(zip(sources, targets))
+    ]
+    for copy in copies:
+        copy.start()
+    for copy in copies[:3]:
         copy.wait()
     low_at, high_at = UP_AT - CZ, DOWN_AT + CZ
     for c in range(2):
@@ -426,24 +449,25 @@
     y = lane % YS - YO + my * CY
     inside_y = (y >= 0) & (y < gy * CY)
     zero = jnp.zeros((8, 128), f32)
+    strips = ROWS // 8
     for t in range(XTILES):
         x = lane // YS + (XPT * t - XO) + mx * CX
         inside_xy = inside_y & (x >= 0) & (x < gx * CX)
         for scratch in (first, second):
             scratch[t, 0:8, :] = zero
             scratch[t, ROWS + 8 : ROWS + 16, :] = zero
-        for i in range(ROWS // 8):
+        for i in range(strips):
             at = slice(8 * i, 8 * i + 8)
-            z = row + (8 * i - ZO) + mz * CZ
-            inside = inside_xy & (z >= 0) & (z < gz * CZ)
+            inside = inside_xy
+            if 8 * i < ZO or 8 * i + 8 > ZO + CZ:
+                z = row + (8 * i - ZO) + mz * CZ
+                inside = inside & (z >= 0) & (z < gz * CZ)
             diagonal = 6.0 + base_screen + point_screen * given[1, t, at, :]
             inv = jnp.where(inside, 1.0 / diagonal, 0.0)
             start = given[0, t, at, :] * inv
             inverse[t, at, :] = inv
-            scaled[t, at, :] = start
+            base[t, at, :] = start
             first[t, 8 * i + 8 : 8 * i + 16, :] = start
-            if FIRST_TILE <= t < END_TILE:
-                total[t - FIRST_TILE, at, :] = start
 
     now, later = first, second
     factors = chebyshev_factors()
@@ -451,11 +475,15 @@
     for k, (keep, gain) in enumerate(factors, 1):
         last = k == len(factors)
         begin, end = k // XPT, (XO + CX + REACH - k + XPT) // XPT
-        for i in range(ROWS // 8):
+        if last:
+            begin, end = max(begin, FIRST_TILE), min(end, END_TILE)
+        for i in range(strips):
             at = slice(8 * i, 8 * i + 8)
-            here = {t: now[t, 8 * i + 8 : 8 * i + 16, :] for t in range(XTILES)}
-            ahead_x = {t: pltpu.roll(here[t], YS, 1) for t in range(XTILES)}
-            behind_x = {t: pltpu.roll(here[t], 128 - YS, 1) for t in range(XTILES)}
+            inner = slice(8 * i + 8, 8 * i + 16)
+            reach = range(max(begin - 1, 0), min(end + 1, XTILES))
+            here = {t: now[t, inner, :] for t in reach}
+            ahead_x = {t: pltpu.roll(here[t], YS, 1) for t in reach if t < end}
+            behind_x = {t: pltpu.roll(here[t], 128 - YS, 1) for t in reach if t >= begin}
             for t in range(begin, end):
                 mine = here[t]
                 near = now[t, 8 * i + 7 : 8 * i + 15, :] + now[t, 8 * i + 9 : 8 * i + 17, :]
@@ -467,13 +495,13 @@
                 if t + 1 < XTILES:
                     after = jnp.where(high_part, behind_x[t + 1], after)
                 near = near + before + after
-                left = scaled[t, at, :] - mine + inverse[t, at, :] * near
-                ahead = keep * mine + gain * left
-                if FIRST_TILE <= t < END_TILE:
-                    total[t - FIRST_TILE, at, :] += ahead
-                if not last:
-                    scaled[t, at, :] = left
-                    later[t, 8 * i + 8 : 8 * i + 16, :] = ahead
+                ahead = (1.0 + keep - gain) * mine + gain * (base[t, at, :] + inverse[t, at, :] * near)
+                if k > 1:
+                    ahead = ahead - keep * later[t, inner, :]
+                if last:
+                    total[t - FIRST_TILE, at, :] = ahead
+                else:
+                    later[t, inner, :] = ahead
         now, later = later, now
 
     parts = [split(total[t - FIRST_TILE]) for t in range(FIRST_TILE, END_TILE)]
@@ -481,11 +509,16 @@
     u_low = jnp.concatenate([part[1] for part in parts], axis=1)
     u_both = jnp.concatenate([u_high, u_low], axis=0)
     z_row = row_iota(ROWS) - float(ZO)
+    for copy in copies[3:]:
+        copy.wait()
+    groups = owned.shape[1]
     for chunk in range(groups // GROUPS):
         if chunk > 0:
-            read_operand(chunk)
-        got = dot_nn(u_both, high_ref[...])
-        got = got[:ROWS] + got[ROWS:] + dot_nn(u_high, low_ref[...])
+            copy = pltpu.make_async_copy(read_ref.at[chunk], operand, arrivals.at[4])
+            copy.start()
+            copy.wait()
+        got = dot_nn(u_both, operand[0])
+        got = got[:ROWS] + got[ROWS:] + dot_nn(u_high, operand[1])
         rows = []
         for g in range(GROUPS):
             main = owned[0, chunk * GROUPS + g]
@@ -576,13 +609,26 @@
     from_high = lax.ppermute(down, "gz", [(i + 1, i) for i in range(gz - 1)])
 
     depth = 128 * (END_TILE - FIRST_TILE)
+    read = pl.pallas_call(
+        read_kernel,
+        out_shape=jax.ShapeDtypeStruct((steps, 2, depth, 128 * GROUPS), bf16),
+        in_specs=[whole],
+        out_specs=whole,
+        scratch_shapes=[pltpu.VMEM((XPT * END_TILE, GROUPS, 128), f32)],
+        compiler_params=pltpu.CompilerParams(vmem_limit_bytes=16 * MIB),
+        cost_estimate=pl.CostEstimate(
+            flops=8 * depth * 128 * groups, bytes_accessed=4 * depth * 128 * groups, transcendentals=0
+        ),
+        name="read_operand",
+    )(own)
+
     indicator, values = pl.pallas_call(
         functools.partial(solve_kernel, shape),
         out_shape=(
             jax.ShapeDtypeStruct((CX, CY, CZ), f32),
             jax.ShapeDtypeStruct((sources, slots), f32),
         ),
-        in_specs=[pl.BlockSpec(memory_space=pl.ANY)] * 4,
+        in_specs=[pl.BlockSpec(memory_space=pl.ANY)] * 5,
         out_specs=(whole, whole),
         scratch_shapes=[
             pltpu.VMEM((2, XTILES, ROWS, 128), f32),
@@ -594,14 +640,12 @@
             pltpu.VMEM((XTILES, ROWS, 128), f32),
             pltpu.VMEM((XTILES, ROWS, 128), f32),
             pltpu.VMEM((END_TILE - FIRST_TILE, ROWS, 128), f32),
-            pltpu.VMEM((XPT * END_TILE, GROUPS, 128), f32),
-            pltpu.VMEM((depth, 128 * GROUPS), bf16),
-            pltpu.VMEM((depth, 128 * GROUPS), bf16),
-            pltpu.SemaphoreType.DMA((4,)),
+            pltpu.VMEM((2, depth, 128 * GROUPS), bf16),
+            pltpu.SemaphoreType.DMA((5,)),
         ],
         compiler_params=pltpu.CompilerParams(vmem_limit_bytes=16 * MIB),
         name="solve_and_read",
-    )(fields, from_low, from_high, own)
+    )(fields, from_low, from_high, own, read)
 
     returned = lax.all_to_all(
         values.reshape(1, sources, slots), AXES, split_axis=1, concat_axis=1, tiled=True

time: 54.5 us -> 52.8 us (0.969)
  waiting for transfers between devices: 4.59 us -> 3.75 us
  Pallas kernels: 17.2 us -> 16.4 us
    pallas_call x1, Pallas kernels: 9.62 us -> 8.45 us  [on_device(): pl.pallas_call(functools.partial(splat_kernel, shape), grid=(steps,), out...]
    pallas_call x0 -> x1, Pallas kernels: none -> 0.83 us  [on_device(): pl.pallas_call(read_kernel, out_shape=jax.ShapeDtypeStruct((steps, 2, dep...]
  transfers between devices with their start and end apart: 2 -> 2, of which waited for: 2 -> 1; matrix products, arithmetic and copies ran while one was open for 0% -> 0% of each run, Pallas kernels for 0% -> 2%
where the time goes in v8:
time: 52.8 us; the launch traced here: 52.6 us
  blocking collectives  26.7 us (51%)
  Pallas kernels  16.4 us (31%)
  starting transfers between devices  4.48 us (8%)
  waiting for transfers between devices  3.75 us (7%)
  between operations  0.67 us (1%)
  local copies, waits for them, and re-layouts  0.61 us (1%)
    all_to_all x1, blocking collectives, on_device(): lax.all_to_all(outgoing, AXES, split_axis=0, concat_axis=0, tiled=True)  17.5 us
    all_to_all x1, blocking collectives, on_device(): lax.all_to_all(values.reshape(1, sources, slots), AXES, split_axis=1, con...  9.17 us
    pallas_call x1, Pallas kernels, on_device(): pl.pallas_call(functools.partial(splat_kernel, shape), grid=(steps,), out...  8.45 us
    pallas_call x1, Pallas kernels, on_device(): pl.pallas_call(functools.partial(solve_kernel, shape), out_shape=(jax.Sha...  4.96 us
    ppermute x1, waiting for transfers between devices, on_device(): from_high = lax.ppermute(down, 'gz', [(i + 1, i) for i in range(gz - 1)])  3.75 us
    ppermute x1, starting transfers between devices, on_device(): from_low = lax.ppermute(up, 'gz', [(i, i + 1) for i in range(gz - 1)])  3 us
    pallas_call x1, Pallas kernels, on_device(): pl.pallas_call(functools.partial(pack_kernel, shape), out_shape=jax.Shape...  2.15 us
    ppermute x1, starting transfers between devices, on_device(): from_high = lax.ppermute(down, 'gz', [(i + 1, i) for i in range(gz - 1)])  1.47 us
  transfers between devices with their start and end apart: 2, of which 1 were waited for; matrix products, arithmetic and copies ran while one was open for 0% of the time, Pallas kernels for 2%

profile of v8, /device:TPU:0, one launch (start us, length us, event | category | flops | bytes accessed | tf_op | source)
XLA Modules:
  0.0 52.6 jit_solution(7094485824488662863)
XLA Ops:
  0.6 2.2 %pack_points.1 = f32[32,16,128]{2,1,0:T(8,128)} custom-call(f32[1,7,32,32]{3,2,1,0:T(8,128)} %bitcast.9, s32[1,3,32,32]{3,2,1,0:T(8,128)} %bitcast.11, s32[1,32]{1,0:T(1,128)} %counts_ref.1), custom_call_target="tpu_custom_call" | custom-call | tf_op jit(solution)/shard_map/pack_points/pallas_call | solution.py:552
  2.8 17.5 %all_to_all.10 = f32[32,16,128]{2,1,0:T(8,128)S(1)} all-to-all(f32[32,16,128]{2,1,0:T(8,128)} %pack_points.1), channel_id=1, replica_groups=mesh['gx'=4,'gy'=2,'gz'=4] {'gx','gy','gz'}, dimensions={0} | all-to-all | bytes 524288 | tf_op jit(solution)/shard_map/all_to_all | solution.py:569
  20.3 8.5 %splat_points.1 = (f32[2,7,144,128]{3,2,1,0:T(8,128)S(1)}, f32[2,7,8,128]{3,2,1,0:T(8,128)S(1)}, f32[2,7,8,128]{3,2,1,0:T(8,128)S(1)}, f32[2,8,8,128]{3,2,1,0:T(8,128)S(1)}) custom-call(f32[4,8,16,128]{3,2,1,0:T(8,128)S(1)} %bitcast.7), custom_call_target="tpu_custom_call" | custom-call | tf_op jit(solution)/shard_map/splat_points/pallas_call | solution.py:581
  28.7 3.0 %collective-permute-start = (f32[2,7,8,128]{3,2,1,0:T(8,128)S(1)}, f32[2,7,8,128]{3,2,1,0:T(8,128)S(1)}, u32[]{:S(2)}, u32[]{:S(2)}) collective-permute-start(f32[2,7,8,128]{3,2,1,0:T(8,128)S(1)} %get-tuple-element.9), channel_id=1, source_target_pairs={{0,1},{1,2},{2,3},{4,5},{5,6},{6,7},{8,9},{9,10},{10,11},{12,13},{... | collective-permute-start | bytes 172040 | tf_op jit(solution)/shard_map/ppermute | solution.py:608
  31.8 1.5 %collective-permute-start.1 = (f32[2,7,8,128]{3,2,1,0:T(8,128)S(1)}, f32[2,7,8,128]{3,2,1,0:T(8,128)S(1)}, u32[]{:S(2)}, u32[]{:S(2)}) collective-permute-start(f32[2,7,8,128]{3,2,1,0:T(8,128)S(1)} %get-tuple-element.10), channel_id=1, source_target_pairs={{1,0},{2,1},{3,2},{5,4},{6,5},{7,6},{9,8},{10,9},{11,10},{13,12},{... | collective-permute-start | bytes 172040 | tf_op jit(solution)/shard_map/ppermute | solution.py:609
  33.2 0.8 %read_operand.1.read_ref = bf16[1,2,640,1024]{3,2,1,0:T(8,128)(2,1)S(1)} custom-call(f32[2,8,8,128]{3,2,1,0:T(8,128)S(1)} %get-tuple-element.11.own_ref), custom_call_target="tpu_custom_call" | custom-call | flops 5242880 | bytes 2621440 | tf_op jit(solution)/shard_map/read_operand/pallas_call | solution.py:612
  34.1 0.0 collective-permute-done.from_low_ref
  34.1 3.7 %collective-permute-done.1.from_high_ref = f32[2,7,8,128]{3,2,1,0:T(8,128)S(1)} collective-permute-done((f32[2,7,8,128]{3,2,1,0:T(8,128)S(1)}, f32[2,7,8,128]{3,2,1,0:T(8,128)S(1)}, u32[]{:S(2)}, u32[]{:S(2)}) %collective-permute-start.1) | collective-permute-done | bytes 57376 | tf_op jit(solution)/shard_map/ppermute | solution.py:609
  37.8 5.0 %solve_and_read.1 = (f32[16,16,128]{2,1,0:T(8,128)}, f32[32,32]{1,0:T(8,128)S(1)}) custom-call(f32[2,7,144,128]{3,2,1,0:T(8,128)S(1)} %get-tuple-element.8.fields_ref, f32[2,7,8,128]{3,2,1,0:T(8,128)S(1)} %collective-permute-done.from_low_ref, f32[2,7,8,128]{3,2,1,0:T(8,128)S(1)} %collective-permute-done.1.from_high_ref, ...), custom_call_target="tpu_custom_call" | custom-call | tf_op jit(solution)/shard_map/solve_and_read/pallas_call | solution.py:625
  42.8 9.2 %all_to_all.11 = f32[1,32,32]{2,0,1:T(1,128)S(1)} all-to-all(f32[1,32,32]{2,0,1:T(1,128)S(1)} %bitcast.8), channel_id=1, replica_groups=mesh['gx'=4,'gy'=2,'gz'=4] {'gx','gy','gz'}, dimensions={1} | all-to-all | bytes 8192 | tf_op jit(solution)/shard_map/all_to_all | solution.py:650
  52.0 0.6 %copy.8 = f32[1,32,32]{2,1,0:T(8,128)} copy(f32[1,32,32]{2,1,0:T(8,128)S(1)} %bitcast.10) | data formatting | bytes 8192
Async XLA Ops:
  28.7 5.3 %collective-permute-start = (f32[2,7,8,128]{3,2,1,0:T(8,128)S(1)}, f32[2,7,8,128]{3,2,1,0:T(8,128)S(1)}, u32[]{:S(2)}, u32[]{:S(2)}) collective-permute-start(f32[2,7,8,128]{3,2,1,0:T(8,128)S(1)} %get-tuple-element.9), channel_id=1, source_target_pairs={{0,1},{1,2},{2,3},{4,5},{5,6},{6,7},{8,9},{9,10},{10,11},{12,13},{... | collective-permute-start | bytes 172040 | tf_op jit(solution)/shard_map/ppermute | solution.py:608
  31.8 6.1 %collective-permute-start.1 = (f32[2,7,8,128]{3,2,1,0:T(8,128)S(1)}, f32[2,7,8,128]{3,2,1,0:T(8,128)S(1)}, u32[]{:S(2)}, u32[]{:S(2)}) collective-permute-start(f32[2,7,8,128]{3,2,1,0:T(8,128)S(1)} %get-tuple-element.10), channel_id=1, source_target_pairs={{1,0},{2,1},{3,2},{5,4},{6,5},{7,6},{9,8},{10,9},{11,10},{13,12},{... | collective-permute-start | bytes 172040 | tf_op jit(solution)/shard_map/ppermute | solution.py:609

commit v9 on v8

--- a/solution.py
+++ b/solution.py
@@ -62,8 +62,22 @@
     return bricks + brick // 4, 2 * (brick % 4)
 
 
-def pack_kernel(shape, data_ref, cells_ref, counts_ref, out_ref, main, extra):
+def pack_kernel(
+    shape, data_hbm, cells_hbm, counts_hbm, out_ref,
+    data_ref, cells_ref, counts_ref, main, extra, arrivals,
+):
     gx, gy, gz = shape
+    copies = [
+        pltpu.make_async_copy(source, target, arrivals.at[i])
+        for i, (source, target) in enumerate(
+            ((data_hbm, data_ref), (cells_hbm, cells_ref), (counts_hbm, counts_ref))
+        )
+    ]
+    for copy in copies:
+        copy.start()
+    extra[...] = jnp.zeros_like(extra)
+    for copy in copies:
+        copy.wait()
     slots = data_ref.shape[3]
     sources = gx * gy * gz
     lane = lax.broadcasted_iota(jnp.int32, (sources, slots), 1)
@@ -88,7 +102,6 @@
     for part in range(min(bricks, 4)):
         for c in range(8):
             main[part, :, c, :] = placed(channels[c], part)
-    extra[...] = jnp.zeros_like(extra)
     for b in range(bricks):
         place, row = extra_place(b, bricks)
         for c in range(2):
@@ -164,8 +177,8 @@
 ):
     gx, gy, gz = shape
     mx, my, mz = lax.axis_index("gx"), lax.axis_index("gy"), lax.axis_index("gz")
-    step = pl.program_id(0)
     single = recv_ref.shape[1] * 4 == gx * gy * gz
+    step = 0 if single else pl.program_id(0)
     others = other_count(gy)
     bricks = 3 * (1 + others)
     tiles = recv_ref.shape[2] // 8
@@ -424,25 +437,25 @@
 def solve_kernel(
     shape, fields_ref, from_low_ref, from_high_ref, own_ref, read_ref,
     indicator_ref, values_ref,
-    given, low_halo, high_halo, owned, first, second, base, inverse, total,
-    operand, arrivals,
+    edge, first, second, base, inverse, total, operand, arrivals,
 ):
     gx, gy, gz = shape
     mx, my, mz = lax.axis_index("gx"), lax.axis_index("gy"), lax.axis_index("gz")
-    sources = (fields_ref, from_low_ref, from_high_ref, own_ref, read_ref.at[0])
-    targets = (given, low_halo, high_halo, owned, operand)
-    copies = [
-        pltpu.make_async_copy(source, target, arrivals.at[i])
-        for i, (source, target) in enumerate(zip(sources, targets))
-    ]
-    for copy in copies:
-        copy.start()
-    for copy in copies[:3]:
-        copy.wait()
-    low_at, high_at = UP_AT - CZ, DOWN_AT + CZ
-    for c in range(2):
-        given[c, :, low_at : low_at + HALO, :] += low_halo[c]
-        given[c, :, high_at : high_at + HALO, :] += high_halo[c]
+    copy = pltpu.make_async_copy(read_ref.at[0], operand, arrivals)
+    copy.start()
+    edge[...] = jnp.zeros_like(edge)
+    low_at, high_at = UP_AT - CZ, DOWN_AT + CZ - (ROWS - 16)
+    edge[0, :, :, low_at : low_at + HALO, :] = from_low_ref[...]
+    edge[1, :, :, high_at : high_at + HALO, :] = from_high_ref[...]
+
+    def given(c, t, i):
+        value = fields_ref[c, t, 8 * i : 8 * i + 8, :]
+        if i < 2:
+            value = value + edge[0, c, t, 8 * i : 8 * i + 8, :]
+        from_end = i - (ROWS // 8 - 2)
+        if from_end >= 0:
+            value = value + edge[1, c, t, 8 * from_end : 8 * from_end + 8, :]
+        return value
 
     lane = lax.broadcasted_iota(jnp.int32, (8, 128), 1)
     row = lax.broadcasted_iota(jnp.int32, (8, 128), 0)
@@ -462,9 +475,9 @@
             if 8 * i < ZO or 8 * i + 8 > ZO + CZ:
                 z = row + (8 * i - ZO) + mz * CZ
                 inside = inside & (z >= 0) & (z < gz * CZ)
-            diagonal = 6.0 + base_screen + point_screen * given[1, t, at, :]
+            diagonal = 6.0 + base_screen + point_screen * given(1, t, i)
             inv = jnp.where(inside, 1.0 / diagonal, 0.0)
-            start = given[0, t, at, :] * inv
+            start = given(0, t, i) * inv
             inverse[t, at, :] = inv
             base[t, at, :] = start
             first[t, 8 * i + 8 : 8 * i + 16, :] = start
@@ -509,21 +522,20 @@
     u_low = jnp.concatenate([part[1] for part in parts], axis=1)
     u_both = jnp.concatenate([u_high, u_low], axis=0)
     z_row = row_iota(ROWS) - float(ZO)
-    for copy in copies[3:]:
-        copy.wait()
-    groups = owned.shape[1]
+    copy.wait()
+    groups = own_ref.shape[1]
     for chunk in range(groups // GROUPS):
         if chunk > 0:
-            copy = pltpu.make_async_copy(read_ref.at[chunk], operand, arrivals.at[4])
+            copy = pltpu.make_async_copy(read_ref.at[chunk], operand, arrivals)
             copy.start()
             copy.wait()
         got = dot_nn(u_both, operand[0])
         got = got[:ROWS] + got[ROWS:] + dot_nn(u_high, operand[1])
         rows = []
         for g in range(GROUPS):
-            main = owned[0, chunk * GROUPS + g]
+            main = own_ref[0, chunk * GROUPS + g]
             off_z = main[6:7]
-            hz = hat(z_row, owned[1, chunk * GROUPS + g, 1:2, :], 1.0 - off_z, off_z)
+            hz = hat(z_row, own_ref[1, chunk * GROUPS + g, 1:2, :], 1.0 - off_z, off_z)
             value = jnp.sum(hz * got[:, 128 * g : 128 * g + 128], axis=0, keepdims=True)
             rows.append(jnp.where(main[3:4] > 0.0, value, 0.0))
         values = jnp.concatenate(rows, axis=0)
@@ -552,11 +564,15 @@
     outgoing = pl.pallas_call(
         functools.partial(pack_kernel, shape),
         out_shape=jax.ShapeDtypeStruct((sources, rows, 128), f32),
-        in_specs=[whole, whole, whole],
+        in_specs=[pl.BlockSpec(memory_space=pl.ANY)] * 3,
         out_specs=whole,
         scratch_shapes=[
+            pltpu.VMEM((1, point_data.shape[2], sources, slots), f32),
+            pltpu.VMEM((1, point_cells.shape[2], sources, slots), jnp.int32),
+            pltpu.VMEM((1, sources), jnp.int32),
             pltpu.VMEM((4, sources, 8, 128), f32),
             pltpu.VMEM((bricks, sources, 8, 128), f32),
+            pltpu.SemaphoreType.DMA((3,)),
         ],
         compiler_params=pltpu.CompilerParams(vmem_limit_bytes=56 * MIB),
         name="pack_points",
@@ -578,20 +594,26 @@
                 lines += 6 * 16 * -(-count * high // 16)
     edge_shape = jax.ShapeDtypeStruct((2, XTILES, HALO, 128), f32)
     steps = groups // GROUPS
+    if steps == 1:
+        blocks = {"in_specs": [whole], "out_specs": (whole,) * 4}
+    else:
+        blocks = {
+            "grid": (steps,),
+            "in_specs": [pl.BlockSpec((4, GROUPS, rows, 128), lambda s: (0, s, 0, 0))],
+            "out_specs": (
+                pl.BlockSpec((2, XTILES, ROWS, 128), lambda s: (0, 0, 0, 0)),
+                pl.BlockSpec((2, XTILES, HALO, 128), lambda s: (0, 0, 0, 0)),
+                pl.BlockSpec((2, XTILES, HALO, 128), lambda s: (0, 0, 0, 0)),
+                pl.BlockSpec((2, GROUPS, 8, 128), lambda s: (0, s, 0, 0)),
+            ),
+        }
     fields, up, down, own = pl.pallas_call(
         functools.partial(splat_kernel, shape),
-        grid=(steps,),
         out_shape=(
             jax.ShapeDtypeStruct((2, XTILES, ROWS, 128), f32), edge_shape, edge_shape,
             jax.ShapeDtypeStruct((2, groups, 8, 128), f32),
         ),
-        in_specs=[pl.BlockSpec((4, GROUPS, rows, 128), lambda s: (0, s, 0, 0))],
-        out_specs=(
-            pl.BlockSpec((2, XTILES, ROWS, 128), lambda s: (0, 0, 0, 0)),
-            pl.BlockSpec((2, XTILES, HALO, 128), lambda s: (0, 0, 0, 0)),
-            pl.BlockSpec((2, XTILES, HALO, 128), lambda s: (0, 0, 0, 0)),
-            pl.BlockSpec((2, GROUPS, 8, 128), lambda s: (0, s, 0, 0)),
-        ),
+        **blocks,
         scratch_shapes=[
             pltpu.VMEM((rows // 2, GROUPS, 8, 128), f32),
             pltpu.VMEM((lines, 128 * GROUPS), bf16),
@@ -628,20 +650,17 @@
             jax.ShapeDtypeStruct((CX, CY, CZ), f32),
             jax.ShapeDtypeStruct((sources, slots), f32),
         ),
-        in_specs=[pl.BlockSpec(memory_space=pl.ANY)] * 5,
+        in_specs=[whole] * 4 + [pl.BlockSpec(memory_space=pl.ANY)],
         out_specs=(whole, whole),
         scratch_shapes=[
-            pltpu.VMEM((2, XTILES, ROWS, 128), f32),
-            pltpu.VMEM((2, XTILES, HALO, 128), f32),
-            pltpu.VMEM((2, XTILES, HALO, 128), f32),
-            pltpu.VMEM((2, groups, 8, 128), f32),
+            pltpu.VMEM((2, 2, XTILES, 16, 128), f32),
             pltpu.VMEM((XTILES, ROWS + 16, 128), f32),
             pltpu.VMEM((XTILES, ROWS + 16, 128), f32),
             pltpu.VMEM((XTILES, ROWS, 128), f32),
             pltpu.VMEM((XTILES, ROWS, 128), f32),
             pltpu.VMEM((END_TILE - FIRST_TILE, ROWS, 128), f32),
             pltpu.VMEM((2, depth, 128 * GROUPS), bf16),
-            pltpu.SemaphoreType.DMA((5,)),
+            pltpu.SemaphoreType.DMA,
         ],
         compiler_params=pltpu.CompilerParams(vmem_limit_bytes=16 * MIB),
         name="solve_and_read",

time: 52.8 us -> 52.2 us (0.989)
  Pallas kernels: 16.4 us -> 15.7 us
    pallas_call x1, Pallas kernels: 4.96 us -> 4.34 us  [on_device(): pl.pallas_call(functools.partial(solve_kernel, shape), out_shape=(jax.Sha...]
where the time goes in v9:
time: 52.2 us; the launch traced here: 51.9 us
  blocking collectives  26.7 us (51%)
  Pallas kernels  15.7 us (30%)
  starting transfers between devices  4.48 us (9%)
  waiting for transfers between devices  3.75 us (7%)
  between operations  0.68 us (1%)
  local copies, waits for them, and re-layouts  0.61 us (1%)
    all_to_all x1, blocking collectives, on_device(): lax.all_to_all(outgoing, AXES, split_axis=0, concat_axis=0, tiled=True)  17.5 us
    all_to_all x1, blocking collectives, on_device(): lax.all_to_all(values.reshape(1, sources, slots), AXES, split_axis=1, con...  9.17 us
    pallas_call x1, Pallas kernels, on_device(): pl.pallas_call(functools.partial(splat_kernel, shape), out_shape=(jax.Sha...  8.46 us
    pallas_call x1, Pallas kernels, on_device(): pl.pallas_call(functools.partial(solve_kernel, shape), out_shape=(jax.Sha...  4.34 us
    ppermute x1, waiting for transfers between devices, on_device(): from_high = lax.ppermute(down, 'gz', [(i + 1, i) for i in range(gz - 1)])  3.75 us
    ppermute x1, starting transfers between devices, on_device(): from_low = lax.ppermute(up, 'gz', [(i, i + 1) for i in range(gz - 1)])  3 us
    pallas_call x1, Pallas kernels, on_device(): pl.pallas_call(functools.partial(pack_kernel, shape), out_shape=jax.Shape...  2.11 us
    ppermute x1, starting transfers between devices, on_device(): from_high = lax.ppermute(down, 'gz', [(i + 1, i) for i in range(gz - 1)])  1.47 us
  transfers between devices with their start and end apart: 2, of which 1 were waited for; matrix products, arithmetic and copies ran while one was open for 0% of the time, Pallas kernels for 2%

profile of v9, /device:TPU:0, one launch (start us, length us, event | category | flops | bytes accessed | tf_op | source)
XLA Modules:
  0.0 51.9 jit_solution(1084347510244145437)
XLA Ops:
  0.6 2.1 %pack_points.1 = f32[32,16,128]{2,1,0:T(8,128)} custom-call(f32[1,7,32,32]{3,2,1,0:T(8,128)} %bitcast.9, s32[1,3,32,32]{3,2,1,0:T(8,128)} %bitcast.11, s32[1,32]{1,0:T(1,128)} %counts_hbm.1), custom_call_target="tpu_custom_call" | custom-call | tf_op jit(solution)/shard_map/pack_points/pallas_call | solution.py:564
  2.7 17.5 %all_to_all.10 = f32[32,16,128]{2,1,0:T(8,128)S(1)} all-to-all(f32[32,16,128]{2,1,0:T(8,128)} %pack_points.1), channel_id=1, replica_groups=mesh['gx'=4,'gy'=2,'gz'=4] {'gx','gy','gz'}, dimensions={0} | all-to-all | bytes 524288 | tf_op jit(solution)/shard_map/all_to_all | solution.py:585
  20.3 8.5 %splat_points.1 = (f32[2,7,144,128]{3,2,1,0:T(8,128)S(1)}, f32[2,7,8,128]{3,2,1,0:T(8,128)S(1)}, f32[2,7,8,128]{3,2,1,0:T(8,128)S(1)}, f32[2,8,8,128]{3,2,1,0:T(8,128)S(1)}) custom-call(f32[4,8,16,128]{3,2,1,0:T(8,128)S(1)} %bitcast.7), custom_call_target="tpu_custom_call" | custom-call | tf_op jit(solution)/shard_map/splat_points/pallas_call | solution.py:610
  28.7 3.0 %collective-permute-start = (f32[2,7,8,128]{3,2,1,0:T(8,128)S(1)}, f32[2,7,8,128]{3,2,1,0:T(8,128)S(1)}, u32[]{:S(2)}, u32[]{:S(2)}) collective-permute-start(f32[2,7,8,128]{3,2,1,0:T(8,128)S(1)} %get-tuple-element.9), channel_id=1, source_target_pairs={{0,1},{1,2},{2,3},{4,5},{5,6},{6,7},{8,9},{9,10},{10,11},{12,13},{... | collective-permute-start | bytes 172040 | tf_op jit(solution)/shard_map/ppermute | solution.py:630
  31.7 1.5 %collective-permute-start.1 = (f32[2,7,8,128]{3,2,1,0:T(8,128)S(1)}, f32[2,7,8,128]{3,2,1,0:T(8,128)S(1)}, u32[]{:S(2)}, u32[]{:S(2)}) collective-permute-start(f32[2,7,8,128]{3,2,1,0:T(8,128)S(1)} %get-tuple-element.10), channel_id=1, source_target_pairs={{1,0},{2,1},{3,2},{5,4},{6,5},{7,6},{9,8},{10,9},{11,10},{13,12},{... | collective-permute-start | bytes 172040 | tf_op jit(solution)/shard_map/ppermute | solution.py:631
  33.2 0.8 %read_operand.1.read_ref = bf16[1,2,640,1024]{3,2,1,0:T(8,128)(2,1)S(1)} custom-call(f32[2,8,8,128]{3,2,1,0:T(8,128)S(1)} %get-tuple-element.11.own_ref), custom_call_target="tpu_custom_call" | custom-call | flops 5242880 | bytes 2621440 | tf_op jit(solution)/shard_map/read_operand/pallas_call | solution.py:634
  34.0 0.0 collective-permute-done.from_low_ref
  34.0 3.7 %collective-permute-done.1.from_high_ref = f32[2,7,8,128]{3,2,1,0:T(8,128)S(1)} collective-permute-done((f32[2,7,8,128]{3,2,1,0:T(8,128)S(1)}, f32[2,7,8,128]{3,2,1,0:T(8,128)S(1)}, u32[]{:S(2)}, u32[]{:S(2)}) %collective-permute-start.1) | collective-permute-done | bytes 57376 | tf_op jit(solution)/shard_map/ppermute | solution.py:631
  37.8 4.3 %solve_and_read.1 = (f32[16,16,128]{2,1,0:T(8,128)}, f32[32,32]{1,0:T(8,128)S(1)}) custom-call(f32[2,7,144,128]{3,2,1,0:T(8,128)S(1)} %get-tuple-element.8.fields_ref, f32[2,7,8,128]{3,2,1,0:T(8,128)S(1)} %collective-permute-done.from_low_ref, f32[2,7,8,128]{3,2,1,0:T(8,128)S(1)} %collective-permute-done.1.from_high_ref, ...), custom_call_target="tpu_custom_call" | custom-call | tf_op jit(solution)/shard_map/solve_and_read/pallas_call | solution.py:647
  42.1 9.2 %all_to_all.11 = f32[1,32,32]{2,0,1:T(1,128)S(1)} all-to-all(f32[1,32,32]{2,0,1:T(1,128)S(1)} %bitcast.8), channel_id=1, replica_groups=mesh['gx'=4,'gy'=2,'gz'=4] {'gx','gy','gz'}, dimensions={1} | all-to-all | bytes 8192 | tf_op jit(solution)/shard_map/all_to_all | solution.py:669
  51.3 0.6 %copy.8 = f32[1,32,32]{2,1,0:T(8,128)} copy(f32[1,32,32]{2,1,0:T(8,128)S(1)} %bitcast.10) | data formatting | bytes 8192
Async XLA Ops:
  28.7 5.3 %collective-permute-start = (f32[2,7,8,128]{3,2,1,0:T(8,128)S(1)}, f32[2,7,8,128]{3,2,1,0:T(8,128)S(1)}, u32[]{:S(2)}, u32[]{:S(2)}) collective-permute-start(f32[2,7,8,128]{3,2,1,0:T(8,128)S(1)} %get-tuple-element.9), channel_id=1, source_target_pairs={{0,1},{1,2},{2,3},{4,5},{5,6},{6,7},{8,9},{9,10},{10,11},{12,13},{... | collective-permute-start | bytes 172040 | tf_op jit(solution)/shard_map/ppermute | solution.py:630
  31.7 6.1 %collective-permute-start.1 = (f32[2,7,8,128]{3,2,1,0:T(8,128)S(1)}, f32[2,7,8,128]{3,2,1,0:T(8,128)S(1)}, u32[]{:S(2)}, u32[]{:S(2)}) collective-permute-start(f32[2,7,8,128]{3,2,1,0:T(8,128)S(1)} %get-tuple-element.10), channel_id=1, source_target_pairs={{1,0},{2,1},{3,2},{5,4},{6,5},{7,6},{9,8},{10,9},{11,10},{13,12},{... | collective-permute-start | bytes 172040 | tf_op jit(solution)/shard_map/ppermute | solution.py:631

commit v10 on v9

--- a/solution.py
+++ b/solution.py
@@ -62,22 +62,8 @@
     return bricks + brick // 4, 2 * (brick % 4)
 
 
-def pack_kernel(
-    shape, data_hbm, cells_hbm, counts_hbm, out_ref,
-    data_ref, cells_ref, counts_ref, main, extra, arrivals,
-):
+def pack_kernel(shape, data_ref, cells_ref, counts_ref, out_ref):
     gx, gy, gz = shape
-    copies = [
-        pltpu.make_async_copy(source, target, arrivals.at[i])
-        for i, (source, target) in enumerate(
-            ((data_hbm, data_ref), (cells_hbm, cells_ref), (counts_hbm, counts_ref))
-        )
-    ]
-    for copy in copies:
-        copy.start()
-    extra[...] = jnp.zeros_like(extra)
-    for copy in copies:
-        copy.wait()
     slots = data_ref.shape[3]
     sources = gx * gy * gz
     lane = lax.broadcasted_iota(jnp.int32, (sources, slots), 1)
@@ -90,46 +76,44 @@
     weight = jnp.where(lane < counts, data_ref[0, 3], 0.0)
     cells = [cells_ref[0, c].astype(f32) for c in range(3)]
     channels = [data_ref[0, c] * (-0.5 * weight) for c in range(3)]
-    channels += [weight] + [data_ref[0, c] for c in range(4, 7)] + [cells[0]]
-
-    def placed(value, part):
-        pieces = [jnp.zeros((sources, slots * part), f32)] if part else []
-        pieces.append(value)
-        if part < 3:
-            pieces.append(jnp.zeros((sources, 128 - slots * (part + 1)), f32))
-        return jnp.concatenate(pieces, axis=1)
-
-    for part in range(min(bricks, 4)):
-        for c in range(8):
-            main[part, :, c, :] = placed(channels[c], part)
+    channels += [weight] + [data_ref[0, c] for c in range(4, 7)] + cells
+    blank = jnp.zeros((sources, 128 - slots), f32)
+    channels = [jnp.concatenate([value, blank], axis=1) for value in channels]
+    row = lax.broadcasted_iota(jnp.int32, (sources, 128), 0)
+    y = (row // gz) % gy
+
+    def moved(value, by):
+        if by == 0:
+            return value
+        gap = jnp.zeros((abs(by), 128), f32)
+        if by > 0:
+            return jnp.concatenate([value[by:], gap], axis=0)
+        return jnp.concatenate([gap, value[:by]], axis=0)
+
+    def beside(value, e):
+        if e == 0:
+            return value
+        up = jnp.where(y < gy - 1, moved(value, gz), 0.0)
+        down = jnp.where(y > 0, moved(value, -gz), 0.0)
+        if others == 1:
+            return up + down
+        return down if e == 1 else up
+
+    by_y = [[beside(value, e) for e in range(1 + others)] for value in channels]
+    lines = {}
     for b in range(bricks):
-        place, row = extra_place(b, bricks)
-        for c in range(2):
-            extra[b, :, row + c, :] = placed(cells[1 + c], place % 4)
-    for d in range(sources):
-        x, y, z = d // (gy * gz), (d // gz) % gy, d % gz
-        if others == 0:
-            ys = (y,)
-        elif others == 1:
-            ys = (y, 1 - y)
-        else:
-            ys = (y, y - 1, y + 1)
-        sums = [None] * (out_ref.shape[1] // 8)
-        for e, by in enumerate(ys):
-            for o, bx in enumerate((x, x - 1, x + 1)):
-                if not (0 <= bx < gx and 0 <= by < gy):
-                    continue
-                b = e * 3 + o
-                source = (bx * gy + by) * gz + z
-                place, _ = extra_place(b, bricks)
-                for tile, value in (
-                    (b // 4, main[b % 4, source]), (place // 4, extra[b, source])
-                ):
-                    sums[tile] = value if sums[tile] is None else sums[tile] + value
-        for tile, value in enumerate(sums):
-            if value is None:
-                value = jnp.zeros((8, 128), f32)
-            out_ref[d, 8 * tile : 8 * tile + 8, :] = value
+        e, o = divmod(b, 3)
+        place, extra_row = extra_place(b, bricks)
+        for c in range(10):
+            block, line = (b, c) if c < 8 else (place, extra_row + c - 8)
+            value = moved(by_y[c][e], (0, -gy * gz, gy * gz)[o])
+            if block % 4:
+                value = pltpu.roll(value, slots * (block % 4), 1)
+            key = 8 * (block // 4) + line
+            lines[key] = value if key not in lines else lines[key] + value
+    for line in range(out_ref.shape[1]):
+        value = lines.get(line)
+        out_ref[:, line, :] = jnp.zeros((sources, 128), f32) if value is None else value
 
 
 def hat(coordinate, cell, low, high):
@@ -172,7 +156,7 @@
 
 
 def splat_kernel(
-    shape, recv_ref, fields_ref, up_ref, down_ref, own_ref,
+    shape, recv_ref, fields_ref, edges_ref, own_ref,
     points, left_ref, right_ref, hx_ref, near, beside, slope,
 ):
     gx, gy, gz = shape
@@ -389,9 +373,17 @@
             finish_all()
     else:
         finish_all()
-    for c in range(2):
-        up_ref[c] = fields_ref[c, :, UP_AT : UP_AT + HALO, :]
-        down_ref[c] = fields_ref[c, :, DOWN_AT : DOWN_AT + HALO, :]
+    edges_ref[...] = jnp.zeros_like(edges_ref)
+
+    @pl.when(mz < gz - 1)
+    def _():
+        for c in range(2):
+            edges_ref[mz + 1, c] = fields_ref[c, :, UP_AT : UP_AT + HALO, :]
+
+    @pl.when(mz > 0)
+    def _():
+        for c in range(2):
+            edges_ref[mz - 1, c] = fields_ref[c, :, DOWN_AT : DOWN_AT + HALO, :]
 
 
 def chebyshev_factors():
@@ -435,7 +427,7 @@
 
 
 def solve_kernel(
-    shape, fields_ref, from_low_ref, from_high_ref, own_ref, read_ref,
+    shape, fields_ref, halos_ref, own_ref, read_ref,
     indicator_ref, values_ref,
     edge, first, second, base, inverse, total, operand, arrivals,
 ):
@@ -445,8 +437,15 @@
     copy.start()
     edge[...] = jnp.zeros_like(edge)
     low_at, high_at = UP_AT - CZ, DOWN_AT + CZ - (ROWS - 16)
-    edge[0, :, :, low_at : low_at + HALO, :] = from_low_ref[...]
-    edge[1, :, :, high_at : high_at + HALO, :] = from_high_ref[...]
+
+    @pl.when(mz > 0)
+    def _():
+        edge[0, :, :, low_at : low_at + HALO, :] = halos_ref[mz - 1]
+
+    @pl.when(mz < gz - 1)
+    def _():
+        edge[1, :, :, high_at : high_at + HALO, :] = halos_ref[mz + 1]
+
 
     def given(c, t, i):
         value = fields_ref[c, t, 8 * i : 8 * i + 8, :]
@@ -564,16 +563,8 @@
     outgoing = pl.pallas_call(
         functools.partial(pack_kernel, shape),
         out_shape=jax.ShapeDtypeStruct((sources, rows, 128), f32),
-        in_specs=[pl.BlockSpec(memory_space=pl.ANY)] * 3,
+        in_specs=[whole] * 3,
         out_specs=whole,
-        scratch_shapes=[
-            pltpu.VMEM((1, point_data.shape[2], sources, slots), f32),
-            pltpu.VMEM((1, point_cells.shape[2], sources, slots), jnp.int32),
-            pltpu.VMEM((1, sources), jnp.int32),
-            pltpu.VMEM((4, sources, 8, 128), f32),
-            pltpu.VMEM((bricks, sources, 8, 128), f32),
-            pltpu.SemaphoreType.DMA((3,)),
-        ],
         compiler_params=pltpu.CompilerParams(vmem_limit_bytes=56 * MIB),
         name="pack_points",
     )(
@@ -592,25 +583,24 @@
             for start in range(0, len(planes), size):
                 count = min(size, len(planes) - start)
                 lines += 6 * 16 * -(-count * high // 16)
-    edge_shape = jax.ShapeDtypeStruct((2, XTILES, HALO, 128), f32)
+    edge_shape = jax.ShapeDtypeStruct((gz, 2, XTILES, HALO, 128), f32)
     steps = groups // GROUPS
     if steps == 1:
-        blocks = {"in_specs": [whole], "out_specs": (whole,) * 4}
+        blocks = {"in_specs": [whole], "out_specs": (whole,) * 3}
     else:
         blocks = {
             "grid": (steps,),
             "in_specs": [pl.BlockSpec((4, GROUPS, rows, 128), lambda s: (0, s, 0, 0))],
             "out_specs": (
                 pl.BlockSpec((2, XTILES, ROWS, 128), lambda s: (0, 0, 0, 0)),
-                pl.BlockSpec((2, XTILES, HALO, 128), lambda s: (0, 0, 0, 0)),
-                pl.BlockSpec((2, XTILES, HALO, 128), lambda s: (0, 0, 0, 0)),
+                pl.BlockSpec((gz, 2, XTILES, HALO, 128), lambda s: (0, 0, 0, 0, 0)),
                 pl.BlockSpec((2, GROUPS, 8, 128), lambda s: (0, s, 0, 0)),
             ),
         }
-    fields, up, down, own = pl.pallas_call(
+    fields, edges, own = pl.pallas_call(
         functools.partial(splat_kernel, shape),
         out_shape=(
-            jax.ShapeDtypeStruct((2, XTILES, ROWS, 128), f32), edge_shape, edge_shape,
+            jax.ShapeDtypeStruct((2, XTILES, ROWS, 128), f32), edge_shape,
             jax.ShapeDtypeStruct((2, groups, 8, 128), f32),
         ),
         **blocks,
@@ -627,8 +617,7 @@
         name="splat_points",
     )(arrived)
 
-    from_low = lax.ppermute(up, "gz", [(i, i + 1) for i in range(gz - 1)])
-    from_high = lax.ppermute(down, "gz", [(i + 1, i) for i in range(gz - 1)])
+    halos = lax.all_to_all(edges, "gz", split_axis=0, concat_axis=0, tiled=True)
 
     depth = 128 * (END_TILE - FIRST_TILE)
     read = pl.pallas_call(
@@ -650,7 +639,7 @@
             jax.ShapeDtypeStruct((CX, CY, CZ), f32),
             jax.ShapeDtypeStruct((sources, slots), f32),
         ),
-        in_specs=[whole] * 4 + [pl.BlockSpec(memory_space=pl.ANY)],
+        in_specs=[whole] * 3 + [pl.BlockSpec(memory_space=pl.ANY)],
         out_specs=(whole, whole),
         scratch_shapes=[
             pltpu.VMEM((2, 2, XTILES, 16, 128), f32),
@@ -664,7 +653,7 @@
         ],
         compiler_params=pltpu.CompilerParams(vmem_limit_bytes=16 * MIB),
         name="solve_and_read",
-    )(fields, from_low, from_high, own, read)
+    )(fields, halos, own, read)
 
     returned = lax.all_to_all(
         values.reshape(1, sources, slots), AXES, split_axis=1, concat_axis=1, tiled=True

time: 52.2 us -> 58.4 us (1.12)
  waiting for transfers between devices: 3.75 us -> 8.14 us
  local copies, waits for them, and re-layouts: 0.61 us -> 2.78 us
  starting transfers between devices: 4.48 us -> 3.38 us
  Pallas kernels: 15.7 us -> 16.5 us
    all_to_all x0 -> x1, waiting for transfers between devices: none -> 8.14 us  [on_device(): halos = lax.all_to_all(edges, 'gz', split_axis=0, concat_axis=0, tiled=True)]
    ppermute x2 -> x0, starting transfers between devices: 4.48 us -> none  [the longest x1 3 us: on_device(): from_low = lax.ppermute(up, 'gz', [(i, i + 1) for i in range(gz - 1)])]
    ppermute x2 -> x0, waiting for transfers between devices: 3.75 us -> none  [the longest x1 3.75 us: on_device(): from_high = lax.ppermute(down, 'gz', [(i + 1, i) for i in range(gz - 1)])]
    all_to_all x0 -> x1, starting transfers between devices: none -> 3.38 us  [on_device(): halos = lax.all_to_all(edges, 'gz', split_axis=0, concat_axis=0, tiled=True)]
    unnamed x1 -> x5, local copies, waits for them, and re-layouts: 0.61 us -> 2.78 us
    pallas_call x1, Pallas kernels: 8.46 us -> 9.17 us  [on_device(): pl.pallas_call(functools.partial(splat_kernel, shape), out_shape=(jax.Sha...]
  transfers between devices with their start and end apart: 2 -> 1, of which waited for: 1 -> 1; matrix products, arithmetic and copies ran while one was open for 0% -> 0% of each run, Pallas kernels for 2% -> 1%
where the time goes in v10:
time: 58.4 us; the launch traced here: 58.1 us
  blocking collectives  26.7 us (46%)
  Pallas kernels  16.5 us (28%)
  waiting for transfers between devices  8.14 us (14%)
  starting transfers between devices  3.38 us (6%)
  local copies, waits for them, and re-layouts  2.78 us (5%)
  between operations  0.66 us (1%)
    all_to_all x1, blocking collectives, on_device(): lax.all_to_all(outgoing, AXES, split_axis=0, concat_axis=0, tiled=True)  17.5 us
    pallas_call x1, Pallas kernels, on_device(): pl.pallas_call(functools.partial(splat_kernel, shape), out_shape=(jax.Sha...  9.17 us
    all_to_all x1, blocking collectives, on_device(): lax.all_to_all(values.reshape(1, sources, slots), AXES, split_axis=1, con...  9.16 us
    all_to_all x1, waiting for transfers between devices, on_device(): halos = lax.all_to_all(edges, 'gz', split_axis=0, concat_axis=0, tiled=True)  8.14 us
    pallas_call x1, Pallas kernels, on_device(): pl.pallas_call(functools.partial(solve_kernel, shape), out_shape=(jax.Sha...  4.5 us
    all_to_all x1, starting transfers between devices, on_device(): halos = lax.all_to_all(edges, 'gz', split_axis=0, concat_axis=0, tiled=True)  3.38 us
    unnamed x5, local copies, waits for them, and re-layouts  2.78 us
    pallas_call x1, Pallas kernels, on_device(): pl.pallas_call(functools.partial(pack_kernel, shape), out_shape=jax.Shape...  1.96 us
  transfers between devices with their start and end apart: 1, of which 1 were waited for; matrix products, arithmetic and copies ran while one was open for 0% of the time, Pallas kernels for 1%

profile of v10, /device:TPU:0, one launch (start us, length us, event | category | flops | bytes accessed | tf_op | source)
XLA Modules:
  0.0 58.1 jit_solution(3372131152766270092)
XLA Ops:
  0.6 2.0 %pack_points.1 = f32[32,16,128]{2,1,0:T(8,128)} custom-call(f32[1,7,32,32]{3,2,1,0:T(8,128)} %bitcast.9, s32[1,3,32,32]{3,2,1,0:T(8,128)} %bitcast.11, s32[1,32]{1,0:T(1,128)} %counts_ref.1), custom_call_target="tpu_custom_call" | custom-call | tf_op jit(solution)/shard_map/pack_points/pallas_call | solution.py:563
  2.6 17.5 %all_to_all.15 = f32[32,16,128]{2,1,0:T(8,128)S(1)} all-to-all(f32[32,16,128]{2,1,0:T(8,128)} %pack_points.1), channel_id=1, replica_groups=mesh['gx'=4,'gy'=2,'gz'=4] {'gx','gy','gz'}, dimensions={0} | all-to-all | bytes 524288 | tf_op jit(solution)/shard_map/all_to_all | solution.py:576
  20.1 9.2 %splat_points.1 = (f32[2,7,144,128]{3,2,1,0:T(8,128)S(1)}, f32[4,2,7,8,128]{4,3,2,1,0:T(8,128)}, f32[2,8,8,128]{3,2,1,0:T(8,128)S(1)}) custom-call(f32[4,8,16,128]{3,2,1,0:T(8,128)S(1)} %bitcast.7), custom_call_target="tpu_custom_call" | custom-call | tf_op jit(solution)/shard_map/splat_points/pallas_call | solution.py:600
  29.3 0.0 copy-start
  29.3 1.0 %copy-done = f32[2,7,144,128]{3,2,1,0:T(8,128)} copy-done((f32[2,7,144,128]{3,2,1,0:T(8,128)}, f32[2,7,144,128]{3,2,1,0:T(8,128)S(1)}, u32[]{:S(2)}) %copy-start) | copy-done | bytes 1032216
  30.2 3.4 %all-to-all-start.1 = ((f32[4,2,7,8,128]{4,3,2,1,0:T(8,128)}), f32[4,2,7,8,128]{4,3,2,1,0:T(8,128)S(1)}, u32[]{:S(2)}, u32[]{:S(2)}) async-start(f32[4,2,7,8,128]{4,3,2,1,0:T(8,128)} %get-tuple-element.8), calls=%async_computation.1 | async-start | bytes 458752 | tf_op jit(solution)/shard_map/all_to_all | solution.py:620
  33.6 0.8 %read_operand.1.read_ref = bf16[1,2,640,1024]{3,2,1,0:T(8,128)(2,1)S(1)} custom-call(f32[2,8,8,128]{3,2,1,0:T(8,128)S(1)} %get-tuple-element.9.own_ref), custom_call_target="tpu_custom_call" | custom-call | flops 5242880 | bytes 2621440 | tf_op jit(solution)/shard_map/read_operand/pallas_call | solution.py:623
  34.5 8.1 %all-to-all-done.1.halos_ref = f32[4,2,7,8,128]{4,3,2,1,0:T(8,128)S(1)} async-done(((f32[4,2,7,8,128]{4,3,2,1,0:T(8,128)}), f32[4,2,7,8,128]{4,3,2,1,0:T(8,128)S(1)}, u32[]{:S(2)}, u32[]{:S(2)}) %all-to-all-start.1) | async-done | bytes 229408 | tf_op jit(solution)/shard_map/all_to_all | solution.py:620
  42.6 0.0 copy-start.1
  42.6 1.2 %copy-done.1 = f32[2,7,144,128]{3,2,1,0:T(8,128)S(1)} copy-done((f32[2,7,144,128]{3,2,1,0:T(8,128)S(1)}, f32[2,7,144,128]{3,2,1,0:T(8,128)}, u32[]{:S(2)}) %copy-start.1) | copy-done | bytes 1032216
  43.8 4.5 %solve_and_read.1 = (f32[16,16,128]{2,1,0:T(8,128)}, f32[32,32]{1,0:T(8,128)S(1)}) custom-call(f32[2,7,144,128]{3,2,1,0:T(8,128)S(1)} %copy-done.1, f32[4,2,7,8,128]{4,3,2,1,0:T(8,128)S(1)} %all-to-all-done.1.halos_ref, f32[2,8,8,128]{3,2,1,0:T(8,128)S(1)} %get-tuple-element.9.own_ref, bf16[1,2,640,1024]{3,2,1,0:T(8,128)(2,1)S(1)} %read_operand.1.read_ref), custom_call_target="tpu_custom_call" | custom-call | tf_op jit(solution)/shard_map/solve_and_read/pallas_call | solution.py:636
  48.3 9.2 %all_to_all.16 = f32[1,32,32]{2,0,1:T(1,128)S(1)} all-to-all(f32[1,32,32]{2,0,1:T(1,128)S(1)} %bitcast.8), channel_id=1, replica_groups=mesh['gx'=4,'gy'=2,'gz'=4] {'gx','gy','gz'}, dimensions={1} | all-to-all | bytes 8192 | tf_op jit(solution)/shard_map/all_to_all | solution.py:658
  57.5 0.6 %copy.8 = f32[1,32,32]{2,1,0:T(8,128)} copy(f32[1,32,32]{2,1,0:T(8,128)S(1)} %bitcast.10) | data formatting | bytes 8192
Async XLA Ops:
  29.3 1.0 %copy-start = (f32[2,7,144,128]{3,2,1,0:T(8,128)}, f32[2,7,144,128]{3,2,1,0:T(8,128)S(1)}, u32[]{:S(2)}) copy-start(f32[2,7,144,128]{3,2,1,0:T(8,128)S(1)} %get-tuple-element.7.fields_ref) | copy-start | bytes 3096580
  30.2 12.4 %all-to-all-start.1 = ((f32[4,2,7,8,128]{4,3,2,1,0:T(8,128)}), f32[4,2,7,8,128]{4,3,2,1,0:T(8,128)S(1)}, u32[]{:S(2)}, u32[]{:S(2)}) async-start(f32[4,2,7,8,128]{4,3,2,1,0:T(8,128)} %get-tuple-element.8), calls=%async_computation.1 | async-start | bytes 458752 | tf_op jit(solution)/shard_map/all_to_all | solution.py:620
  42.6 1.2 %copy-start.1 = (f32[2,7,144,128]{3,2,1,0:T(8,128)S(1)}, f32[2,7,144,128]{3,2,1,0:T(8,128)}, u32[]{:S(2)}) copy-start(f32[2,7,144,128]{3,2,1,0:T(8,128)} %copy-done) | copy-start | bytes 3096580

commit v11 on v10

--- a/solution.py
+++ b/solution.py
@@ -156,7 +156,7 @@
 
 
 def splat_kernel(
-    shape, recv_ref, fields_ref, edges_ref, own_ref,
+    shape, recv_ref, fields_ref, up_ref, down_ref, own_ref,
     points, left_ref, right_ref, hx_ref, near, beside, slope,
 ):
     gx, gy, gz = shape
@@ -373,17 +373,9 @@
             finish_all()
     else:
         finish_all()
-    edges_ref[...] = jnp.zeros_like(edges_ref)
-
-    @pl.when(mz < gz - 1)
-    def _():
-        for c in range(2):
-            edges_ref[mz + 1, c] = fields_ref[c, :, UP_AT : UP_AT + HALO, :]
-
-    @pl.when(mz > 0)
-    def _():
-        for c in range(2):
-            edges_ref[mz - 1, c] = fields_ref[c, :, DOWN_AT : DOWN_AT + HALO, :]
+    for c in range(2):
+        up_ref[c] = fields_ref[c, :, UP_AT : UP_AT + HALO, :]
+        down_ref[c] = fields_ref[c, :, DOWN_AT : DOWN_AT + HALO, :]
 
 
 def chebyshev_factors():
@@ -399,9 +391,81 @@
 
 
 READ_PLANES = range(XPT * FIRST_TILE, XPT * END_TILE)
-
-
-def read_kernel(own_ref, out_ref, hx_ref):
+STRIPS = ROWS // 8
+INNER = range((UP_AT - CZ + HALO + REACH + 7) // 8, (DOWN_AT + CZ - REACH) // 8)
+LOW_ZONE = range(0, INNER[0] + 1)
+HIGH_ZONE = range(INNER[-1], STRIPS)
+
+
+def relax(shape, given, zone, wanted, work, store):
+    gx, gy, gz = shape
+    mx, my, mz = lax.axis_index("gx"), lax.axis_index("gy"), lax.axis_index("gz")
+    first, second, base, inverse = work
+    lane = lax.broadcasted_iota(jnp.int32, (8, 128), 1)
+    row = lax.broadcasted_iota(jnp.int32, (8, 128), 0)
+    y = lane % YS - YO + my * CY
+    inside_y = (y >= 0) & (y < gy * CY)
+    zero = jnp.zeros((8, 128), f32)
+    end_row = 8 * len(zone) + 8
+    for t in range(XTILES):
+        x = lane // YS + (XPT * t - XO) + mx * CX
+        inside_xy = inside_y & (x >= 0) & (x < gx * CX)
+        for scratch in (first, second):
+            scratch[t, 0:8, :] = zero
+            scratch[t, end_row : end_row + 8, :] = zero
+        for j, i in enumerate(zone):
+            inside = inside_xy
+            if 8 * i < ZO or 8 * i + 8 > ZO + CZ:
+                z = row + (8 * i - ZO) + mz * CZ
+                inside = inside & (z >= 0) & (z < gz * CZ)
+            diagonal = 6.0 + base_screen + point_screen * given(1, t, i)
+            inv = jnp.where(inside, 1.0 / diagonal, 0.0)
+            start = given(0, t, i) * inv
+            inverse[t, 8 * j : 8 * j + 8, :] = inv
+            base[t, 8 * j : 8 * j + 8, :] = start
+            first[t, 8 * j + 8 : 8 * j + 16, :] = start
+
+    now, later = first, second
+    factors = chebyshev_factors()
+    low_part, high_part = lane < YS, lane >= 128 - YS
+    for k, (keep, gain) in enumerate(factors, 1):
+        last = k == len(factors)
+        begin, end = k // XPT, (XO + CX + REACH - k + XPT) // XPT
+        if last:
+            begin, end = max(begin, FIRST_TILE), min(end, END_TILE)
+        for j, i in enumerate(zone):
+            if last and i not in wanted:
+                continue
+            at = slice(8 * j, 8 * j + 8)
+            inner = slice(8 * j + 8, 8 * j + 16)
+            reach = range(max(begin - 1, 0), min(end + 1, XTILES))
+            here = {t: now[t, inner, :] for t in reach}
+            ahead_x = {t: pltpu.roll(here[t], YS, 1) for t in reach if t < end}
+            behind_x = {t: pltpu.roll(here[t], 128 - YS, 1) for t in reach if t >= begin}
+            for t in range(begin, end):
+                mine = here[t]
+                near = now[t, 8 * j + 7 : 8 * j + 15, :] + now[t, 8 * j + 9 : 8 * j + 17, :]
+                near = near + pltpu.roll(mine, 1, 1) + pltpu.roll(mine, 127, 1)
+                before = ahead_x[t]
+                if t > 0:
+                    before = jnp.where(low_part, ahead_x[t - 1], before)
+                after = behind_x[t]
+                if t + 1 < XTILES:
+                    after = jnp.where(high_part, behind_x[t + 1], after)
+                near = near + before + after
+                if k == 1:
+                    ahead = (1.0 + keep) * mine + gain * (inverse[t, at, :] * near)
+                else:
+                    ahead = gain * (base[t, at, :] + inverse[t, at, :] * near)
+                    ahead = ahead + (1.0 + keep - gain) * mine - keep * later[t, inner, :]
+                if last:
+                    store(t - FIRST_TILE, i, ahead)
+                else:
+                    later[t, inner, :] = ahead
+        now, later = later, now
+
+
+def inner_kernel(shape, fields_ref, own_ref, out_ref, inner_ref, hx_ref, *work):
     y_row = row_iota(24) + float(8 - YO)
     blank = jnp.zeros((8, 128), f32)
     for chunk in range(own_ref.shape[1] // GROUPS):
@@ -425,111 +489,59 @@
                 out_ref[chunk, 0, start : start + YS, at] = high
                 out_ref[chunk, 1, start : start + YS, at] = low
 
+    def given(c, t, i):
+        return fields_ref[c, t, 8 * i : 8 * i + 8, :]
+
+    def store(t, i, value):
+        at = 8 * (i - INNER[0])
+        inner_ref[t, at : at + 8, :] = value
+
+    relax(shape, given, range(INNER[0] - 1, INNER[-1] + 2), INNER, work, store)
+
 
 def solve_kernel(
-    shape, fields_ref, halos_ref, own_ref, read_ref,
+    shape, fields_ref, from_low_ref, from_high_ref, own_ref, inner_ref, read_ref,
     indicator_ref, values_ref,
-    edge, first, second, base, inverse, total, operand, arrivals,
+    edge, total, first, second, base, inverse, first_high, second_high, base_high, inverse_high,
 ):
-    gx, gy, gz = shape
-    mx, my, mz = lax.axis_index("gx"), lax.axis_index("gy"), lax.axis_index("gz")
-    copy = pltpu.make_async_copy(read_ref.at[0], operand, arrivals)
-    copy.start()
     edge[...] = jnp.zeros_like(edge)
     low_at, high_at = UP_AT - CZ, DOWN_AT + CZ - (ROWS - 16)
-
-    @pl.when(mz > 0)
-    def _():
-        edge[0, :, :, low_at : low_at + HALO, :] = halos_ref[mz - 1]
-
-    @pl.when(mz < gz - 1)
-    def _():
-        edge[1, :, :, high_at : high_at + HALO, :] = halos_ref[mz + 1]
-
+    edge[0, :, :, low_at : low_at + HALO, :] = from_low_ref[...]
+    edge[1, :, :, high_at : high_at + HALO, :] = from_high_ref[...]
 
     def given(c, t, i):
         value = fields_ref[c, t, 8 * i : 8 * i + 8, :]
         if i < 2:
             value = value + edge[0, c, t, 8 * i : 8 * i + 8, :]
-        from_end = i - (ROWS // 8 - 2)
+        from_end = i - (STRIPS - 2)
         if from_end >= 0:
             value = value + edge[1, c, t, 8 * from_end : 8 * from_end + 8, :]
         return value
 
-    lane = lax.broadcasted_iota(jnp.int32, (8, 128), 1)
-    row = lax.broadcasted_iota(jnp.int32, (8, 128), 0)
-    y = lane % YS - YO + my * CY
-    inside_y = (y >= 0) & (y < gy * CY)
-    zero = jnp.zeros((8, 128), f32)
-    strips = ROWS // 8
-    for t in range(XTILES):
-        x = lane // YS + (XPT * t - XO) + mx * CX
-        inside_xy = inside_y & (x >= 0) & (x < gx * CX)
-        for scratch in (first, second):
-            scratch[t, 0:8, :] = zero
-            scratch[t, ROWS + 8 : ROWS + 16, :] = zero
-        for i in range(strips):
-            at = slice(8 * i, 8 * i + 8)
-            inside = inside_xy
-            if 8 * i < ZO or 8 * i + 8 > ZO + CZ:
-                z = row + (8 * i - ZO) + mz * CZ
-                inside = inside & (z >= 0) & (z < gz * CZ)
-            diagonal = 6.0 + base_screen + point_screen * given(1, t, i)
-            inv = jnp.where(inside, 1.0 / diagonal, 0.0)
-            start = given(0, t, i) * inv
-            inverse[t, at, :] = inv
-            base[t, at, :] = start
-            first[t, 8 * i + 8 : 8 * i + 16, :] = start
-
-    now, later = first, second
-    factors = chebyshev_factors()
-    low_part, high_part = lane < YS, lane >= 128 - YS
-    for k, (keep, gain) in enumerate(factors, 1):
-        last = k == len(factors)
-        begin, end = k // XPT, (XO + CX + REACH - k + XPT) // XPT
-        if last:
-            begin, end = max(begin, FIRST_TILE), min(end, END_TILE)
-        for i in range(strips):
-            at = slice(8 * i, 8 * i + 8)
-            inner = slice(8 * i + 8, 8 * i + 16)
-            reach = range(max(begin - 1, 0), min(end + 1, XTILES))
-            here = {t: now[t, inner, :] for t in reach}
-            ahead_x = {t: pltpu.roll(here[t], YS, 1) for t in reach if t < end}
-            behind_x = {t: pltpu.roll(here[t], 128 - YS, 1) for t in reach if t >= begin}
-            for t in range(begin, end):
-                mine = here[t]
-                near = now[t, 8 * i + 7 : 8 * i + 15, :] + now[t, 8 * i + 9 : 8 * i + 17, :]
-                near = near + pltpu.roll(mine, 1, 1) + pltpu.roll(mine, 127, 1)
-                before = ahead_x[t]
-                if t > 0:
-                    before = jnp.where(low_part, ahead_x[t - 1], before)
-                after = behind_x[t]
-                if t + 1 < XTILES:
-                    after = jnp.where(high_part, behind_x[t + 1], after)
-                near = near + before + after
-                ahead = (1.0 + keep - gain) * mine + gain * (base[t, at, :] + inverse[t, at, :] * near)
-                if k > 1:
-                    ahead = ahead - keep * later[t, inner, :]
-                if last:
-                    total[t - FIRST_TILE, at, :] = ahead
-                else:
-                    later[t, inner, :] = ahead
-        now, later = later, now
+    def store(t, i, value):
+        total[t, 8 * i : 8 * i + 8, :] = value
+
+    inner_rows = slice(8 * INNER[0], 8 * INNER[-1] + 8)
+    for t in range(END_TILE - FIRST_TILE):
+        total[t, 0:8, :] = jnp.zeros((8, 128), f32)
+        total[t, inner_rows, :] = inner_ref[t]
+    low_wanted = range(1, INNER[0])
+    high_wanted = range(INNER[-1] + 1, STRIPS)
+    relax(shape, given, LOW_ZONE, low_wanted, (first, second, base, inverse), store)
+    relax(
+        shape, given, HIGH_ZONE, high_wanted,
+        (first_high, second_high, base_high, inverse_high), store,
+    )
 
     parts = [split(total[t - FIRST_TILE]) for t in range(FIRST_TILE, END_TILE)]
     u_high = jnp.concatenate([part[0] for part in parts], axis=1)
     u_low = jnp.concatenate([part[1] for part in parts], axis=1)
     u_both = jnp.concatenate([u_high, u_low], axis=0)
     z_row = row_iota(ROWS) - float(ZO)
-    copy.wait()
     groups = own_ref.shape[1]
     for chunk in range(groups // GROUPS):
-        if chunk > 0:
-            copy = pltpu.make_async_copy(read_ref.at[chunk], operand, arrivals)
-            copy.start()
-            copy.wait()
-        got = dot_nn(u_both, operand[0])
-        got = got[:ROWS] + got[ROWS:] + dot_nn(u_high, operand[1])
+        got = dot_nn(u_both, read_ref[chunk, 0])
+        got = got[:ROWS] + got[ROWS:] + dot_nn(u_high, read_ref[chunk, 1])
         rows = []
         for g in range(GROUPS):
             main = own_ref[0, chunk * GROUPS + g]
@@ -551,6 +563,11 @@
                 indicator_ref[plane] = turned[YS * i + YO : YS * i + YO + CY, :]
 
 
+def work_shapes(strips):
+    padded = pltpu.VMEM((XTILES, 8 * strips + 16, 128), f32)
+    return [padded, padded] + 2 * [pltpu.VMEM((XTILES, 8 * strips, 128), f32)]
+
+
 def on_device(shape, point_data, point_cells, send_counts):
     gx, gy, gz = shape
     sources = gx * gy * gz
@@ -583,24 +600,25 @@
             for start in range(0, len(planes), size):
                 count = min(size, len(planes) - start)
                 lines += 6 * 16 * -(-count * high // 16)
-    edge_shape = jax.ShapeDtypeStruct((gz, 2, XTILES, HALO, 128), f32)
+    edge_shape = jax.ShapeDtypeStruct((2, XTILES, HALO, 128), f32)
     steps = groups // GROUPS
     if steps == 1:
-        blocks = {"in_specs": [whole], "out_specs": (whole,) * 3}
+        blocks = {"in_specs": [whole], "out_specs": (whole,) * 4}
     else:
         blocks = {
             "grid": (steps,),
             "in_specs": [pl.BlockSpec((4, GROUPS, rows, 128), lambda s: (0, s, 0, 0))],
             "out_specs": (
                 pl.BlockSpec((2, XTILES, ROWS, 128), lambda s: (0, 0, 0, 0)),
-                pl.BlockSpec((gz, 2, XTILES, HALO, 128), lambda s: (0, 0, 0, 0, 0)),
+                pl.BlockSpec((2, XTILES, HALO, 128), lambda s: (0, 0, 0, 0)),
+                pl.BlockSpec((2, XTILES, HALO, 128), lambda s: (0, 0, 0, 0)),
                 pl.BlockSpec((2, GROUPS, 8, 128), lambda s: (0, s, 0, 0)),
             ),
         }
-    fields, edges, own = pl.pallas_call(
+    fields, up, down, own = pl.pallas_call(
         functools.partial(splat_kernel, shape),
         out_shape=(
-            jax.ShapeDtypeStruct((2, XTILES, ROWS, 128), f32), edge_shape,
+            jax.ShapeDtypeStruct((2, XTILES, ROWS, 128), f32), edge_shape, edge_shape,
             jax.ShapeDtypeStruct((2, groups, 8, 128), f32),
         ),
         **blocks,
@@ -617,21 +635,27 @@
         name="splat_points",
     )(arrived)
 
-    halos = lax.all_to_all(edges, "gz", split_axis=0, concat_axis=0, tiled=True)
+    from_low = lax.ppermute(up, "gz", [(i, i + 1) for i in range(gz - 1)])
+    from_high = lax.ppermute(down, "gz", [(i + 1, i) for i in range(gz - 1)])
 
     depth = 128 * (END_TILE - FIRST_TILE)
-    read = pl.pallas_call(
-        read_kernel,
-        out_shape=jax.ShapeDtypeStruct((steps, 2, depth, 128 * GROUPS), bf16),
-        in_specs=[whole],
-        out_specs=whole,
-        scratch_shapes=[pltpu.VMEM((XPT * END_TILE, GROUPS, 128), f32)],
-        compiler_params=pltpu.CompilerParams(vmem_limit_bytes=16 * MIB),
+    tiles = END_TILE - FIRST_TILE
+    read, inner = pl.pallas_call(
+        functools.partial(inner_kernel, shape),
+        out_shape=(
+            jax.ShapeDtypeStruct((steps, 2, depth, 128 * GROUPS), bf16),
+            jax.ShapeDtypeStruct((tiles, 8 * len(INNER), 128), f32),
+        ),
+        in_specs=[whole, whole],
+        out_specs=(whole, whole),
+        scratch_shapes=[pltpu.VMEM((XPT * END_TILE, GROUPS, 128), f32)]
+        + work_shapes(len(INNER) + 2),
+        compiler_params=pltpu.CompilerParams(vmem_limit_bytes=24 * MIB),
         cost_estimate=pl.CostEstimate(
             flops=8 * depth * 128 * groups, bytes_accessed=4 * depth * 128 * groups, transcendentals=0
         ),
-        name="read_operand",
-    )(own)
+        name="solve_inner",
+    )(fields, own)
 
     indicator, values = pl.pallas_call(
         functools.partial(solve_kernel, shape),
@@ -639,21 +663,17 @@
             jax.ShapeDtypeStruct((CX, CY, CZ), f32),
             jax.ShapeDtypeStruct((sources, slots), f32),
         ),
-        in_specs=[whole] * 3 + [pl.BlockSpec(memory_space=pl.ANY)],
+        in_specs=[whole] * 6,
         out_specs=(whole, whole),
         scratch_shapes=[
             pltpu.VMEM((2, 2, XTILES, 16, 128), f32),
-            pltpu.VMEM((XTILES, ROWS + 16, 128), f32),
-            pltpu.VMEM((XTILES, ROWS + 16, 128), f32),
-            pltpu.VMEM((XTILES, ROWS, 128), f32),
-            pltpu.VMEM((XTILES, ROWS, 128), f32),
-            pltpu.VMEM((END_TILE - FIRST_TILE, ROWS, 128), f32),
-            pltpu.VMEM((2, depth, 128 * GROUPS), bf16),
-            pltpu.SemaphoreType.DMA,
-        ],
-        compiler_params=pltpu.CompilerParams(vmem_limit_bytes=16 * MIB),
+            pltpu.VMEM((tiles, ROWS, 128), f32),
+        ]
+        + work_shapes(len(LOW_ZONE))
+        + work_shapes(len(HIGH_ZONE)),
+        compiler_params=pltpu.CompilerParams(vmem_limit_bytes=24 * MIB),
         name="solve_and_read",
-    )(fields, halos, own, read)
+    )(fields, from_low, from_high, own, inner, read)
 
     returned = lax.all_to_all(
         values.reshape(1, sources, slots), AXES, split_axis=1, concat_axis=1, tiled=True

time: 58.4 us -> 50.6 us (0.87)
  waiting for transfers between devices: 8.14 us -> 1.61 us
  local copies, waits for them, and re-layouts: 2.78 us -> 0.61 us
  starting transfers between devices: 3.38 us -> 4.48 us
  Pallas kernels: 16.5 us -> 15.8 us
    all_to_all x1 -> x0, waiting for transfers between devices: 8.14 us -> none  [on_device(): halos = lax.all_to_all(edges, 'gz', split_axis=0, concat_axis=0, tiled=True)]
    ppermute x0 -> x2, starting transfers between devices: none -> 4.48 us  [the longest x1 3.01 us: on_device(): from_low = lax.ppermute(up, 'gz', [(i, i + 1) for i in range(gz - 1)])]
    all_to_all x1 -> x0, starting transfers between devices: 3.38 us -> none  [on_device(): halos = lax.all_to_all(edges, 'gz', split_axis=0, concat_axis=0, tiled=True)]
    unnamed x5 -> x1, local copies, waits for them, and re-layouts: 2.78 us -> 0.61 us
    pallas_call x1, Pallas kernels: 0.83 us -> 2.97 us  [on_device(): pl.pallas_call(functools.partial(inner_kernel, shape), out_shape=(jax.Sha...]
    pallas_call x1, Pallas kernels: 4.5 us -> 2.44 us  [on_device(): pl.pallas_call(functools.partial(solve_kernel, shape), out_shape=(jax.Sha...]
    ppermute x0 -> x2, waiting for transfers between devices: none -> 1.61 us  [the longest x1 1.61 us: on_device(): from_high = lax.ppermute(down, 'gz', [(i + 1, i) for i in range(gz - 1)])]
    pallas_call x1, Pallas kernels: 9.17 us -> 8.45 us  [on_device(): pl.pallas_call(functools.partial(splat_kernel, shape), out_shape=(jax.Sha...]
  transfers between devices with their start and end apart: 1 -> 2, of which waited for: 1 -> 1; matrix products, arithmetic and copies ran while one was open for 0% -> 0% of each run, Pallas kernels for 1% -> 6%
where the time goes in v11:
time: 50.6 us; the launch traced here: 50.3 us
  blocking collectives  27.1 us (54%)
  Pallas kernels  15.8 us (31%)
  starting transfers between devices  4.48 us (9%)
  waiting for transfers between devices  1.61 us (3%)
  between operations  0.66 us (1%)
  local copies, waits for them, and re-layouts  0.61 us (1%)
    all_to_all x1, blocking collectives, on_device(): lax.all_to_all(outgoing, AXES, split_axis=0, concat_axis=0, tiled=True)  17.5 us
    all_to_all x1, blocking collectives, on_device(): lax.all_to_all(values.reshape(1, sources, slots), AXES, split_axis=1, con...  9.64 us
    pallas_call x1, Pallas kernels, on_device(): pl.pallas_call(functools.partial(splat_kernel, shape), out_shape=(jax.Sha...  8.45 us
    ppermute x1, starting transfers between devices, on_device(): from_low = lax.ppermute(up, 'gz', [(i, i + 1) for i in range(gz - 1)])  3.01 us
    pallas_call x1, Pallas kernels, on_device(): pl.pallas_call(functools.partial(inner_kernel, shape), out_shape=(jax.Sha...  2.97 us
    pallas_call x1, Pallas kernels, on_device(): pl.pallas_call(functools.partial(solve_kernel, shape), out_shape=(jax.Sha...  2.44 us
    pallas_call x1, Pallas kernels, on_device(): pl.pallas_call(functools.partial(pack_kernel, shape), out_shape=jax.Shape...  1.95 us
    ppermute x1, waiting for transfers between devices, on_device(): from_high = lax.ppermute(down, 'gz', [(i + 1, i) for i in range(gz - 1)])  1.61 us
  transfers between devices with their start and end apart: 2, of which 1 were waited for; matrix products, arithmetic and copies ran while one was open for 0% of the time, Pallas kernels for 6%

profile of v11, /device:TPU:0, one launch (start us, length us, event | category | flops | bytes accessed | tf_op | source)
XLA Modules:
  0.0 50.3 jit_solution(5085249246742676898)
XLA Ops:
  0.6 2.0 %pack_points.1 = f32[32,16,128]{2,1,0:T(8,128)} custom-call(f32[1,7,32,32]{3,2,1,0:T(8,128)} %bitcast.9, s32[1,3,32,32]{3,2,1,0:T(8,128)} %bitcast.11, s32[1,32]{1,0:T(1,128)} %counts_ref.1), custom_call_target="tpu_custom_call" | custom-call | tf_op jit(solution)/shard_map/pack_points/pallas_call | solution.py:580
  2.6 17.5 %all_to_all.10 = f32[32,16,128]{2,1,0:T(8,128)S(1)} all-to-all(f32[32,16,128]{2,1,0:T(8,128)} %pack_points.1), channel_id=1, replica_groups=mesh['gx'=4,'gy'=2,'gz'=4] {'gx','gy','gz'}, dimensions={0} | all-to-all | bytes 524288 | tf_op jit(solution)/shard_map/all_to_all | solution.py:593
  20.1 8.5 %splat_points.1 = (f32[2,7,144,128]{3,2,1,0:T(8,128)S(1)}, f32[2,7,8,128]{3,2,1,0:T(8,128)S(1)}, f32[2,7,8,128]{3,2,1,0:T(8,128)S(1)}, f32[2,8,8,128]{3,2,1,0:T(8,128)S(1)}) custom-call(f32[4,8,16,128]{3,2,1,0:T(8,128)S(1)} %bitcast.7), custom_call_target="tpu_custom_call" | custom-call | tf_op jit(solution)/shard_map/splat_points/pallas_call | solution.py:618
  28.5 3.0 %collective-permute-start = (f32[2,7,8,128]{3,2,1,0:T(8,128)S(1)}, f32[2,7,8,128]{3,2,1,0:T(8,128)S(1)}, u32[]{:S(2)}, u32[]{:S(2)}) collective-permute-start(f32[2,7,8,128]{3,2,1,0:T(8,128)S(1)} %get-tuple-element.11), channel_id=1, source_target_pairs={{0,1},{1,2},{2,3},{4,5},{5,6},{6,7},{8,9},{9,10},{10,11},{12,13},{... | collective-permute-start | bytes 172040 | tf_op jit(solution)/shard_map/ppermute | solution.py:638
  31.6 1.5 %collective-permute-start.1 = (f32[2,7,8,128]{3,2,1,0:T(8,128)S(1)}, f32[2,7,8,128]{3,2,1,0:T(8,128)S(1)}, u32[]{:S(2)}, u32[]{:S(2)}) collective-permute-start(f32[2,7,8,128]{3,2,1,0:T(8,128)S(1)} %get-tuple-element.12), channel_id=1, source_target_pairs={{1,0},{2,1},{3,2},{5,4},{6,5},{7,6},{9,8},{10,9},{11,10},{13,12},{... | collective-permute-start | bytes 172040 | tf_op jit(solution)/shard_map/ppermute | solution.py:639
  33.0 3.0 %solve_inner.1 = (bf16[1,2,640,1024]{3,2,1,0:T(8,128)(2,1)S(1)}, f32[5,112,128]{2,1,0:T(8,128)S(1)}) custom-call(f32[2,7,144,128]{3,2,1,0:T(8,128)S(1)} %get-tuple-element.10.fields_ref, f32[2,8,8,128]{3,2,1,0:T(8,128)S(1)} %get-tuple-element.13.own_ref), custom_call_target="tpu_custom_call" | custom-call | flops 5242880 | bytes 2621440 | tf_op jit(solution)/shard_map/solve_inner/pallas_call | solution.py:643
  36.0 0.0 collective-permute-done.from_low_ref
  36.0 1.6 %collective-permute-done.1.from_high_ref = f32[2,7,8,128]{3,2,1,0:T(8,128)S(1)} collective-permute-done((f32[2,7,8,128]{3,2,1,0:T(8,128)S(1)}, f32[2,7,8,128]{3,2,1,0:T(8,128)S(1)}, u32[]{:S(2)}, u32[]{:S(2)}) %collective-permute-start.1) | collective-permute-done | bytes 57376 | tf_op jit(solution)/shard_map/ppermute | solution.py:639
  37.6 2.4 %solve_and_read.1 = (f32[16,16,128]{2,1,0:T(8,128)}, f32[32,32]{1,0:T(8,128)S(1)}) custom-call(f32[2,7,144,128]{3,2,1,0:T(8,128)S(1)} %get-tuple-element.10.fields_ref, f32[2,7,8,128]{3,2,1,0:T(8,128)S(1)} %collective-permute-done.from_low_ref, f32[2,7,8,128]{3,2,1,0:T(8,128)S(1)} %collective-permute-done.1.from_high_ref, ...), custom_call_target="tpu_custom_call" | custom-call | tf_op jit(solution)/shard_map/solve_and_read/pallas_call | solution.py:660
  40.1 9.6 %all_to_all.11 = f32[1,32,32]{2,0,1:T(1,128)S(1)} all-to-all(f32[1,32,32]{2,0,1:T(1,128)S(1)} %bitcast.8), channel_id=1, replica_groups=mesh['gx'=4,'gy'=2,'gz'=4] {'gx','gy','gz'}, dimensions={1} | all-to-all | bytes 8192 | tf_op jit(solution)/shard_map/all_to_all | solution.py:678
  49.7 0.6 %copy.8 = f32[1,32,32]{2,1,0:T(8,128)} copy(f32[1,32,32]{2,1,0:T(8,128)S(1)} %bitcast.10) | data formatting | bytes 8192
Async XLA Ops:
  28.5 7.5 %collective-permute-start = (f32[2,7,8,128]{3,2,1,0:T(8,128)S(1)}, f32[2,7,8,128]{3,2,1,0:T(8,128)S(1)}, u32[]{:S(2)}, u32[]{:S(2)}) collective-permute-start(f32[2,7,8,128]{3,2,1,0:T(8,128)S(1)} %get-tuple-element.11), channel_id=1, source_target_pairs={{0,1},{1,2},{2,3},{4,5},{5,6},{6,7},{8,9},{9,10},{10,11},{12,13},{... | collective-permute-start | bytes 172040 | tf_op jit(solution)/shard_map/ppermute | solution.py:638
  31.6 6.1 %collective-permute-start.1 = (f32[2,7,8,128]{3,2,1,0:T(8,128)S(1)}, f32[2,7,8,128]{3,2,1,0:T(8,128)S(1)}, u32[]{:S(2)}, u32[]{:S(2)}) collective-permute-start(f32[2,7,8,128]{3,2,1,0:T(8,128)S(1)} %get-tuple-element.12), channel_id=1, source_target_pairs={{1,0},{2,1},{3,2},{5,4},{6,5},{7,6},{9,8},{10,9},{11,10},{13,12},{... | collective-permute-start | bytes 172040 | tf_op jit(solution)/shard_map/ppermute | solution.py:639

commit v12 on v11

--- a/solution.py
+++ b/solution.py
@@ -156,7 +156,7 @@
 
 
 def splat_kernel(
-    shape, recv_ref, fields_ref, up_ref, down_ref, own_ref,
+    shape, recv_ref, fields_ref, first_ref, second_ref, own_ref,
     points, left_ref, right_ref, hx_ref, near, beside, slope,
 ):
     gx, gy, gz = shape
@@ -201,6 +201,8 @@
     z_row = row_iota(CZ).astype(bf16)
     own_row = row_iota(24) + float(8 - YO)
     point_lane = lax.broadcasted_iota(jnp.int32, (128, 128), 1)
+    lane_number = point_lane.astype(f32).astype(bf16)
+    no_top = jnp.zeros((128, 128), bf16)
 
     def multiply(begin, lists, b, e, high):
         counts = [-(-len(planes) * high // 16) * 16 for planes in lists]
@@ -318,8 +320,7 @@
             cell_z, off_z = points[place, :, row + 1, :], points[b, :, 6, :]
             top = jnp.where((cell_z + 1.0 == float(CZ)) & (cell_z + 1.0 < z_limit), off_z, 0.0)
             top_columns = jnp.concatenate([top, jnp.zeros((128 - GROUPS, 128), f32)], axis=0).T
-            top_high = top_columns.astype(bf16).astype(f32)
-            top_low = top_columns - top_high
+            top_high, top_low = split(top_columns)
             y_parts = []
             for g in range(GROUPS):
                 main = points[b, g]
@@ -330,8 +331,9 @@
                 hz_high, hz_low = split_hat(z_row, cell_z, off_z)
                 right_ref[b, 0, at, 0:CZ] = hz_high.T
                 right_ref[b, 1, at, 0:CZ] = hz_low.T
-                right_ref[b, 0, at, CZ : CZ + 128] = jnp.where(point_lane == g, top_high, 0.0).astype(bf16)
-                right_ref[b, 1, at, CZ : CZ + 128] = jnp.where(point_lane == g, top_low, 0.0).astype(bf16)
+                column = lane_number == float(g)
+                right_ref[b, 0, at, CZ : CZ + 128] = jnp.where(column, top_high, no_top)
+                right_ref[b, 1, at, CZ : CZ + 128] = jnp.where(column, top_low, no_top)
                 high_y = jnp.where(cell_y + 1.0 < y_limit, off_y, 0.0)
                 hy = hat(y_row, cell_y, 1.0 - off_y, high_y)
                 dy = hat_slope(y_row, cell_y, 1.0 - off_y, high_y)
@@ -374,8 +376,10 @@
     else:
         finish_all()
     for c in range(2):
-        up_ref[c] = fields_ref[c, :, UP_AT : UP_AT + HALO, :]
-        down_ref[c] = fields_ref[c, :, DOWN_AT : DOWN_AT + HALO, :]
+        up = fields_ref[c, :, UP_AT : UP_AT + HALO, :]
+        down = fields_ref[c, :, DOWN_AT : DOWN_AT + HALO, :]
+        first_ref[c] = jnp.where(mz % 2 == 0, up, down)
+        second_ref[c] = jnp.where(mz % 2 == 0, down, up)
 
 
 def chebyshev_factors():
@@ -500,14 +504,16 @@
 
 
 def solve_kernel(
-    shape, fields_ref, from_low_ref, from_high_ref, own_ref, inner_ref, read_ref,
+    shape, fields_ref, first_ref, second_ref, own_ref, inner_ref, read_ref,
     indicator_ref, values_ref,
     edge, total, first, second, base, inverse, first_high, second_high, base_high, inverse_high,
 ):
     edge[...] = jnp.zeros_like(edge)
     low_at, high_at = UP_AT - CZ, DOWN_AT + CZ - (ROWS - 16)
-    edge[0, :, :, low_at : low_at + HALO, :] = from_low_ref[...]
-    edge[1, :, :, high_at : high_at + HALO, :] = from_high_ref[...]
+    even = lax.axis_index("gz") % 2 == 0
+    got_first, got_second = first_ref[...], second_ref[...]
+    edge[0, :, :, low_at : low_at + HALO, :] = jnp.where(even, got_second, got_first)
+    edge[1, :, :, high_at : high_at + HALO, :] = jnp.where(even, got_first, got_second)
 
     def given(c, t, i):
         value = fields_ref[c, t, 8 * i : 8 * i + 8, :]
@@ -615,7 +621,7 @@
                 pl.BlockSpec((2, GROUPS, 8, 128), lambda s: (0, s, 0, 0)),
             ),
         }
-    fields, up, down, own = pl.pallas_call(
+    fields, first, second, own = pl.pallas_call(
         functools.partial(splat_kernel, shape),
         out_shape=(
             jax.ShapeDtypeStruct((2, XTILES, ROWS, 128), f32), edge_shape, edge_shape,
@@ -635,8 +641,11 @@
         name="splat_points",
     )(arrived)
 
-    from_low = lax.ppermute(up, "gz", [(i, i + 1) for i in range(gz - 1)])
-    from_high = lax.ppermute(down, "gz", [(i + 1, i) for i in range(gz - 1)])
+    def swapped(edge, start):
+        pairs = [(i, i + 1) for i in range(start, gz - 1, 2)]
+        return lax.ppermute(edge, "gz", pairs + [(j, i) for i, j in pairs])
+
+    got_first, got_second = swapped(first, 0), swapped(second, 1)
 
     depth = 128 * (END_TILE - FIRST_TILE)
     tiles = END_TILE - FIRST_TILE
@@ -673,7 +682,7 @@
         + work_shapes(len(HIGH_ZONE)),
         compiler_params=pltpu.CompilerParams(vmem_limit_bytes=24 * MIB),
         name="solve_and_read",
-    )(fields, from_low, from_high, own, inner, read)
+    )(fields, got_first, got_second, own, inner, read)
 
     returned = lax.all_to_all(
         values.reshape(1, sources, slots), AXES, split_axis=1, concat_axis=1, tiled=True

time: 50.6 us -> 48.2 us (0.953)
  starting transfers between devices: 4.48 us -> 1.99 us
  blocking collectives: 27.1 us -> 29 us
  waiting for transfers between devices: 1.61 us -> 0.01 us
    ppermute x2, starting transfers between devices: 4.48 us -> 1.99 us  [swapped(): return lax.ppermute(edge, 'gz', pairs + [(j, i) for i, j in pairs])]
    all_to_all x1, blocking collectives: 9.64 us -> 11.5 us  [on_device(): lax.all_to_all(values.reshape(1, sources, slots), AXES, split_axis=1, con...]
    ppermute x2, waiting for transfers between devices: 1.61 us -> 0.01 us  [swapped(): return lax.ppermute(edge, 'gz', pairs + [(j, i) for i, j in pairs])]
  transfers between devices with their start and end apart: 2 -> 2, of which waited for: 1 -> 0; matrix products, arithmetic and copies ran while one was open for 0% -> 0% of each run, Pallas kernels for 6% -> 6%
where the time goes in v12:
time: 48.2 us; the launch traced here: 48 us
  blocking collectives  29 us (60%)
  Pallas kernels  15.7 us (33%)
  starting transfers between devices  1.99 us (4%)
  between operations  0.66 us (1%)
  local copies, waits for them, and re-layouts  0.61 us (1%)
    all_to_all x1, blocking collectives, on_device(): lax.all_to_all(outgoing, AXES, split_axis=0, concat_axis=0, tiled=True)  17.5 us
    all_to_all x1, blocking collectives, on_device(): lax.all_to_all(values.reshape(1, sources, slots), AXES, split_axis=1, con...  11.5 us
    pallas_call x1, Pallas kernels, on_device(): pl.pallas_call(functools.partial(splat_kernel, shape), out_shape=(jax.Sha...  8.37 us
    pallas_call x1, Pallas kernels, on_device(): pl.pallas_call(functools.partial(inner_kernel, shape), out_shape=(jax.Sha...  2.97 us
    pallas_call x1, Pallas kernels, on_device(): pl.pallas_call(functools.partial(solve_kernel, shape), out_shape=(jax.Sha...  2.46 us
    ppermute x2, starting transfers between devices, swapped(): return lax.ppermute(edge, 'gz', pairs + [(j, i) for i, j in pairs])  1.99 us
    pallas_call x1, Pallas kernels, on_device(): pl.pallas_call(functools.partial(pack_kernel, shape), out_shape=jax.Shape...  1.95 us
  transfers between devices with their start and end apart: 2, of which 0 were waited for; matrix products, arithmetic and copies ran while one was open for 0% of the time, Pallas kernels for 6%

profile of v12, /device:TPU:0, one launch (start us, length us, event | category | flops | bytes accessed | tf_op | source)
XLA Modules:
  0.0 48.0 jit_solution(13514171766775390778)
XLA Ops:
  0.6 2.0 %pack_points.1 = f32[32,16,128]{2,1,0:T(8,128)} custom-call(f32[1,7,32,32]{3,2,1,0:T(8,128)} %bitcast.9, s32[1,3,32,32]{3,2,1,0:T(8,128)} %bitcast.11, s32[1,32]{1,0:T(1,128)} %counts_ref.1), custom_call_target="tpu_custom_call" | custom-call | tf_op jit(solution)/shard_map/pack_points/pallas_call | solution.py:586
  2.6 17.5 %all_to_all.10 = f32[32,16,128]{2,1,0:T(8,128)S(1)} all-to-all(f32[32,16,128]{2,1,0:T(8,128)} %pack_points.1), channel_id=1, replica_groups=mesh['gx'=4,'gy'=2,'gz'=4] {'gx','gy','gz'}, dimensions={0} | all-to-all | bytes 524288 | tf_op jit(solution)/shard_map/all_to_all | solution.py:599
  20.1 8.4 %splat_points.1 = (f32[2,7,144,128]{3,2,1,0:T(8,128)S(1)}, f32[2,7,8,128]{3,2,1,0:T(8,128)S(1)}, f32[2,7,8,128]{3,2,1,0:T(8,128)S(1)}, f32[2,8,8,128]{3,2,1,0:T(8,128)S(1)}) custom-call(f32[4,8,16,128]{3,2,1,0:T(8,128)S(1)} %bitcast.7), custom_call_target="tpu_custom_call" | custom-call | tf_op jit(solution)/shard_map/splat_points/pallas_call | solution.py:624
  28.5 1.2 %collective-permute-start = (f32[2,7,8,128]{3,2,1,0:T(8,128)S(1)}, f32[2,7,8,128]{3,2,1,0:T(8,128)S(1)}, u32[]{:S(2)}, u32[]{:S(2)}) collective-permute-start(f32[2,7,8,128]{3,2,1,0:T(8,128)S(1)} %get-tuple-element.11), channel_id=1, source_target_pairs={{0,1},{2,3},{1,0},{3,2},{4,5},{6,7},{5,4},{7,6},{8,9},{10,11},{9,8... | collective-permute-start | bytes 172040 | tf_op jit(solution)/shard_map/ppermute | solution.py:646
  29.6 0.8 %collective-permute-start.1 = (f32[2,7,8,128]{3,2,1,0:T(8,128)S(1)}, f32[2,7,8,128]{3,2,1,0:T(8,128)S(1)}, u32[]{:S(2)}, u32[]{:S(2)}) collective-permute-start(f32[2,7,8,128]{3,2,1,0:T(8,128)S(1)} %get-tuple-element.12), channel_id=1, source_target_pairs={{1,2},{2,1},{5,6},{6,5},{9,10},{10,9},{13,14},{14,13},{17,18},{18,... | collective-permute-start | bytes 172040 | tf_op jit(solution)/shard_map/ppermute | solution.py:646
  30.5 3.0 %solve_inner.1 = (bf16[1,2,640,1024]{3,2,1,0:T(8,128)(2,1)S(1)}, f32[5,112,128]{2,1,0:T(8,128)S(1)}) custom-call(f32[2,7,144,128]{3,2,1,0:T(8,128)S(1)} %get-tuple-element.10.fields_ref, f32[2,8,8,128]{3,2,1,0:T(8,128)S(1)} %get-tuple-element.13.own_ref), custom_call_target="tpu_custom_call" | custom-call | flops 5242880 | bytes 2621440 | tf_op jit(solution)/shard_map/solve_inner/pallas_call | solution.py:652
  33.4 0.0 collective-permute-done.first_ref
  33.4 0.0 collective-permute-done.1.second_ref
  33.5 2.5 %solve_and_read.1 = (f32[16,16,128]{2,1,0:T(8,128)}, f32[32,32]{1,0:T(8,128)S(1)}) custom-call(f32[2,7,144,128]{3,2,1,0:T(8,128)S(1)} %get-tuple-element.10.fields_ref, f32[2,7,8,128]{3,2,1,0:T(8,128)S(1)} %collective-permute-done.first_ref, f32[2,7,8,128]{3,2,1,0:T(8,128)S(1)} %collective-permute-done.1.second_ref, ...), custom_call_target="tpu_custom_call" | custom-call | tf_op jit(solution)/shard_map/solve_and_read/pallas_call | solution.py:669
  35.9 11.5 %all_to_all.11 = f32[1,32,32]{2,0,1:T(1,128)S(1)} all-to-all(f32[1,32,32]{2,0,1:T(1,128)S(1)} %bitcast.8), channel_id=1, replica_groups=mesh['gx'=4,'gy'=2,'gz'=4] {'gx','gy','gz'}, dimensions={1} | all-to-all | bytes 8192 | tf_op jit(solution)/shard_map/all_to_all | solution.py:687
  47.4 0.6 %copy.8 = f32[1,32,32]{2,1,0:T(8,128)} copy(f32[1,32,32]{2,1,0:T(8,128)S(1)} %bitcast.10) | data formatting | bytes 8192
Async XLA Ops:
  28.5 5.0 %collective-permute-start = (f32[2,7,8,128]{3,2,1,0:T(8,128)S(1)}, f32[2,7,8,128]{3,2,1,0:T(8,128)S(1)}, u32[]{:S(2)}, u32[]{:S(2)}) collective-permute-start(f32[2,7,8,128]{3,2,1,0:T(8,128)S(1)} %get-tuple-element.11), channel_id=1, source_target_pairs={{0,1},{2,3},{1,0},{3,2},{4,5},{6,7},{5,4},{7,6},{8,9},{10,11},{9,8... | collective-permute-start | bytes 172040 | tf_op jit(solution)/shard_map/ppermute | solution.py:646
  29.6 3.8 %collective-permute-start.1 = (f32[2,7,8,128]{3,2,1,0:T(8,128)S(1)}, f32[2,7,8,128]{3,2,1,0:T(8,128)S(1)}, u32[]{:S(2)}, u32[]{:S(2)}) collective-permute-start(f32[2,7,8,128]{3,2,1,0:T(8,128)S(1)} %get-tuple-element.12), channel_id=1, source_target_pairs={{1,2},{2,1},{5,6},{6,5},{9,10},{10,9},{13,14},{14,13},{17,18},{18,... | collective-permute-start | bytes 172040 | tf_op jit(solution)/shard_map/ppermute | solution.py:646

commit v13 on v12

--- a/solution.py
+++ b/solution.py
@@ -469,7 +469,7 @@
         now, later = later, now
 
 
-def inner_kernel(shape, fields_ref, own_ref, out_ref, inner_ref, hx_ref, *work):
+def read_kernel(own_ref, out_ref, hx_ref):
     y_row = row_iota(24) + float(8 - YO)
     blank = jnp.zeros((8, 128), f32)
     for chunk in range(own_ref.shape[1] // GROUPS):
@@ -493,6 +493,8 @@
                 out_ref[chunk, 0, start : start + YS, at] = high
                 out_ref[chunk, 1, start : start + YS, at] = low
 
+
+def inner_kernel(shape, fields_ref, inner_ref, *work):
     def given(c, t, i):
         return fields_ref[c, t, 8 * i : 8 * i + 8, :]
 
@@ -645,26 +647,35 @@
         pairs = [(i, i + 1) for i in range(start, gz - 1, 2)]
         return lax.ppermute(edge, "gz", pairs + [(j, i) for i, j in pairs])
 
-    got_first, got_second = swapped(first, 0), swapped(second, 1)
-
     depth = 128 * (END_TILE - FIRST_TILE)
     tiles = END_TILE - FIRST_TILE
-    read, inner = pl.pallas_call(
-        functools.partial(inner_kernel, shape),
-        out_shape=(
-            jax.ShapeDtypeStruct((steps, 2, depth, 128 * GROUPS), bf16),
-            jax.ShapeDtypeStruct((tiles, 8 * len(INNER), 128), f32),
-        ),
-        in_specs=[whole, whole],
-        out_specs=(whole, whole),
-        scratch_shapes=[pltpu.VMEM((XPT * END_TILE, GROUPS, 128), f32)]
-        + work_shapes(len(INNER) + 2),
+    got_first = swapped(first, 0)
+    read = pl.pallas_call(
+        read_kernel,
+        out_shape=jax.ShapeDtypeStruct((steps, 2, depth, 128 * GROUPS), bf16),
+        in_specs=[whole],
+        out_specs=whole,
+        scratch_shapes=[pltpu.VMEM((XPT * END_TILE, GROUPS, 128), f32)],
         compiler_params=pltpu.CompilerParams(vmem_limit_bytes=24 * MIB),
         cost_estimate=pl.CostEstimate(
             flops=8 * depth * 128 * groups, bytes_accessed=4 * depth * 128 * groups, transcendentals=0
         ),
+        name="read_operand",
+    )(own)
+    second, read = lax.optimization_barrier((second, read))
+    got_second = swapped(second, 1)
+    inner = pl.pallas_call(
+        functools.partial(inner_kernel, shape),
+        out_shape=jax.ShapeDtypeStruct((tiles, 8 * len(INNER), 128), f32),
+        in_specs=[whole],
+        out_specs=whole,
+        scratch_shapes=work_shapes(len(INNER) + 2),
+        compiler_params=pltpu.CompilerParams(vmem_limit_bytes=24 * MIB),
+        cost_estimate=pl.CostEstimate(
+            flops=70 * ROWS * 128 * XTILES, bytes_accessed=8 * ROWS * 128 * XTILES, transcendentals=0
+        ),
         name="solve_inner",
-    )(fields, own)
+    )(fields)
 
     indicator, values = pl.pallas_call(
         functools.partial(solve_kernel, shape),

time: 48.2 us -> 49 us (1.017)
  blocking collectives: 29 us -> 29.7 us
    all_to_all x1, blocking collectives: 11.5 us -> 12.2 us  [on_device(): lax.all_to_all(values.reshape(1, sources, slots), AXES, split_axis=1, con...]
    pallas_call x1 -> x2, Pallas kernels: 2.97 us -> 2.98 us  [the longest x1 2.16 us: on_device(): pl.pallas_call(functools.partial(inner_kernel, shape), out_shape=jax.Shap...]
where the time goes in v13:
time: 49 us; the launch traced here: 48.8 us
  blocking collectives  29.7 us (61%)
  Pallas kernels  15.8 us (32%)
  starting transfers between devices  2.01 us (4%)
  between operations  0.67 us (1%)
  local copies, waits for them, and re-layouts  0.61 us (1%)
    all_to_all x1, blocking collectives, on_device(): lax.all_to_all(outgoing, AXES, split_axis=0, concat_axis=0, tiled=True)  17.5 us
    all_to_all x1, blocking collectives, on_device(): lax.all_to_all(values.reshape(1, sources, slots), AXES, split_axis=1, con...  12.2 us
    pallas_call x1, Pallas kernels, on_device(): pl.pallas_call(functools.partial(splat_kernel, shape), out_shape=(jax.Sha...  8.37 us
    pallas_call x1, Pallas kernels, on_device(): pl.pallas_call(functools.partial(solve_kernel, shape), out_shape=(jax.Sha...  2.49 us
    pallas_call x1, Pallas kernels, on_device(): pl.pallas_call(functools.partial(inner_kernel, shape), out_shape=jax.Shap...  2.16 us
    ppermute x2, starting transfers between devices, swapped(): return lax.ppermute(edge, 'gz', pairs + [(j, i) for i, j in pairs])  2.01 us
    pallas_call x1, Pallas kernels, on_device(): pl.pallas_call(functools.partial(pack_kernel, shape), out_shape=jax.Shape...  1.95 us
  transfers between devices with their start and end apart: 2, of which 0 were waited for; matrix products, arithmetic and copies ran while one was open for 0% of the time, Pallas kernels for 6%

profile of v13, /device:TPU:0, one launch (start us, length us, event | category | flops | bytes accessed | tf_op | source)
XLA Modules:
  0.0 48.8 jit_solution(5003894279824975591)
XLA Ops:
  0.6 2.0 %pack_points.1 = f32[32,16,128]{2,1,0:T(8,128)} custom-call(f32[1,7,32,32]{3,2,1,0:T(8,128)} %bitcast.9, s32[1,3,32,32]{3,2,1,0:T(8,128)} %bitcast.11, s32[1,32]{1,0:T(1,128)} %counts_ref.1), custom_call_target="tpu_custom_call" | custom-call | tf_op jit(solution)/shard_map/pack_points/pallas_call | solution.py:588
  2.6 17.5 %all_to_all.10 = f32[32,16,128]{2,1,0:T(8,128)S(1)} all-to-all(f32[32,16,128]{2,1,0:T(8,128)} %pack_points.1), channel_id=1, replica_groups=mesh['gx'=4,'gy'=2,'gz'=4] {'gx','gy','gz'}, dimensions={0} | all-to-all | bytes 524288 | tf_op jit(solution)/shard_map/all_to_all | solution.py:601
  20.1 8.4 %splat_points.1 = (f32[2,7,144,128]{3,2,1,0:T(8,128)S(1)}, f32[2,7,8,128]{3,2,1,0:T(8,128)S(1)}, f32[2,7,8,128]{3,2,1,0:T(8,128)S(1)}, f32[2,8,8,128]{3,2,1,0:T(8,128)S(1)}) custom-call(f32[4,8,16,128]{3,2,1,0:T(8,128)S(1)} %bitcast.7), custom_call_target="tpu_custom_call" | custom-call | tf_op jit(solution)/shard_map/splat_points/pallas_call | solution.py:626
  28.5 1.2 %collective-permute-start = (f32[2,7,8,128]{3,2,1,0:T(8,128)S(1)}, f32[2,7,8,128]{3,2,1,0:T(8,128)S(1)}, u32[]{:S(2)}, u32[]{:S(2)}) collective-permute-start(f32[2,7,8,128]{3,2,1,0:T(8,128)S(1)} %get-tuple-element.11), channel_id=1, source_target_pairs={{0,1},{2,3},{1,0},{3,2},{4,5},{6,7},{5,4},{7,6},{8,9},{10,11},{9,8... | collective-permute-start | bytes 172040 | tf_op jit(solution)/shard_map/ppermute | solution.py:648
  29.6 0.8 %read_operand.1.read_ref = bf16[1,2,640,1024]{3,2,1,0:T(8,128)(2,1)S(1)} custom-call(f32[2,8,8,128]{3,2,1,0:T(8,128)S(1)} %get-tuple-element.13.own_ref), custom_call_target="tpu_custom_call" | custom-call | flops 5242880 | bytes 2621440 | tf_op jit(solution)/shard_map/read_operand/pallas_call | solution.py:653
  30.5 0.8 %collective-permute-start.1 = (f32[2,7,8,128]{3,2,1,0:T(8,128)S(1)}, f32[2,7,8,128]{3,2,1,0:T(8,128)S(1)}, u32[]{:S(2)}, u32[]{:S(2)}) collective-permute-start(f32[2,7,8,128]{3,2,1,0:T(8,128)S(1)} %get-tuple-element.14), channel_id=1, source_target_pairs={{1,2},{2,1},{5,6},{6,5},{9,10},{10,9},{13,14},{14,13},{17,18},{18,... | collective-permute-start | bytes 172040 | tf_op jit(solution)/shard_map/ppermute | solution.py:648
  31.3 2.2 %solve_inner.1.inner_ref = f32[5,112,128]{2,1,0:T(8,128)S(1)} custom-call(f32[2,7,144,128]{3,2,1,0:T(8,128)S(1)} %get-tuple-element.10.fields_ref), custom_call_target="tpu_custom_call" | custom-call | flops 9031680 | bytes 1032192 | tf_op jit(solution)/shard_map/solve_inner/pallas_call | solution.py:667
  33.5 0.0 collective-permute-done.first_ref
  33.5 0.0 collective-permute-done.1.second_ref
  33.5 2.5 %solve_and_read.1 = (f32[16,16,128]{2,1,0:T(8,128)}, f32[32,32]{1,0:T(8,128)S(1)}) custom-call(f32[2,7,144,128]{3,2,1,0:T(8,128)S(1)} %get-tuple-element.10.fields_ref, f32[2,7,8,128]{3,2,1,0:T(8,128)S(1)} %collective-permute-done.first_ref, f32[2,7,8,128]{3,2,1,0:T(8,128)S(1)} %collective-permute-done.1.second_ref, ...), custom_call_target="tpu_custom_call" | custom-call | tf_op jit(solution)/shard_map/solve_and_read/pallas_call | solution.py:680
  36.0 12.2 %all_to_all.11 = f32[1,32,32]{2,0,1:T(1,128)S(1)} all-to-all(f32[1,32,32]{2,0,1:T(1,128)S(1)} %bitcast.8), channel_id=1, replica_groups=mesh['gx'=4,'gy'=2,'gz'=4] {'gx','gy','gz'}, dimensions={1} | all-to-all | bytes 8192 | tf_op jit(solution)/shard_map/all_to_all | solution.py:698
  48.2 0.6 %copy.8 = f32[1,32,32]{2,1,0:T(8,128)} copy(f32[1,32,32]{2,1,0:T(8,128)S(1)} %bitcast.10) | data formatting | bytes 8192
Async XLA Ops:
  28.5 5.0 %collective-permute-start = (f32[2,7,8,128]{3,2,1,0:T(8,128)S(1)}, f32[2,7,8,128]{3,2,1,0:T(8,128)S(1)}, u32[]{:S(2)}, u32[]{:S(2)}) collective-permute-start(f32[2,7,8,128]{3,2,1,0:T(8,128)S(1)} %get-tuple-element.11), channel_id=1, source_target_pairs={{0,1},{2,3},{1,0},{3,2},{4,5},{6,7},{5,4},{7,6},{8,9},{10,11},{9,8... | collective-permute-start | bytes 172040 | tf_op jit(solution)/shard_map/ppermute | solution.py:648
  30.5 3.0 %collective-permute-start.1 = (f32[2,7,8,128]{3,2,1,0:T(8,128)S(1)}, f32[2,7,8,128]{3,2,1,0:T(8,128)S(1)}, u32[]{:S(2)}, u32[]{:S(2)}) collective-permute-start(f32[2,7,8,128]{3,2,1,0:T(8,128)S(1)} %get-tuple-element.14), channel_id=1, source_target_pairs={{1,2},{2,1},{5,6},{6,5},{9,10},{10,9},{13,14},{14,13},{17,18},{18,... | collective-permute-start | bytes 172040 | tf_op jit(solution)/shard_map/ppermute | solution.py:648

commit v14 on v12

--- a/solution.py
+++ b/solution.py
@@ -510,10 +510,13 @@
 ):
     edge[...] = jnp.zeros_like(edge)
     low_at, high_at = UP_AT - CZ, DOWN_AT + CZ - (ROWS - 16)
-    even = lax.axis_index("gz") % 2 == 0
+    mz = lax.axis_index("gz")
+    even = mz % 2 == 0
     got_first, got_second = first_ref[...], second_ref[...]
-    edge[0, :, :, low_at : low_at + HALO, :] = jnp.where(even, got_second, got_first)
-    edge[1, :, :, high_at : high_at + HALO, :] = jnp.where(even, got_first, got_second)
+    from_low = jnp.where(even, got_second, got_first)
+    from_high = jnp.where(even, got_first, got_second)
+    edge[0, :, :, low_at : low_at + HALO, :] = jnp.where(mz > 0, from_low, 0.0)
+    edge[1, :, :, high_at : high_at + HALO, :] = jnp.where(mz < shape[2] - 1, from_high, 0.0)
 
     def given(c, t, i):
         value = fields_ref[c, t, 8 * i : 8 * i + 8, :]
@@ -643,6 +646,8 @@
 
     def swapped(edge, start):
         pairs = [(i, i + 1) for i in range(start, gz - 1, 2)]
+        if start == 1 and gz % 2 == 0:
+            pairs.append((gz - 1, 0))
         return lax.ppermute(edge, "gz", pairs + [(j, i) for i, j in pairs])
 
     got_first, got_second = swapped(first, 0), swapped(second, 1)

time: 48.2 us -> 48 us (level)
  blocking collectives: 29 us -> 26.6 us
  waiting for transfers between devices: 0.01 us -> 1.88 us
    all_to_all x1, blocking collectives: 11.5 us -> 9.11 us  [on_device(): lax.all_to_all(values.reshape(1, sources, slots), AXES, split_axis=1, con...]
    ppermute x2, waiting for transfers between devices: 0.01 us -> 1.88 us  [swapped(): return lax.ppermute(edge, 'gz', pairs + [(j, i) for i, j in pairs])]
  transfers between devices with their start and end apart: 2 -> 2, of which waited for: 0 -> 1; matrix products, arithmetic and copies ran while one was open for 0% -> 0% of each run, Pallas kernels for 6% -> 6%
where the time goes in v14:
time: 48 us; the launch traced here: 47.8 us
  blocking collectives  26.6 us (55%)
  Pallas kernels  15.7 us (33%)
  starting transfers between devices  2.28 us (5%)
  waiting for transfers between devices  1.88 us (4%)
  between operations  0.65 us (1%)
  local copies, waits for them, and re-layouts  0.61 us (1%)
    all_to_all x1, blocking collectives, on_device(): lax.all_to_all(outgoing, AXES, split_axis=0, concat_axis=0, tiled=True)  17.5 us
    all_to_all x1, blocking collectives, on_device(): lax.all_to_all(values.reshape(1, sources, slots), AXES, split_axis=1, con...  9.11 us
    pallas_call x1, Pallas kernels, on_device(): pl.pallas_call(functools.partial(splat_kernel, shape), out_shape=(jax.Sha...  8.37 us
    pallas_call x1, Pallas kernels, on_device(): pl.pallas_call(functools.partial(inner_kernel, shape), out_shape=(jax.Sha...  2.96 us
    pallas_call x1, Pallas kernels, on_device(): pl.pallas_call(functools.partial(solve_kernel, shape), out_shape=(jax.Sha...  2.45 us
    ppermute x2, starting transfers between devices, swapped(): return lax.ppermute(edge, 'gz', pairs + [(j, i) for i, j in pairs])  2.28 us
    pallas_call x1, Pallas kernels, on_device(): pl.pallas_call(functools.partial(pack_kernel, shape), out_shape=jax.Shape...  1.95 us
    ppermute x2, waiting for transfers between devices, swapped(): return lax.ppermute(edge, 'gz', pairs + [(j, i) for i, j in pairs])  1.88 us
  transfers between devices with their start and end apart: 2, of which 1 were waited for; matrix products, arithmetic and copies ran while one was open for 0% of the time, Pallas kernels for 6%

profile of v14, /device:TPU:0, one launch (start us, length us, event | category | flops | bytes accessed | tf_op | source)
XLA Modules:
  0.0 47.8 jit_solution(13219318991430913065)
XLA Ops:
  0.6 2.0 %pack_points.1 = f32[32,16,128]{2,1,0:T(8,128)} custom-call(f32[1,7,32,32]{3,2,1,0:T(8,128)} %bitcast.9, s32[1,3,32,32]{3,2,1,0:T(8,128)} %bitcast.11, s32[1,32]{1,0:T(1,128)} %counts_ref.1), custom_call_target="tpu_custom_call" | custom-call | tf_op jit(solution)/shard_map/pack_points/pallas_call | solution.py:589
  2.6 17.5 %all_to_all.10 = f32[32,16,128]{2,1,0:T(8,128)S(1)} all-to-all(f32[32,16,128]{2,1,0:T(8,128)} %pack_points.1), channel_id=1, replica_groups=mesh['gx'=4,'gy'=2,'gz'=4] {'gx','gy','gz'}, dimensions={0} | all-to-all | bytes 524288 | tf_op jit(solution)/shard_map/all_to_all | solution.py:602
  20.1 8.4 %splat_points.1 = (f32[2,7,144,128]{3,2,1,0:T(8,128)S(1)}, f32[2,7,8,128]{3,2,1,0:T(8,128)S(1)}, f32[2,7,8,128]{3,2,1,0:T(8,128)S(1)}, f32[2,8,8,128]{3,2,1,0:T(8,128)S(1)}) custom-call(f32[4,8,16,128]{3,2,1,0:T(8,128)S(1)} %bitcast.7), custom_call_target="tpu_custom_call" | custom-call | tf_op jit(solution)/shard_map/splat_points/pallas_call | solution.py:627
  28.5 1.2 %collective-permute-start = (f32[2,7,8,128]{3,2,1,0:T(8,128)S(1)}, f32[2,7,8,128]{3,2,1,0:T(8,128)S(1)}, u32[]{:S(2)}, u32[]{:S(2)}) collective-permute-start(f32[2,7,8,128]{3,2,1,0:T(8,128)S(1)} %get-tuple-element.11), channel_id=1, source_target_pairs={{0,1},{2,3},{1,0},{3,2},{4,5},{6,7},{5,4},{7,6},{8,9},{10,11},{9,8... | collective-permute-start | bytes 172040 | tf_op jit(solution)/shard_map/ppermute | solution.py:651
  29.6 1.1 %collective-permute-start.1 = (f32[2,7,8,128]{3,2,1,0:T(8,128)S(1)}, f32[2,7,8,128]{3,2,1,0:T(8,128)S(1)}, u32[]{:S(2)}, u32[]{:S(2)}) collective-permute-start(f32[2,7,8,128]{3,2,1,0:T(8,128)S(1)} %get-tuple-element.12), channel_id=1, source_target_pairs={{1,2},{3,0},{2,1},{0,3},{5,6},{7,4},{6,5},{4,7},{9,10},{11,8},{10,... | collective-permute-start | bytes 172040 | tf_op jit(solution)/shard_map/ppermute | solution.py:651
  30.7 3.0 %solve_inner.1 = (bf16[1,2,640,1024]{3,2,1,0:T(8,128)(2,1)S(1)}, f32[5,112,128]{2,1,0:T(8,128)S(1)}) custom-call(f32[2,7,144,128]{3,2,1,0:T(8,128)S(1)} %get-tuple-element.10.fields_ref, f32[2,8,8,128]{3,2,1,0:T(8,128)S(1)} %get-tuple-element.13.own_ref), custom_call_target="tpu_custom_call" | custom-call | flops 5242880 | bytes 2621440 | tf_op jit(solution)/shard_map/solve_inner/pallas_call | solution.py:657
  33.7 0.0 collective-permute-done.first_ref
  33.7 1.9 %collective-permute-done.1.second_ref = f32[2,7,8,128]{3,2,1,0:T(8,128)S(1)} collective-permute-done((f32[2,7,8,128]{3,2,1,0:T(8,128)S(1)}, f32[2,7,8,128]{3,2,1,0:T(8,128)S(1)}, u32[]{:S(2)}, u32[]{:S(2)}) %collective-permute-start.1) | collective-permute-done | bytes 57376 | tf_op jit(solution)/shard_map/ppermute | solution.py:651
  35.6 2.5 %solve_and_read.1 = (f32[16,16,128]{2,1,0:T(8,128)}, f32[32,32]{1,0:T(8,128)S(1)}) custom-call(f32[2,7,144,128]{3,2,1,0:T(8,128)S(1)} %get-tuple-element.10.fields_ref, f32[2,7,8,128]{3,2,1,0:T(8,128)S(1)} %collective-permute-done.first_ref, f32[2,7,8,128]{3,2,1,0:T(8,128)S(1)} %collective-permute-done.1.second_ref, ...), custom_call_target="tpu_custom_call" | custom-call | tf_op jit(solution)/shard_map/solve_and_read/pallas_call | solution.py:674
  38.1 9.1 %all_to_all.11 = f32[1,32,32]{2,0,1:T(1,128)S(1)} all-to-all(f32[1,32,32]{2,0,1:T(1,128)S(1)} %bitcast.8), channel_id=1, replica_groups=mesh['gx'=4,'gy'=2,'gz'=4] {'gx','gy','gz'}, dimensions={1} | all-to-all | bytes 8192 | tf_op jit(solution)/shard_map/all_to_all | solution.py:692
  47.2 0.6 %copy.8 = f32[1,32,32]{2,1,0:T(8,128)} copy(f32[1,32,32]{2,1,0:T(8,128)S(1)} %bitcast.10) | data formatting | bytes 8192
Async XLA Ops:
  28.5 5.3 %collective-permute-start = (f32[2,7,8,128]{3,2,1,0:T(8,128)S(1)}, f32[2,7,8,128]{3,2,1,0:T(8,128)S(1)}, u32[]{:S(2)}, u32[]{:S(2)}) collective-permute-start(f32[2,7,8,128]{3,2,1,0:T(8,128)S(1)} %get-tuple-element.11), channel_id=1, source_target_pairs={{0,1},{2,3},{1,0},{3,2},{4,5},{6,7},{5,4},{7,6},{8,9},{10,11},{9,8... | collective-permute-start | bytes 172040 | tf_op jit(solution)/shard_map/ppermute | solution.py:651
  29.6 6.0 %collective-permute-start.1 = (f32[2,7,8,128]{3,2,1,0:T(8,128)S(1)}, f32[2,7,8,128]{3,2,1,0:T(8,128)S(1)}, u32[]{:S(2)}, u32[]{:S(2)}) collective-permute-start(f32[2,7,8,128]{3,2,1,0:T(8,128)S(1)} %get-tuple-element.12), channel_id=1, source_target_pairs={{1,2},{3,0},{2,1},{0,3},{5,6},{7,4},{6,5},{4,7},{9,10},{11,8},{10,... | collective-permute-start | bytes 172040 | tf_op jit(solution)/shard_map/ppermute | solution.py:651

commit v15 on v14

--- a/solution.py
+++ b/solution.py
@@ -646,9 +646,9 @@
 
     def swapped(edge, start):
         pairs = [(i, i + 1) for i in range(start, gz - 1, 2)]
-        if start == 1 and gz % 2 == 0:
-            pairs.append((gz - 1, 0))
-        return lax.ppermute(edge, "gz", pairs + [(j, i) for i, j in pairs])
+        pairs += [(j, i) for i, j in pairs]
+        alone = set(range(gz)) - {i for i, _ in pairs}
+        return lax.ppermute(edge, "gz", pairs + [(i, i) for i in sorted(alone)])
 
     got_first, got_second = swapped(first, 0), swapped(second, 1)
 

time: 48 us -> 48.2 us (level)
  blocking collectives: 26.6 us -> 29 us
  waiting for transfers between devices: 1.88 us -> 0.01 us
    all_to_all x1, blocking collectives: 9.11 us -> 11.5 us  [on_device(): lax.all_to_all(values.reshape(1, sources, slots), AXES, split_axis=1, con...]
    ppermute x2, waiting for transfers between devices: 1.88 us -> 0.01 us  [swapped(): return lax.ppermute(edge, 'gz', pairs + [(i, i) for i in sorted(alone)])]
  transfers between devices with their start and end apart: 2 -> 2, of which waited for: 1 -> 0; matrix products, arithmetic and copies ran while one was open for 0% -> 0% of each run, Pallas kernels for 6% -> 6%
where the time goes in v15:
time: 48.2 us; the launch traced here: 48 us
  blocking collectives  29 us (60%)
  Pallas kernels  15.7 us (33%)
  starting transfers between devices  1.99 us (4%)
  between operations  0.66 us (1%)
  local copies, waits for them, and re-layouts  0.61 us (1%)
    all_to_all x1, blocking collectives, on_device(): lax.all_to_all(outgoing, AXES, split_axis=0, concat_axis=0, tiled=True)  17.5 us
    all_to_all x1, blocking collectives, on_device(): lax.all_to_all(values.reshape(1, sources, slots), AXES, split_axis=1, con...  11.5 us
    pallas_call x1, Pallas kernels, on_device(): pl.pallas_call(functools.partial(splat_kernel, shape), out_shape=(jax.Sha...  8.37 us
    pallas_call x1, Pallas kernels, on_device(): pl.pallas_call(functools.partial(inner_kernel, shape), out_shape=(jax.Sha...  2.97 us
    pallas_call x1, Pallas kernels, on_device(): pl.pallas_call(functools.partial(solve_kernel, shape), out_shape=(jax.Sha...  2.46 us
    ppermute x2, starting transfers between devices, swapped(): return lax.ppermute(edge, 'gz', pairs + [(i, i) for i in sorted(alone)])  1.99 us
    pallas_call x1, Pallas kernels, on_device(): pl.pallas_call(functools.partial(pack_kernel, shape), out_shape=jax.Shape...  1.95 us
  transfers between devices with their start and end apart: 2, of which 0 were waited for; matrix products, arithmetic and copies ran while one was open for 0% of the time, Pallas kernels for 6%

profile of v15, /device:TPU:0, one launch (start us, length us, event | category | flops | bytes accessed | tf_op | source)
XLA Modules:
  0.0 48.0 jit_solution(17604397769211935112)
XLA Ops:
  0.6 2.0 %pack_points.1 = f32[32,16,128]{2,1,0:T(8,128)} custom-call(f32[1,7,32,32]{3,2,1,0:T(8,128)} %bitcast.9, s32[1,3,32,32]{3,2,1,0:T(8,128)} %bitcast.11, s32[1,32]{1,0:T(1,128)} %counts_ref.1), custom_call_target="tpu_custom_call" | custom-call | tf_op jit(solution)/shard_map/pack_points/pallas_call | solution.py:589
  2.6 17.5 %all_to_all.10 = f32[32,16,128]{2,1,0:T(8,128)S(1)} all-to-all(f32[32,16,128]{2,1,0:T(8,128)} %pack_points.1), channel_id=1, replica_groups=mesh['gx'=4,'gy'=2,'gz'=4] {'gx','gy','gz'}, dimensions={0} | all-to-all | bytes 524288 | tf_op jit(solution)/shard_map/all_to_all | solution.py:602
  20.1 8.4 %splat_points.1 = (f32[2,7,144,128]{3,2,1,0:T(8,128)S(1)}, f32[2,7,8,128]{3,2,1,0:T(8,128)S(1)}, f32[2,7,8,128]{3,2,1,0:T(8,128)S(1)}, f32[2,8,8,128]{3,2,1,0:T(8,128)S(1)}) custom-call(f32[4,8,16,128]{3,2,1,0:T(8,128)S(1)} %bitcast.7), custom_call_target="tpu_custom_call" | custom-call | tf_op jit(solution)/shard_map/splat_points/pallas_call | solution.py:627
  28.5 1.2 %collective-permute-start = (f32[2,7,8,128]{3,2,1,0:T(8,128)S(1)}, f32[2,7,8,128]{3,2,1,0:T(8,128)S(1)}, u32[]{:S(2)}, u32[]{:S(2)}) collective-permute-start(f32[2,7,8,128]{3,2,1,0:T(8,128)S(1)} %get-tuple-element.11), channel_id=1, source_target_pairs={{0,1},{2,3},{1,0},{3,2},{4,5},{6,7},{5,4},{7,6},{8,9},{10,11},{9,8... | collective-permute-start | bytes 172040 | tf_op jit(solution)/shard_map/ppermute | solution.py:651
  29.6 0.8 %collective-permute-start.1 = (f32[2,7,8,128]{3,2,1,0:T(8,128)S(1)}, f32[2,7,8,128]{3,2,1,0:T(8,128)S(1)}, u32[]{:S(2)}, u32[]{:S(2)}) collective-permute-start(f32[2,7,8,128]{3,2,1,0:T(8,128)S(1)} %get-tuple-element.12), channel_id=1, source_target_pairs={{1,2},{2,1},{0,0},{3,3},{5,6},{6,5},{4,4},{7,7},{9,10},{10,9},{8,8... | collective-permute-start | bytes 172040 | tf_op jit(solution)/shard_map/ppermute | solution.py:651
  30.5 3.0 %solve_inner.1 = (bf16[1,2,640,1024]{3,2,1,0:T(8,128)(2,1)S(1)}, f32[5,112,128]{2,1,0:T(8,128)S(1)}) custom-call(f32[2,7,144,128]{3,2,1,0:T(8,128)S(1)} %get-tuple-element.10.fields_ref, f32[2,8,8,128]{3,2,1,0:T(8,128)S(1)} %get-tuple-element.13.own_ref), custom_call_target="tpu_custom_call" | custom-call | flops 5242880 | bytes 2621440 | tf_op jit(solution)/shard_map/solve_inner/pallas_call | solution.py:657
  33.4 0.0 collective-permute-done.first_ref
  33.4 0.0 collective-permute-done.1.second_ref
  33.5 2.5 %solve_and_read.1 = (f32[16,16,128]{2,1,0:T(8,128)}, f32[32,32]{1,0:T(8,128)S(1)}) custom-call(f32[2,7,144,128]{3,2,1,0:T(8,128)S(1)} %get-tuple-element.10.fields_ref, f32[2,7,8,128]{3,2,1,0:T(8,128)S(1)} %collective-permute-done.first_ref, f32[2,7,8,128]{3,2,1,0:T(8,128)S(1)} %collective-permute-done.1.second_ref, ...), custom_call_target="tpu_custom_call" | custom-call | tf_op jit(solution)/shard_map/solve_and_read/pallas_call | solution.py:674
  35.9 11.5 %all_to_all.11 = f32[1,32,32]{2,0,1:T(1,128)S(1)} all-to-all(f32[1,32,32]{2,0,1:T(1,128)S(1)} %bitcast.8), channel_id=1, replica_groups=mesh['gx'=4,'gy'=2,'gz'=4] {'gx','gy','gz'}, dimensions={1} | all-to-all | bytes 8192 | tf_op jit(solution)/shard_map/all_to_all | solution.py:692
  47.4 0.6 %copy.8 = f32[1,32,32]{2,1,0:T(8,128)} copy(f32[1,32,32]{2,1,0:T(8,128)S(1)} %bitcast.10) | data formatting | bytes 8192
Async XLA Ops:
  28.5 5.0 %collective-permute-start = (f32[2,7,8,128]{3,2,1,0:T(8,128)S(1)}, f32[2,7,8,128]{3,2,1,0:T(8,128)S(1)}, u32[]{:S(2)}, u32[]{:S(2)}) collective-permute-start(f32[2,7,8,128]{3,2,1,0:T(8,128)S(1)} %get-tuple-element.11), channel_id=1, source_target_pairs={{0,1},{2,3},{1,0},{3,2},{4,5},{6,7},{5,4},{7,6},{8,9},{10,11},{9,8... | collective-permute-start | bytes 172040 | tf_op jit(solution)/shard_map/ppermute | solution.py:651
  29.6 3.8 %collective-permute-start.1 = (f32[2,7,8,128]{3,2,1,0:T(8,128)S(1)}, f32[2,7,8,128]{3,2,1,0:T(8,128)S(1)}, u32[]{:S(2)}, u32[]{:S(2)}) collective-permute-start(f32[2,7,8,128]{3,2,1,0:T(8,128)S(1)} %get-tuple-element.12), channel_id=1, source_target_pairs={{1,2},{2,1},{0,0},{3,3},{5,6},{6,5},{4,4},{7,7},{9,10},{10,9},{8,8... | collective-permute-start | bytes 172040 | tf_op jit(solution)/shard_map/ppermute | solution.py:651
